TPU v7x, 32 devices: a whole 2x2x4 slice. The times are simulated.
32 devices in a mesh: fsdp: 8 (over z, y), rep: 4 (over x, core).
Axes of the slice: x: 2, y: 2, z: 4, core: 2. Of those that a mesh axis runs over, the one named last changes fastest.
Arguments:
- tokens: bfloat16 [32768, 768], P(('fsdp', 'rep')), may hold values from -6 to 6
- lengths: int32 [32, 2], P(('fsdp', 'rep')), may hold values from 0 to 1024, as said below
- w_qkv: bfloat16 [768, 2304], P('fsdp'), may hold values from -0.21875 to 0.21875
- vectors: bfloat16 [8, 768], P(None, 'fsdp')
- w_attn_out: bfloat16 [768, 768], P('fsdp'), may hold values from -2 to 2
- w_in: bfloat16 [768, 3072], P('fsdp'), may hold values from -0.21875 to 0.21875
- b_in: bfloat16 [3072], P('fsdp'), may hold values from -3 to 3
- w_down: bfloat16 [3072, 768], P('fsdp'), may hold values from -0.109375 to 0.109375
- cotangent: bfloat16 [32768, 768], P(('fsdp', 'rep')), may hold values from -6 to 6
Outputs:
- layer_out: bfloat16 [32768, 768], P(('fsdp', 'rep'))
- grad_tokens: bfloat16 [32768, 768], P(('fsdp', 'rep'))
- grad_w_qkv: float32 [768, 2304], P('fsdp')
- grad_vectors: float32 [8, 768], P(None, 'fsdp')
- grad_w_attn_out: float32 [768, 768], P('fsdp')
- grad_w_in: float32 [768, 3072], P('fsdp')
- grad_b_in: float32 [3072], P('fsdp')
- grad_w_down: float32 [3072, 768], P('fsdp')
Inputs may be any that keep to these rules, and one draw needn't show every extreme that they name: Row g holds the lengths of the two sequences of the g-th group of 1024 tokens (groups in the order of the token rows). The first starts at the group's row 0, the second at the first multiple of 128 at or after the first one's end, and both end within the group. One group holds a single sequence of 1024 tokens and a second of length 0; every other group has two sequences of 1 or more tokens.
All inputs are finite; a program needn't handle non-finite values.
Results may differ from a plain program's by a relative error of at most 0.017.
Values may be sent and summed in bfloat16 or wider, within the bound.
No kernel may reach another device: no remote copies, remote signals or barrier semaphores. Data moves between devices by JAX's collectives and lax.ppermute only.
A program may use at most 256 MiB of HBM per device.

v0:
```python
import jax
import jax.numpy as jnp
from jax import lax
from jax.sharding import PartitionSpec as P

D = 768
HEADS = 12
HEAD_DIM = 64
BLOCK = 128


NORM_EPS = 1e-12
MASKED_SCORE = -1e30


def layout(length_row, row_count):
    first_len = length_row[0]
    second_len = length_row[1]
    second_start = (first_len + BLOCK - 1) // BLOCK * BLOCK
    positions = jnp.arange(row_count, dtype=jnp.int32)
    in_first = positions < first_len
    in_second = (positions >= second_start) & (positions < second_start + second_len)
    doc_ids = jnp.where(in_first, 0, jnp.where(in_second, 1, 2)).astype(jnp.int32)
    return (in_first | in_second, doc_ids)


def gelu_exact(values):
    return jax.nn.gelu(values, approximate=False)


def norm_forward(hidden, gain_row, shift_row):
    centre = jnp.mean(hidden, axis=-1, keepdims=True)
    spread = jnp.mean(jnp.square(hidden - centre), axis=-1, keepdims=True)
    inverse = lax.rsqrt(spread + NORM_EPS)
    normed = (hidden - centre) * inverse
    return (normed * gain_row + shift_row, normed, inverse)


def norm_backward(grad_rows, normed, inverse, gain_row):
    scaled = grad_rows * gain_row
    grad_in = inverse * (
        scaled
        - jnp.mean(scaled, axis=-1, keepdims=True)
        - normed * jnp.mean(scaled * normed, axis=-1, keepdims=True)
    )
    return (grad_in, jnp.sum(grad_rows * normed, axis=0), jnp.sum(grad_rows, axis=0))


def split_heads(rows, blocks, rows_block):
    return rows.reshape(blocks, rows_block, HEADS, HEAD_DIM)


def masked_scores(query_part, key_split, doc_part, doc_ids):
    scores = (
        jnp.einsum("qhd,khd->hqk", query_part, key_split, preferred_element_type=jnp.float32)
        * 0.125
    )
    allowed = doc_part[:, None] == doc_ids[None, :]
    return jnp.where(allowed[None], scores, MASKED_SCORE)


def attention_forward(queries, key_rows, value_rows, doc_ids):
    row_count = queries.shape[0]
    rows_block = min(512, row_count)
    blocks = row_count // rows_block
    key_split = key_rows.reshape(row_count, HEADS, HEAD_DIM)
    value_split = value_rows.reshape(row_count, HEADS, HEAD_DIM)

    def one_block(block_pair):
        query_part, doc_part = block_pair
        scores = masked_scores(query_part, key_split, doc_part, doc_ids)
        row_top = jnp.max(scores, axis=-1, keepdims=True)
        exp_scores = jnp.exp(scores - row_top)
        row_total = jnp.sum(exp_scores, axis=-1, keepdims=True)
        weights = (exp_scores / row_total).astype(jnp.bfloat16)
        attended = jnp.einsum(
            "hqk,khd->qhd", weights, value_split, preferred_element_type=jnp.float32
        )
        return (attended.astype(jnp.bfloat16), row_top + jnp.log(row_total))

    attended, log_total = lax.map(
        one_block, (split_heads(queries, blocks, rows_block), doc_ids.reshape(blocks, rows_block))
    )
    return (attended.reshape(row_count, D), log_total)


def attention_backward(queries, key_rows, value_rows, doc_ids, grad_context, log_total):
    row_count = queries.shape[0]
    rows_block = min(512, row_count)
    blocks = row_count // rows_block
    key_split = key_rows.reshape(row_count, HEADS, HEAD_DIM)
    value_split = value_rows.reshape(row_count, HEADS, HEAD_DIM)

    def one_block(running, block_parts):
        key_grad, value_grad = running
        query_part, doc_part, grad_part, lse_part = block_parts
        scores = masked_scores(query_part, key_split, doc_part, doc_ids)
        weights = jnp.exp(scores - lse_part)
        grad_weights = jnp.einsum(
            "qhd,khd->hqk", grad_part, value_split, preferred_element_type=jnp.float32
        )
        grad_scores = (
            weights * (grad_weights - jnp.sum(weights * grad_weights, axis=-1, keepdims=True))
        ).astype(jnp.bfloat16)
        query_grad = (
            jnp.einsum("hqk,khd->qhd", grad_scores, key_split, preferred_element_type=jnp.float32)
            * 0.125
        )
        key_grad = (
            key_grad
            + jnp.einsum(
                "hqk,qhd->khd", grad_scores, query_part, preferred_element_type=jnp.float32
            )
            * 0.125
        )
        value_grad = value_grad + jnp.einsum(
            "hqk,qhd->khd",
            weights.astype(jnp.bfloat16),
            grad_part,
            preferred_element_type=jnp.float32,
        )
        return ((key_grad, value_grad), query_grad)

    empty_grad = jnp.zeros((row_count, HEADS, HEAD_DIM), jnp.float32)
    block_parts = (
        split_heads(queries, blocks, rows_block),
        doc_ids.reshape(blocks, rows_block),
        split_heads(grad_context, blocks, rows_block),
        log_total,
    )
    (key_grad, value_grad), query_grad = lax.scan(one_block, (empty_grad, empty_grad), block_parts)
    return (
        query_grad.reshape(row_count, D),
        key_grad.reshape(row_count, D),
        value_grad.reshape(row_count, D),
    )


def body(tokens, lengths, w_qkv, vectors, w_attn_out, w_in, b_in, w_down, cotangent):
    row_count = tokens.shape[0]
    valid_rows, doc_ids = layout(lengths[0], row_count)
    qkv_full, out_full, vector_full = (
        lax.all_gather(w_qkv, "fsdp", axis=0, tiled=True),
        lax.all_gather(w_attn_out, "fsdp", axis=0, tiled=True),
        lax.all_gather(vectors, "fsdp", axis=1, tiled=True),
    )
    vector_wide = vector_full.astype(jnp.float32)
    projected = jnp.dot(tokens, qkv_full, preferred_element_type=jnp.float32)
    queries = (projected[:, :D] + vector_wide[0]).astype(jnp.bfloat16)
    key_rows = projected[:, D : 2 * D].astype(jnp.bfloat16)
    value_rows = (projected[:, 2 * D :] + vector_wide[1]).astype(jnp.bfloat16)
    context, log_total = attention_forward(queries, key_rows, value_rows, doc_ids)
    attn_branch = jnp.dot(context, out_full, preferred_element_type=jnp.float32) + vector_wide[2]
    first_norm, normed_one, inverse_one = norm_forward(
        tokens.astype(jnp.float32) + attn_branch, vector_wide[3], vector_wide[4]
    )
    in_full, down_full, bias_full = (
        lax.all_gather(w_in, "fsdp", axis=0, tiled=True),
        lax.all_gather(w_down, "fsdp", axis=0, tiled=True),
        lax.all_gather(b_in, "fsdp", axis=0, tiled=True),
    )
    first_low = first_norm.astype(jnp.bfloat16)
    inner_act = jnp.dot(first_low, in_full, preferred_element_type=jnp.float32) + bias_full.astype(
        jnp.float32
    )
    active = gelu_exact(inner_act).astype(jnp.bfloat16)
    mlp_branch = jnp.dot(active, down_full, preferred_element_type=jnp.float32) + vector_wide[5]
    second_norm, normed_two, inverse_two = norm_forward(
        first_norm + mlp_branch, vector_wide[6], vector_wide[7]
    )
    layer_out = jnp.where(valid_rows[:, None], second_norm, 0.0).astype(jnp.bfloat16)
    grad_out = jnp.where(valid_rows[:, None], cotangent.astype(jnp.float32), 0.0)
    grad_two, gain_two, shift_two = norm_backward(grad_out, normed_two, inverse_two, vector_wide[6])
    grad_mlp = grad_two.astype(jnp.bfloat16)
    in_back, down_back = (
        lax.all_gather(w_in, "fsdp", axis=0, tiled=True),
        lax.all_gather(w_down, "fsdp", axis=0, tiled=True),
    )
    grad_active = jnp.dot(grad_mlp, down_back.T, preferred_element_type=jnp.float32)
    grad_inner = jax.vjp(gelu_exact, inner_act)[1](grad_active)[0].astype(jnp.bfloat16)
    grad_w_down = jnp.dot(active.T, grad_mlp, preferred_element_type=jnp.float32)
    grad_b_down = jnp.sum(grad_mlp.astype(jnp.float32), axis=0)
    grad_w_in = jnp.dot(first_low.T, grad_inner, preferred_element_type=jnp.float32)
    grad_b_in = jnp.sum(grad_inner.astype(jnp.float32), axis=0)
    grad_first = grad_two + jnp.dot(grad_inner, in_back.T, preferred_element_type=jnp.float32)
    grad_one, gain_one, shift_one = norm_backward(
        grad_first, normed_one, inverse_one, vector_wide[3]
    )
    grad_attn = grad_one.astype(jnp.bfloat16)
    qkv_back, out_back = (
        lax.all_gather(w_qkv, "fsdp", axis=0, tiled=True),
        lax.all_gather(w_attn_out, "fsdp", axis=0, tiled=True),
    )
    grad_w_out = jnp.dot(context.T, grad_attn, preferred_element_type=jnp.float32)
    grad_context = jnp.dot(grad_attn, out_back.T, preferred_element_type=jnp.float32).astype(
        jnp.bfloat16
    )
    query_grad, key_grad, value_grad = attention_backward(
        queries, key_rows, value_rows, doc_ids, grad_context, log_total
    )
    query_low = query_grad.astype(jnp.bfloat16)
    value_low = value_grad.astype(jnp.bfloat16)
    grad_proj = jnp.concatenate([query_low, key_grad.astype(jnp.bfloat16), value_low], axis=1)
    grad_w_qkv = jnp.dot(tokens.T, grad_proj, preferred_element_type=jnp.float32)
    grad_vectors = jnp.stack(
        [
            jnp.sum(query_low.astype(jnp.float32), axis=0),
            jnp.sum(value_low.astype(jnp.float32), axis=0),
            jnp.sum(grad_attn.astype(jnp.float32), axis=0),
            gain_one,
            shift_one,
            grad_b_down,
            gain_two,
            shift_two,
        ]
    )
    grad_tokens = (
        grad_one + jnp.dot(grad_proj, qkv_back.T, preferred_element_type=jnp.float32)
    ).astype(jnp.bfloat16)
    qkv_shard, out_shard, vector_shard, in_shard, down_shard, bias_shard = (
        lax.psum_scatter(grad_w_qkv, "fsdp", scatter_dimension=0, tiled=True),
        lax.psum_scatter(grad_w_out, "fsdp", scatter_dimension=0, tiled=True),
        lax.psum_scatter(grad_vectors, "fsdp", scatter_dimension=1, tiled=True),
        lax.psum_scatter(grad_w_in, "fsdp", scatter_dimension=0, tiled=True),
        lax.psum_scatter(grad_w_down, "fsdp", scatter_dimension=0, tiled=True),
        lax.psum_scatter(grad_b_in, "fsdp", scatter_dimension=0, tiled=True),
    )
    qkv_shard, out_shard, vector_shard, in_shard, down_shard, bias_shard = (
        lax.psum(qkv_shard.astype(jnp.bfloat16), "rep").astype(jnp.float32),
        lax.psum(out_shard.astype(jnp.bfloat16), "rep").astype(jnp.float32),
        lax.psum(vector_shard.astype(jnp.bfloat16), "rep").astype(jnp.float32),
        lax.psum(in_shard.astype(jnp.bfloat16), "rep").astype(jnp.float32),
        lax.psum(down_shard.astype(jnp.bfloat16), "rep").astype(jnp.float32),
        lax.psum(bias_shard.astype(jnp.bfloat16), "rep").astype(jnp.float32),
    )
    return (
        layer_out,
        grad_tokens,
        qkv_shard,
        vector_shard,
        out_shard,
        in_shard,
        bias_shard,
        down_shard,
    )


def solution(mesh):
    return jax.shard_map(
        body,
        mesh=mesh,
        in_specs=(
            P(("fsdp", "rep"), None),
            P(("fsdp", "rep"), None),
            P("fsdp", None),
            P(None, "fsdp"),
            P("fsdp", None),
            P("fsdp", None),
            P("fsdp"),
            P("fsdp", None),
            P(("fsdp", "rep"), None),
        ),
        out_specs=(
            P(("fsdp", "rep"), None),
            P(("fsdp", "rep"), None),
            P("fsdp", None),
            P(None, "fsdp"),
            P("fsdp", None),
            P("fsdp", None),
            P("fsdp"),
            P("fsdp", None),
        ),
        check_vma=False,
    )
```

profile of v0, /device:TPU:25, one launch (start us, length us, event | category | flops | bytes accessed | tf_op | source)
XLA Modules:
  0.0 1136.6 jit_solution(1394089618169609565)
XLA Ops:
  15.4 19.0 %all-gather.1 = bf16[8,1,384]{2,1,0:T(2,128)(2,1)S(1)} all-gather(bf16[1,1,384]{2,1,0:T(2,128)(2,1)S(1)} %reshape.195), channel_id=1, replica_groups=mesh['fsdp'=8,'rep'=4] {'fsdp'}, dimensions={0}, use_global_device_ids=true | all-gather | bytes 6912 | tf_op jit(solution)/shard_map/all_gather | solution.py:160
  35.1 22.8 %all-gather = bf16[8,96,8]{1,2,0:T(8,128)(2,1)S(1)} all-gather(bf16[1,96,8]{1,2,0:T(8,128)(2,1)} %bitcast.154), channel_id=1, replica_groups=mesh['fsdp'=8,'rep'=4] {'fsdp'}, dimensions={0}, use_global_device_ids=true | all-gather | bytes 13824 | tf_op jit(solution)/shard_map/all_gather | solution.py:145
  58.6 2.6 copy.58
  62.8 12.6 %all-gather.7.cloned.1.call-done = bf16[768,2304]{1,0:T(8,128)(2,1)} async-done(((bf16[96,2304]{1,0:T(8,128)(2,1)}), bf16[768,2304]{1,0:T(8,128)(2,1)}) %all-gather.7.cloned.1.call-update) | async-done | bytes 3538960 | tf_op jit(solution)/shard_map/all_gather | solution.py:143
  75.4 5.8 fusion.70
  81.4 1.8 fusion.46
  87.4 2.4 reshape.188
  89.8 1.7 copy.55
  91.5 71.8 %while.28 = (s32[]{:T(128)}, bf16[2,512,12,64]{1,3,2,0:T(8,128)(2,1)}, f32[2,12,512,1]{2,1,3,0:T(8,128)S(1)}, s32[2,512]{1,0:T(2,128)S(1)}, bf16[2,512,12,64]{1,...) while((s32[]{:T(128)}, ...), condition=%wide.region_3.4_spmd.clone, body=%wide.region_0.3_spmd.clone.sunk | while | flops 1687027712 | bytes 189503696 | solution.py:81
  92.6 10.7 fusion.114
  103.3 12.4 %fusion.115 = f32[12,512]{1,0:T(8,128)S(1)} fusion(f32[12,512,1024]{2,1,0:T(8,128)} %get-tuple-element.506, f32[12,512]{1,0:T(8,128)S(1)} %get-tuple-element.507, pred[512,1024]{1,0:T(8,128)(4,1)S(1)} %broadcast_compare_fusion.4), kind=kLoop, calls=%fused_computation.6.clone.1 | loop fusion | flops 25159680 | bytes 25739264 | tf_op jit(solution)/shard_map/while/body/eval_jaxpr/reduce_sum | solution.py:74
  115.7 3.1 copy-done
  118.8 8.5 fusion.116
  128.4 10.7 fusion.114
  139.0 12.3 %fusion.115 = f32[12,512]{1,0:T(8,128)S(1)} fusion(f32[12,512,1024]{2,1,0:T(8,128)} %get-tuple-element.506, f32[12,512]{1,0:T(8,128)S(1)} %get-tuple-element.507, pred[512,1024]{1,0:T(8,128)(4,1)S(1)} %broadcast_compare_fusion.4), kind=kLoop, calls=%fused_computation.6.clone.1 | loop fusion | flops 25159680 | bytes 25739264 | tf_op jit(solution)/shard_map/while/body/eval_jaxpr/reduce_sum | solution.py:74
  151.4 3.1 copy-done
  154.5 8.5 fusion.116
  163.3 4.2 copy.56
  169.1 3.8 fusion.68
  173.4 24.3 %all-gather.11.cloned.1.call-done = bf16[768,3072]{1,0:T(8,128)(2,1)} async-done(((bf16[96,3072]{1,0:T(8,128)(2,1)}), bf16[768,3072]{1,0:T(8,128)(2,1)}) %all-gather.11.cloned.1.call-update) | async-done | bytes 4718608 | tf_op jit(solution)/shard_map/all_gather | solution.py:158
  197.8 37.5 %multiply_convert_fusion.1 = (bf16[1024,3072]{1,0:T(8,128)(2,1)}, f32[1024,3072]{1,0:T(8,128)}, f32[1024,3072]{1,0:T(8,128)}) fusion(f32[3072]{0:T(1024)S(1)} %bitcast.152, bf16[768,3072]{1,0:T(8,128)(2,1)} %all-gather.11.cloned.1.call-done, f32[1024,768]{0,1:T(8,128)S(1)} %get-tuple-element.366, f32[768]{0:T(1024)S(1)} %copy-done.44, ...), kind=kOutput, calls=%fused_computation.62 | convolution fusion | flops 5043388416 | bytes 39348224 | tf_op jit(solution)/shard_map/dot_general | solution.py:163
  235.3 42.5 %all-gather.13.cloned.1.call-done = bf16[3072,768]{1,0:T(8,128)(2,1)} async-done(((bf16[384,768]{1,0:T(8,128)(2,1)}), bf16[3072,768]{1,0:T(8,128)(2,1)}) %all-gather.13.cloned.1.call-update) | async-done | bytes 4718608 | tf_op jit(solution)/shard_map/all_gather | solution.py:159
  277.8 21.3 %fusion.69 = (f32[1024]{0:T(1024)S(1)}, f32[1024,768]{0,1:T(8,128)S(1)}) fusion(f32[768]{0:T(1024)S(1)} %copy-done.46, bf16[1024,3072]{1,0:T(8,128)(2,1)} %get-tuple-element.354, bf16[3072,768]{1,0:T(8,128)(2,1)} %all-gather.13.cloned.1.call-done, f32[768]{0:T(1024)S(1)} %copy-done.44, f32[768]{0:T(1024)S(1)} %copy-done.32, f32[1024]{0:T(1024)S(1)} %add_rsqrt_fusion.1, ...), kind=kOutput, calls=%fused_computation.145 | convolution fusion | flops 4837342208 | bytes 17323008 | tf_op jit(solution)/shard_map/dot_general | solution.py:167
  300.6 2.0 multiply_reduce_fusion.1
  302.6 3.4 convert_reduce_fusion.1
  306.0 18.0 %convert_reduce_fusion = (f32[3072]{0:T(1024)}, bf16[1024,3072]{1,0:T(8,128)(2,1)}) fusion(f32[1024,3072]{1,0:T(8,128)} %get-tuple-element.355, bf16[1024,768]{0,1:T(8,128)(2,1)S(1)} %get-tuple-element.349, bf16[3072,768]{1,0:T(8,128)(2,1)} %all-gather.13.cloned.1.call-done, f32[1024,3072]{1,0:T(8,128)} %get-tuple-element.367, f32[3072]{0:T(1024)S(1)} %bitcast.153), kind=kOutput, calls=%fused_computation.60 | convolution fusion | flops 4885312512 | bytes 37773312 | tf_op jit(solution)/shard_map/dot_general | solution.py:179
  324.1 11.6 %multiply_reduce_fusion.2 = (f32[768]{0:T(1024)}, f32[1024]{0:T(1024)S(1)}, f32[1024]{0:T(1024)S(1)}, f32[768]{0:T(1024)}, f32[1024,768]{0,1:T(8,128)S(1)}) fusion(f32[1024,768]{0,1:T(8,128)} %copy-done.8, f32[1024]{0:T(1024)S(1)} %add_rsqrt_fusion.1, f32[1024]{0:T(1024)S(1)} %broadcast_multiply_fusion.5, f32[768]{0:T(1024)S(1)} %copy-done.32, ...), kind=kOutput, calls=%fused_computation.85 | convolution fusion | flops 4846776320 | bytes 22066176 | tf_op jit(solution)/shard_map/dot_general | solution.py:185
  337.4 2.9 fusion.58
  340.3 3.9 convolution_convert_fusion
  348.8 170.6 %while.29 = (s32[]{:T(128)}, f32[1024,12,64]{0,2,1:T(8,128)}, f32[1024,12,64]{0,2,1:T(8,128)}, bf16[2,512,12,64]{1,3,2,0:T(8,128)(2,1)}, bf16[2,512,12,64]{1,3,2...) while((s32[]{:T(128)}, f32[1024,12,64]{0,2,1:T(8,128)}, ...), condition=%wide.region_14.15_spmd.clone, body=%wide.region_12.14_spmd.clone.sunk | while | flops 4125753344 | bytes 225638672 | solution.py:131
  350.3 11.7 %fusion.126 = f32[12,512,1024]{2,1,0:T(8,128)} fusion(bf16[1024,12,64]{0,2,1:T(8,128)(2,1)S(1)} %get-tuple-element.592, bf16[2,512,12,64]{1,3,2,0:T(8,128)(2,1)} %get-tuple-element.590, s32[]{:T(128)S(6)} %copy.93), kind=kOutput, calls=%fused_computation.39.clone.1 | convolution fusion | flops 805306368 | bytes 27525124 | tf_op jit(solution)/shard_map/while/body/eval_jaxpr/qhd,khd->hqk/dot_general | solution.py:55
  361.9 13.8 %bitcast_add_fusion.5 = f32[1024,12,64]{0,2,1:T(8,128)} fusion(f32[1024,12,64]{0,2,1:T(8,128)} %get-tuple-element.573, f32[12,512,1024]{2,1,0:T(8,128)} %fusion.126, f32[12,512]{1,0:T(8,128)S(1)} %dynamic-slice_bitcast_fusion.2, pred[512,1024]{1,0:T(8,128)(4,1)S(1)} %broadcast_compare_fusion.5, pred[]{:T(512)S(6)} %compare.5, ...), kind=kOutput, calls=%fused_computation.31.clone.1 | convolution fusion | flops 832045056 | bytes 32800772 | tf_op jit(solution)/shard_map/while/body/eval_jaxpr/hqk,qhd->khd/dot_general | solution.py:116
  375.7 18.2 %multiply_reduce_fusion.9 = (f32[12,512]{1,0:T(8,128)S(1)}, f32[12,512,1024]{2,1,0:T(8,128)}) fusion(f32[12,512,1024]{2,1,0:T(8,128)} %fusion.126, f32[12,512]{1,0:T(8,128)S(1)} %dynamic-slice_bitcast_fusion.2, pred[512,1024]{1,0:T(8,128)(4,1)S(1)} %broadcast_compare_fusion.5, bf16[1024,12,64]{0,2,1:T(8,128)(2,1)} %get-tuple-element.595, ...), kind=kOutput, calls=%fused_computation.26.clone.1 | convolution fusion | flops 836757504 | bytes 53264388 | tf_op jit(solution)/shard_map/while/body/eval_jaxpr/qhd,khd->hqk/dot_general | solution.py:99
  394.0 22.1 %multiply_convert_fusion.3 = bf16[12,512,1024]{2,1,0:T(8,128)(2,1)} fusion(f32[12,512,1024]{2,1,0:T(8,128)} %get-tuple-element.521, f32[12,512,1024]{2,1,0:T(8,128)} %fusion.126, f32[12,512]{1,0:T(8,128)S(1)} %get-tuple-element.522, f32[12,512]{1,0:T(8,128)S(1)} %dynamic-slice_bitcast_fusion.2, pred[512,1024]{1,0:T(8,128)(4,1)S(1)} %broadcast_compare_fusion.5), kind=kLoop, calls=%fused_computation.25.clone.1 | loop fusion | flops 37748736 | bytes 63488000 | tf_op jit(solution)/shard_map/while/body/eval_jaxpr/convert_element_type | solution.py:104
  416.0 9.5 bitcast_dynamic-update-slice_fusion.5
  425.5 8.6 bitcast_add_fusion.4
  435.2 11.4 %fusion.126 = f32[12,512,1024]{2,1,0:T(8,128)} fusion(bf16[1024,12,64]{0,2,1:T(8,128)(2,1)S(1)} %get-tuple-element.592, bf16[2,512,12,64]{1,3,2,0:T(8,128)(2,1)} %get-tuple-element.590, s32[]{:T(128)S(6)} %copy.93), kind=kOutput, calls=%fused_computation.39.clone.1 | convolution fusion | flops 805306368 | bytes 27525124 | tf_op jit(solution)/shard_map/while/body/eval_jaxpr/qhd,khd->hqk/dot_general | solution.py:55
  446.6 14.3 %bitcast_add_fusion.5 = f32[1024,12,64]{0,2,1:T(8,128)} fusion(f32[1024,12,64]{0,2,1:T(8,128)} %get-tuple-element.573, f32[12,512,1024]{2,1,0:T(8,128)} %fusion.126, f32[12,512]{1,0:T(8,128)S(1)} %dynamic-slice_bitcast_fusion.2, pred[512,1024]{1,0:T(8,128)(4,1)S(1)} %broadcast_compare_fusion.5, pred[]{:T(512)S(6)} %compare.5, ...), kind=kOutput, calls=%fused_computation.31.clone.1 | convolution fusion | flops 832045056 | bytes 32800772 | tf_op jit(solution)/shard_map/while/body/eval_jaxpr/hqk,qhd->khd/dot_general | solution.py:116
  460.9 18.1 %multiply_reduce_fusion.9 = (f32[12,512]{1,0:T(8,128)S(1)}, f32[12,512,1024]{2,1,0:T(8,128)}) fusion(f32[12,512,1024]{2,1,0:T(8,128)} %fusion.126, f32[12,512]{1,0:T(8,128)S(1)} %dynamic-slice_bitcast_fusion.2, pred[512,1024]{1,0:T(8,128)(4,1)S(1)} %broadcast_compare_fusion.5, bf16[1024,12,64]{0,2,1:T(8,128)(2,1)} %get-tuple-element.595, ...), kind=kOutput, calls=%fused_computation.26.clone.1 | convolution fusion | flops 836757504 | bytes 53264388 | tf_op jit(solution)/shard_map/while/body/eval_jaxpr/qhd,khd->hqk/dot_general | solution.py:99
  479.0 21.2 %multiply_convert_fusion.3 = bf16[12,512,1024]{2,1,0:T(8,128)(2,1)} fusion(f32[12,512,1024]{2,1,0:T(8,128)} %get-tuple-element.521, f32[12,512,1024]{2,1,0:T(8,128)} %fusion.126, f32[12,512]{1,0:T(8,128)S(1)} %get-tuple-element.522, f32[12,512]{1,0:T(8,128)S(1)} %dynamic-slice_bitcast_fusion.2, pred[512,1024]{1,0:T(8,128)(4,1)S(1)} %broadcast_compare_fusion.5), kind=kLoop, calls=%fused_computation.25.clone.1 | loop fusion | flops 37748736 | bytes 63488000 | tf_op jit(solution)/shard_map/while/body/eval_jaxpr/convert_element_type | solution.py:104
  500.2 9.5 bitcast_dynamic-update-slice_fusion.5
  509.7 9.4 bitcast_add_fusion.4
  519.3 2.2 convert_element_type.146
  523.8 2.7 convert_reduce_fusion.3
  527.7 9.2 convolution_bitcast_fusion
  536.9 8.0 copy.71
  545.0 1.8 copy-done.10
  546.8 10.5 fusion.61
  558.7 10.2 fusion.71
  573.2 1.8 copy.65
  576.6 95.9 %reduce-scatter.16.cloned.1.call-done = f32[96,2304]{1,0:T(8,128)} async-done(((f32[768,2304]{1,0:T(8,128)}), f32[96,2304]{1,0:T(8,128)}) %reduce-scatter.16.cloned.1.call-update) | async-done | bytes 884752
  672.5 2.2 copy.72
  674.7 163.7 %reduce-scatter.12.cloned.1.call-done = f32[96,3072]{1,0:T(8,128)} async-done(((f32[768,3072]{1,0:T(8,128)}), f32[96,3072]{1,0:T(8,128)}) %reduce-scatter.12.cloned.1.call-update) | async-done | bytes 1179664 | tf_op jit(solution)/shard_map/reduce_scatter | solution.py:224
  838.4 2.2 convert_element_type.161
  840.6 164.3 %reduce-scatter.14.cloned.1.call-done = f32[384,768]{1,0:T(8,128)} async-done(((f32[3072,768]{1,0:T(8,128)}), f32[384,768]{1,0:T(8,128)}) %reduce-scatter.14.cloned.1.call-update) | async-done | bytes 1179664 | tf_op jit(solution)/shard_map/reduce_scatter | solution.py:225
  1004.9 2.1 convert_element_type.166
  1007.0 8.5 add_convert_fusion.1
  1015.5 2.6 copy.66
  1018.1 25.8 %all-reduce = bf16[3072]{0:T(1024)(128)(2,1)S(1)} all-reduce(f32[3072]{0:T(1024)S(1)} %copy-done.41), channel_id=6, replica_groups=mesh['fsdp'=8,'rep'=4] {'fsdp'}, use_global_device_ids=true, to_apply=%region_32.33.clone | all-reduce | flops 3072 | bytes 18432
  1044.0 23.7 %reduce-scatter.18.cloned.1.call-done = f32[96,8]{1,0:T(8,128)} async-done(((f32[768,8]{1,0:T(8,128)}), f32[96,8]{1,0:T(8,128)}) %reduce-scatter.18.cloned.1.call-update) | async-done | bytes 3088
  1068.6 7.9 all-reduce.1
  1077.6 44.7 %all-reduce.5.cloned.1.call-done = (bf16[96,2304]{0,1:T(8,128)(2,1)}, bf16[96,768]{1,0:T(8,128)(2,1)}, bf16[96,3072]{1,0:T(8,128)(2,1)}, bf16[384,768]{1,0:T(8,128)(2,1)}) async-done(((bf16[96,2304]{0,1:T(8,128)(2,1)}, bf16[96,768]{1,0:T(8,128)(2,1)}, bf16[96,3072]{1,0:T(8,128)(2,1)}, bf16[384,768]{1,0:T(8,128)(2,1)}), (bf16[96,2304]{0,1:T(8,128)(2,1)}, bf16[96,768]{1,0:T(8,128)(2,1)}, ...) | async-done | bytes 1769488 | tf_op jit(solution)/shard_map/psum | solution.py:229
  1122.3 2.3 copy.67
  1126.2 2.2 convert_element_type.162
  (198 shorter events, 42.8 us)
Async XLA Ops:
  7.2 54.0 %copy-start.16 = (bf16[1024,768]{1,0:T(8,128)(2,1)S(1)}, bf16[1024,768]{1,0:T(8,128)(2,1)}, u32[]{:S(2)}) copy-start(bf16[1024,768]{1,0:T(8,128)(2,1)} %param.13) | copy-start | bytes 4718596
  7.2 68.2 %all-gather.7.cloned.1.call-start = ((), (), s32[]{:S(2)}) async-start(), calls=%async_computation.5 | async-start | bytes 3981312 | tf_op jit(solution)/shard_map/all_gather | solution.py:143
  7.9 161.2 %all-gather.9.cloned.1.call-start = ((), (), s32[]{:S(2)}) async-start(), calls=%async_computation.6 | async-start | bytes 1327104 | tf_op jit(solution)/shard_map/all_gather | solution.py:144
  8.7 189.1 %all-gather.11.cloned.1.call-start = ((), (), s32[]{:S(2)}) async-start(), calls=%async_computation.7 | async-start | bytes 5308416 | tf_op jit(solution)/shard_map/all_gather | solution.py:158
  9.4 268.4 %all-gather.13.cloned.1.call-start = ((), (), s32[]{:S(2)}) async-start(), calls=%async_computation.8 | async-start | bytes 5308416 | tf_op jit(solution)/shard_map/all_gather | solution.py:159
  10.0 565.0 %reduce-scatter.10.cloned.1.call-start = ((), (), s32[]{:S(2)}) async-start(), calls=%async_computation.9 | async-start | bytes 2654208 | tf_op jit(solution)/shard_map/reduce_scatter | solution.py:222
  92.6 23.1 %copy-start.5 = (bf16[1024,12,64]{0,2,1:T(8,128)(2,1)S(1)}, bf16[1024,12,64]{0,2,1:T(8,128)(2,1)}, u32[]{:S(2)}) copy-start(bf16[1024,12,64]{0,2,1:T(8,128)(2,1)} %get-tuple-element.551) | copy-start | bytes 4718596 | tf_op jit(solution)/shard_map/while
  103.3 15.5 %copy-start = (f32[12,512,1024]{2,1,0:T(8,128)S(1)}, f32[12,512,1024]{2,1,0:T(8,128)}, u32[]{:S(2)}) copy-start(f32[12,512,1024]{2,1,0:T(8,128)} %get-tuple-element.506) | copy-start | bytes 75497472 | tf_op jit(solution)/shard_map/while
  128.4 23.0 %copy-start.5 = (bf16[1024,12,64]{0,2,1:T(8,128)(2,1)S(1)}, bf16[1024,12,64]{0,2,1:T(8,128)(2,1)}, u32[]{:S(2)}) copy-start(bf16[1024,12,64]{0,2,1:T(8,128)(2,1)} %get-tuple-element.551) | copy-start | bytes 4718596 | tf_op jit(solution)/shard_map/while
  139.0 15.5 %copy-start = (f32[12,512,1024]{2,1,0:T(8,128)S(1)}, f32[12,512,1024]{2,1,0:T(8,128)}, u32[]{:S(2)}) copy-start(f32[12,512,1024]{2,1,0:T(8,128)} %get-tuple-element.506) | copy-start | bytes 75497472 | tf_op jit(solution)/shard_map/while
  163.3 5.8 copy-start.1
  163.3 5.8 copy-start.3
  163.3 5.8 copy-start.25
  163.3 5.8 copy-start.27
  163.3 5.8 copy-start.47
  173.0 104.9 %copy-start.8 = (f32[1024,768]{0,1:T(8,128)}, f32[1024,768]{0,1:T(8,128)S(1)}, u32[]{:S(2)}) copy-start(f32[1024,768]{0,1:T(8,128)S(1)} %get-tuple-element.366) | copy-start | bytes 9437188
  173.0 24.8 %copy-start.32 = (f32[768]{0:T(1024)S(1)}, f32[768]{0:T(1024)}, u32[]{:S(2)}) copy-start(f32[768]{0:T(1024)} %get-tuple-element.292) | copy-start | bytes 9220
  173.0 24.8 %copy-start.42 = (f32[8,1,384]{2,1,0:T(1,128)S(1)}, f32[8,1,384]{2,1,0:T(1,128)}, u32[]{:S(2)}) copy-start(f32[8,1,384]{2,1,0:T(1,128)} %convert_element_type.169) | copy-start | bytes 36868
  173.0 24.8 %copy-start.44 = (f32[768]{0:T(1024)S(1)}, f32[768]{0:T(1024)}, u32[]{:S(2)}) copy-start(f32[768]{0:T(1024)} %get-tuple-element.291) | copy-start | bytes 9220
  173.0 162.6 %copy-start.30 = (f32[1024]{0:T(1024)}, f32[1024]{0:T(1024)S(1)}, u32[]{:S(2)}) copy-start(f32[1024]{0:T(1024)S(1)} %broadcast_multiply_fusion.5) | copy-start | bytes 12292
  173.4 162.2 %copy-start.39 = (f32[1024]{0:T(1024)}, f32[1024]{0:T(1024)S(1)}, u32[]{:S(2)}) copy-start(f32[1024]{0:T(1024)S(1)} %add_rsqrt_fusion.1) | copy-start | bytes 12292
  197.7 80.1 %copy-start.46 = (f32[768]{0:T(1024)S(1)}, f32[768]{0:T(1024)}, u32[]{:S(2)}) copy-start(f32[768]{0:T(1024)} %get-tuple-element.290) | copy-start | bytes 9220
  299.2 1.4 copy-start.7
  299.2 1.4 copy-start.29
  299.2 1.4 copy-start.43
  299.6 3.0 copy-start.34
  306.0 18.0 %copy-start.20 = (bf16[1024,768]{0,1:T(8,128)(2,1)}, bf16[1024,768]{0,1:T(8,128)(2,1)S(1)}, u32[]{:S(2)}) copy-start(bf16[1024,768]{0,1:T(8,128)(2,1)S(1)} %get-tuple-element.349) | copy-start | bytes 4718596
  324.1 11.6 %copy-start.9 = (f32[1024,768]{0,1:T(8,128)S(1)}, f32[1024,768]{0,1:T(8,128)}, u32[]{:S(2)}) copy-start(f32[1024,768]{0,1:T(8,128)} %copy-done.8) | copy-start | bytes 9437188
  335.7 1.7 copy-start.19
  337.4 2.9 copy-start.14
  347.1 1.7 copy-start.2
  347.1 1.7 copy-start.26
  347.1 1.7 copy-start.28
  348.6 323.9 %reduce-scatter.16.cloned.1.call-start = ((), (), s32[]{:S(2)}) async-start(), calls=%async_computation.12 | async-start | bytes 7962624
  350.3 11.7 %copy-start.6 = (bf16[2,512,12,64]{1,3,2,0:T(8,128)(2,1)S(1)}, bf16[2,512,12,64]{1,3,2,0:T(8,128)(2,1)}, u32[]{:S(2)}) copy-start(bf16[2,512,12,64]{1,3,2,0:T(8,128)(2,1)} %get-tuple-element.594) | copy-start | bytes 4718596 | tf_op jit(solution)/shard_map/while
  416.0 9.5 copy-start.4
  435.2 11.4 %copy-start.6 = (bf16[2,512,12,64]{1,3,2,0:T(8,128)(2,1)S(1)}, bf16[2,512,12,64]{1,3,2,0:T(8,128)(2,1)}, u32[]{:S(2)}) copy-start(bf16[2,512,12,64]{1,3,2,0:T(8,128)(2,1)} %get-tuple-element.594) | copy-start | bytes 4718596 | tf_op jit(solution)/shard_map/while
  500.2 9.5 copy-start.4
  519.3 2.4 copy-start.11
  521.6 4.9 copy-start.22
  523.7 2.8 copy-start.18
  523.7 3.9 copy-start.17
  526.5 1.2 copy-start.23
  544.9 1.9 copy-start.10
  544.9 1.9 copy-start.31
  544.9 1.9 copy-start.33
  544.9 1.9 copy-start.40
  544.9 1.9 copy-start.45
  544.9 293.5 %reduce-scatter.12.cloned.1.call-start = ((), (), s32[]{:S(2)}) async-start(), calls=%async_computation.10 | async-start | bytes 10616832 | tf_op jit(solution)/shard_map/reduce_scatter | solution.py:224
  557.3 1.4 copy-start.21
  557.3 447.6 %reduce-scatter.14.cloned.1.call-start = ((), (), s32[]{:S(2)}) async-start(), calls=%async_computation.11 | async-start | bytes 10616832 | tf_op jit(solution)/shard_map/reduce_scatter | solution.py:225
  568.9 0.7 copy-start.35
  568.9 0.7 copy-start.49
  568.9 0.7 copy-start.37
  568.9 0.7 copy-start.48
  569.0 0.7 copy-start.38
  569.0 1.5 copy-start.12
  569.0 2.9 copy-start.50
  569.0 4.2 copy-start.13
  569.0 498.7 %reduce-scatter.18.cloned.1.call-start = ((), (), s32[]{:S(2)}) async-start(), calls=%async_computation.13 | async-start | bytes 442368
  571.9 550.4 %all-reduce.5.cloned.1.call-start = ((), (), s32[]{:S(2)}) async-start(), calls=%async_computation.14 | async-start | bytes 3833856 | tf_op jit(solution)/shard_map/psum | solution.py:229
  576.6 430.4 %copy-start.15 = (f32[1024,768]{0,1:T(8,128)S(1)}, f32[1024,768]{0,1:T(8,128)}, u32[]{:S(2)}) copy-start(f32[1024,768]{0,1:T(8,128)} %copy-done.14) | copy-start | bytes 9437188
  1015.5 2.6 copy-start.41
  1122.3 6.1 copy-start.24
  (1 other events, 0.7 us)
Sparse Core Ops, SparseCore 0:
  10.2 65.1 all-gather.6
  77.6 38.4 all-gather.8
  118.2 79.4 all-gather.10
  199.8 78.0 all-gather.12
  348.7 65.8 reduce-scatter.9
  545.0 127.3 reduce-scatter.15
  676.5 161.8 reduce-scatter.11
  842.4 162.3 reduce-scatter.13
  1008.5 59.1 reduce-scatter.17
  1070.9 51.3 all-reduce.4
where the time goes:
time: 1140 us
  waiting for transfers between devices  574 us (50%)
  matrix products  306 us (27%)
  other arithmetic  102 us (9%)
  blocking collectives  75.5 us (7%)
  local copies, waits for them, and re-layouts  60.3 us (5%)
  between operations  17 us (1%)
    reduce_scatter x1, waiting for transfers between devices, body(): lax.psum_scatter(grad_w_down, 'fsdp', scatter_dimension=0, tiled=True)  164 us
    reduce_scatter x1, waiting for transfers between devices, body(): lax.psum_scatter(grad_w_in, 'fsdp', scatter_dimension=0, tiled=True)  164 us
    unnamed x12, waiting for transfers between devices  122 us
    psum x1, waiting for transfers between devices, body(): lax.psum(qkv_shard.astype(jnp.bfloat16), 'rep').astype(jnp.float32)  44.7 us
    dot_general x4, matrix products, masked_scores(): jnp.einsum('qhd,khd->hqk', query_part, key_split, preferred_element_type=...  44.4 us
    convert_element_type x2, other arithmetic, one_block(): grad_scores = (weights * (grad_weights - jnp.sum(weights * grad_weights,...  43.3 us
    all_gather x1, waiting for transfers between devices, body(): lax.all_gather(w_down, 'fsdp', axis=0, tiled=True)  42.5 us
    dot_general x1, matrix products, body(): jnp.dot(first_low, in_full, preferred_element_type=jnp.float32)  37.5 us
  transfers between devices with their start and end apart: 10, of which 8 were waited for; matrix products, arithmetic and copies ran while one was open for 33% of the time, Pallas kernels for 0%

commit v1 on v0

v1 whole, which is shorter than its diff:
```python
import functools
import math

import jax
import jax.numpy as jnp
from jax import lax
from jax.experimental import pallas as pl
from jax.experimental.pallas import tpu as pltpu
from jax.sharding import PartitionSpec as P

D = 768
HEADS = 12
HEAD_DIM = 64
BLOCK = 128

NORM_EPS = 1e-12
MASKED_SCORE = -1e30
SCALE_TWO = 0.125 * math.log2(math.e)
MIB = 1 << 20

NT = (((1,), (1,)), ((), ()))
TN = (((0,), (0,)), ((), ()))


def wide_dot(left, right, dims=(((1,), (0,)), ((), ()))):
    return lax.dot_general(left, right, dims, preferred_element_type=jnp.float32)


def vmem(mib):
    return pltpu.CompilerParams(vmem_limit_bytes=mib * MIB)


def layout(length_row, row_count):
    first_len = length_row[0]
    second_len = length_row[1]
    second_start = (first_len + BLOCK - 1) // BLOCK * BLOCK
    positions = jnp.arange(row_count, dtype=jnp.int32)
    in_first = positions < first_len
    in_second = (positions >= second_start) & (positions < second_start + second_len)
    doc_ids = jnp.where(in_first, 0, jnp.where(in_second, 1, 2)).astype(jnp.int32)
    return (in_first | in_second, doc_ids)


def norm_forward(hidden, gain_row, shift_row):
    centre = jnp.mean(hidden, axis=-1, keepdims=True)
    spread = jnp.mean(jnp.square(hidden - centre), axis=-1, keepdims=True)
    inverse = lax.rsqrt(spread + NORM_EPS)
    normed = (hidden - centre) * inverse
    return (normed * gain_row + shift_row, normed, inverse)


def norm_backward(grad_rows, normed, inverse, gain_row):
    scaled = grad_rows * gain_row
    grad_in = inverse * (
        scaled
        - jnp.mean(scaled, axis=-1, keepdims=True)
        - normed * jnp.mean(scaled * normed, axis=-1, keepdims=True)
    )
    return (grad_in, jnp.sum(grad_rows * normed, axis=0), jnp.sum(grad_rows, axis=0))


LANES = 384
ROWS = 96


class Place:
    def __init__(self):
        fsdp, rep = lax.axis_index("fsdp"), lax.axis_index("rep")
        self.z, self.y = fsdp // 2, fsdp % 2
        self.x, self.c = rep // 2, rep % 2
        self.scalars = jnp.stack([self.z, self.y, self.x, self.c]).astype(jnp.int32)


def swap_core(rows):
    return lax.ppermute(rows, "rep", [(i, i ^ 1) for i in range(4)])


def swap_x(rows):
    return lax.ppermute(rows, "rep", [(i, i ^ 2) for i in range(4)])


def swap_y(rows):
    return lax.ppermute(rows, "fsdp", [(i, i ^ 1) for i in range(8)])


def turn_z(rows, step):
    return lax.ppermute(rows, "fsdp", [(i, (i + 2 * step) % 8) for i in range(8)])


def pick(rows, index):
    return lax.dynamic_index_in_dim(rows, index, 0, keepdims=False)


def after(rows, *others):
    return lax.optimization_barrier((rows, *others))[0]


def gather_z(own):
    return jnp.stack([own] + [turn_z(own, step) for step in (1, 2, 3)])


def place_kernel(split_x, down, nb, near_ref, *refs):
    pieces, full_ref = refs[:-1], refs[-1]
    z, y, x, c = near_ref[0], near_ref[1], near_ref[2], near_ref[3]
    for p, piece in enumerate(pieces):
        far_y, far_x, far_c = (p & 1, (p >> 1) & 1, p >> 2) if split_x else (p & 1, 0, p >> 1)
        core = 1 - c if far_c else c
        side = 1 - x if far_x else x
        for k in range(4):
            f = lax.rem(z + 4 - k, 4) * 2 + (1 - y if far_y else y)
            for j in range(nb):
                inner = side * nb + j if split_x else j
                half = 2 * nb if split_x else nb
                if down:
                    row, col = f * (half * ROWS) + inner * ROWS, core * LANES
                else:
                    row, col = f * ROWS, (core * half + inner) * LANES
                row, col = pl.multiple_of(row, ROWS), pl.multiple_of(col, LANES)
                full_ref[pl.ds(row, ROWS), pl.ds(col, LANES)] = (
                    piece[k, j] if piece.shape[2] == ROWS else piece[k, 0, j * ROWS : (j + 1) * ROWS]
                )


def put_together(near, pieces, nb, shape, split_x, down):
    return pl.pallas_call(
        functools.partial(place_kernel, split_x, down, nb),
        out_shape=jax.ShapeDtypeStruct(shape, jnp.bfloat16),
        in_specs=[pl.BlockSpec(memory_space=pltpu.SMEM)]
        + [pl.BlockSpec(memory_space=pltpu.VMEM)] * len(pieces),
        out_specs=pl.BlockSpec(memory_space=pltpu.VMEM),
        compiler_params=vmem(16),
        cost_estimate=pl.CostEstimate(
            flops=0, bytes_accessed=4 * shape[0] * shape[1], transcendentals=0
        ),
    )(near, *pieces)


def to_blocks(shard, down):
    if down:
        return shard.reshape(4, ROWS, 2, LANES).transpose(2, 0, 1, 3).reshape(8, ROWS, LANES)
    return shard.reshape(ROWS, -1, LANES).transpose(1, 0, 2)


def own_blocks(blocks, place, split_x):
    half = blocks.shape[0] // 2
    if split_x:
        return lax.dynamic_slice_in_dim(
            blocks, place.c * half + place.x * (half // 2), half // 2, 0
        )
    return lax.dynamic_slice_in_dim(blocks, place.c * half, half, 0)


def gather_rest_of(place, pieces, nb, shape, split_x, down):
    if split_x:
        pieces = pieces + [swap_x(piece) for piece in pieces]
    pieces = pieces + [swap_core(piece) for piece in pieces]
    return put_together(place.scalars, pieces, nb, shape, split_x, down)


def gather_rest(place, near, shape, split_x, down):
    return gather_rest_of(place, [near, swap_y(near)], near.shape[1], shape, split_x, down)


def wide(rows):
    return rows.astype(jnp.float32)


def reduce_blocks(place, mate, mine, split_x):
    both = [mine, swap_core(mate)]
    if split_x:
        quarter = mine.shape[2] // 2

        def part(rows, side):
            return wide(lax.dynamic_slice_in_dim(rows, side * quarter, quarter, 2))

        sent = sum(part(rows, 1 - place.x) for rows in both).astype(jnp.bfloat16)
        came = swap_x(sent)

        def half_y(index):
            return sum(pick(part(rows, place.x), index) for rows in both) + wide(pick(came, index))
    else:

        def half_y(index):
            return sum(wide(pick(rows, index)) for rows in both)

    came_y = swap_y(half_y(1 - place.y).astype(jnp.bfloat16))
    near = half_y(place.y) + wide(came_y)
    total = pick(near, place.z)
    for step in (1, 2, 3):
        sent = pick(near, (place.z + step) % 4).astype(jnp.bfloat16)
        total = total + wide(turn_z(sent, step))
    total = total.astype(jnp.bfloat16)
    if split_x:
        far = swap_x(total)
        total = jnp.where(
            place.x == 0, jnp.concatenate([total, far]), jnp.concatenate([far, total])
        )
    else:
        total = (wide(total) + wide(swap_x(total))).astype(jnp.bfloat16)
    far = swap_core(total)
    return jnp.where(
        place.c == 0, jnp.concatenate([total, far]), jnp.concatenate([far, total])
    ).astype(jnp.float32)


def document_columns(doc_ids):
    hot = (doc_ids[:, None] == jnp.arange(128)[None, :]) & (jnp.arange(128) < 3)[None, :]
    other = (~hot) & (jnp.arange(128) < 3)[None, :]
    return (
        jnp.where(other, MASKED_SCORE, 0.0).astype(jnp.bfloat16),
        hot.astype(jnp.bfloat16),
    )


def head_part(rows, side):
    column = lax.broadcasted_iota(jnp.int32, rows.shape, 1)
    inside = column < HEAD_DIM if side == 0 else column >= HEAD_DIM
    return jnp.where(inside, rows, jnp.zeros_like(rows))


def attend_kernel(q_ref, k_ref, v_ref, qx_ref, kx_ref, ctx_ref, lse_ref, out_scr):
    rows = q_ref.shape[0]
    step = min(256, rows)
    keys = jnp.concatenate([k_ref[...], kx_ref[...]], axis=1)
    values_t = v_ref[...].T
    for side in range(2):
        queries = jnp.concatenate([head_part(q_ref[...], side), qx_ref[...]], axis=1)
        mine = slice(side * HEAD_DIM, (side + 1) * HEAD_DIM)
        for at in range(0, rows, step):
            scores = wide_dot(keys, queries[at : at + step], NT)
            top = jnp.max(scores, axis=0, keepdims=True)
            weights = jnp.exp2((scores - top) * SCALE_TWO)
            total = jnp.sum(weights, axis=0, keepdims=True)
            attended = wide_dot(values_t[mine], weights.astype(jnp.bfloat16))
            out_scr[mine, at : at + step] = attended * (1.0 / total)
            lse_ref[0, side : side + 1, at : at + step] = top * SCALE_TWO + jnp.log2(total)
    ctx_ref[...] = out_scr[...].T.astype(jnp.bfloat16)


def attention_forward(queries, key_rows, value_rows, doc_columns):
    rows = queries.shape[0]
    pair = pl.BlockSpec((rows, 128), lambda h: (0, h))
    fixed = pl.BlockSpec((rows, 128), lambda h: (0, 0))
    return pl.pallas_call(
        attend_kernel,
        grid=(HEADS // 2,),
        out_shape=(
            jax.ShapeDtypeStruct((rows, D), jnp.bfloat16),
            jax.ShapeDtypeStruct((HEADS // 2, 2, rows), jnp.float32),
        ),
        in_specs=[pair, pair, pair, fixed, fixed],
        out_specs=(pair, pl.BlockSpec((1, 2, rows), lambda h: (h, 0, 0))),
        scratch_shapes=[pltpu.VMEM((128, rows), jnp.float32)],
        compiler_params=vmem(40),
        cost_estimate=pl.CostEstimate(
            flops=8 * HEADS * rows * rows * 128, bytes_accessed=8 * rows * D, transcendentals=HEADS * rows * rows
        ),
    )(queries, key_rows, value_rows, *doc_columns)


def attend_back_kernel(
    q_ref, k_ref, v_ref, do_ref, ctx_ref, lse_ref, qx_ref, kx_ref,
    dq_ref, dk_ref, dv_ref, sums_ref, dq_scr,
):
    rows = q_ref.shape[0]
    step = min(256, rows)
    grads = do_ref[...]
    product_t = (grads.astype(jnp.float32) * ctx_ref[...].astype(jnp.float32)).T
    keys_t = k_ref[...].T
    heads = []
    for side in range(2):
        mine = slice(side * HEAD_DIM, (side + 1) * HEAD_DIM)
        q_side = head_part(q_ref[...], side)
        heads.append((
            mine,
            q_side,
            jnp.concatenate([q_side, qx_ref[...]], axis=1),
            head_part(grads, side),
            jnp.sum(product_t[mine], axis=0, keepdims=True),
            lse_ref[0, side : side + 1, :],
        ))
    value_sum = jnp.zeros((1, 128), jnp.float32)
    for at in range(0, rows, step):
        here = slice(at, at + step)
        keys = jnp.concatenate([k_ref[here], kx_ref[here]], axis=1)
        key_grad = jnp.zeros((step, 128), jnp.float32)
        value_grad = jnp.zeros((step, 128), jnp.float32)
        for mine, q_side, queries, do_side, delta, lse in heads:
            weights = jnp.exp2(wide_dot(keys, queries, NT) * SCALE_TWO - lse)
            grad_weights = wide_dot(v_ref[here], do_side, NT)
            grad_scores = (weights * (grad_weights - delta)).astype(jnp.bfloat16)
            value_grad += wide_dot(weights.astype(jnp.bfloat16), do_side)
            key_grad += wide_dot(grad_scores, q_side)
            query_grad = wide_dot(keys_t[mine, here], grad_scores)
            if at == 0:
                dq_scr[mine] = query_grad
            else:
                dq_scr[mine] += query_grad
        dk_ref[here] = (key_grad * 0.125).astype(jnp.bfloat16)
        value_low = value_grad.astype(jnp.bfloat16)
        dv_ref[here] = value_low
        value_sum += jnp.sum(value_low.astype(jnp.float32), axis=0, keepdims=True)
    query_low = (dq_scr[...].T * 0.125).astype(jnp.bfloat16)
    dq_ref[...] = query_low
    query_sum = jnp.sum(query_low.astype(jnp.float32), axis=0, keepdims=True)
    sums_ref[...] = jnp.concatenate([query_sum, value_sum], axis=0)


def attention_backward(queries, key_rows, value_rows, doc_columns, grad_context, context, log_total):
    rows = queries.shape[0]
    pair = pl.BlockSpec((rows, 128), lambda h: (0, h))
    fixed = pl.BlockSpec((rows, 128), lambda h: (0, 0))
    like = jax.ShapeDtypeStruct((rows, D), jnp.bfloat16)
    return pl.pallas_call(
        attend_back_kernel,
        grid=(HEADS // 2,),
        out_shape=(like, like, like, jax.ShapeDtypeStruct((2, D), jnp.float32)),
        in_specs=[pair] * 5 + [pl.BlockSpec((1, 2, rows), lambda h: (h, 0, 0)), fixed, fixed],
        out_specs=(pair, pair, pair, pl.BlockSpec((2, 128), lambda h: (0, h))),
        scratch_shapes=[pltpu.VMEM((128, rows), jnp.float32)],
        compiler_params=vmem(40),
        cost_estimate=pl.CostEstimate(
            flops=20 * HEADS * rows * rows * 128, bytes_accessed=18 * rows * D, transcendentals=HEADS * rows * rows
        ),
    )(queries, key_rows, value_rows, grad_context, context, log_total, *doc_columns)


def gelu_kernel(x_ref, w_ref, b_ref, act_ref, slope_ref):
    inner = wide_dot(x_ref[...], w_ref[...]) + b_ref[...].astype(jnp.float32)
    phi = 0.5 + 0.5 * lax.erf(inner * math.sqrt(0.5))
    bell = jnp.exp(inner * inner * -0.5) * (1.0 / math.sqrt(2.0 * math.pi))
    act_ref[...] = (inner * phi).astype(jnp.bfloat16)
    slope_ref[...] = (phi + inner * bell).astype(jnp.bfloat16)


def gelu_forward(rows, w_in, b_in):
    count, units = rows.shape[0], w_in.shape[1]
    tile = 512
    column = pl.BlockSpec((count, tile), lambda j: (0, j))
    like = jax.ShapeDtypeStruct((count, units), jnp.bfloat16)
    return pl.pallas_call(
        gelu_kernel,
        grid=(units // tile,),
        out_shape=(like, like),
        in_specs=[
            pl.BlockSpec((count, D), lambda j: (0, 0)),
            pl.BlockSpec((D, tile), lambda j: (0, j)),
            pl.BlockSpec((1, tile), lambda j: (0, j)),
        ],
        out_specs=(column, column),
        compiler_params=vmem(40),
        cost_estimate=pl.CostEstimate(
            flops=2 * count * D * units, bytes_accessed=4 * count * units, transcendentals=2 * count * units
        ),
    )(rows, w_in, b_in.reshape(1, -1))


def inner_grad_kernel(g_ref, w_ref, slope_ref, out_ref, sum_ref):
    grad = wide_dot(g_ref[...], w_ref[...], NT) * slope_ref[...].astype(jnp.float32)
    low = grad.astype(jnp.bfloat16)
    out_ref[...] = low
    sum_ref[...] = jnp.sum(low.astype(jnp.float32), axis=0, keepdims=True)


def inner_backward(grad_mlp, w_down, slope):
    count, units = slope.shape
    tile = 512
    column = pl.BlockSpec((count, tile), lambda j: (0, j))
    return pl.pallas_call(
        inner_grad_kernel,
        grid=(units // tile,),
        out_shape=(
            jax.ShapeDtypeStruct((count, units), jnp.bfloat16),
            jax.ShapeDtypeStruct((1, units), jnp.float32),
        ),
        in_specs=[
            pl.BlockSpec((count, D), lambda j: (0, 0)),
            pl.BlockSpec((tile, D), lambda j: (j, 0)),
            column,
        ],
        out_specs=(column, pl.BlockSpec((1, tile), lambda j: (0, j))),
        compiler_params=vmem(40),
        cost_estimate=pl.CostEstimate(
            flops=2 * count * D * units, bytes_accessed=6 * count * units, transcendentals=0
        ),
    )(grad_mlp, w_down, slope)


def weight_grad_kernel(down, side_ref, a_ref, b_ref, out_ref):
    total = wide_dot(a_ref[...], b_ref[...], TN).astype(jnp.bfloat16)
    for part in range(total.shape[0] // ROWS):
        piece = total[part * ROWS : (part + 1) * ROWS]
        if down:
            out_ref[0, 0, part] = piece
        else:
            out_ref[part % 2, part // 2, 0] = piece


def weight_grad(side, left, right, down=False):
    count = left.shape[0]
    if down:
        grid, nb = (8,), 4
        specs = [
            pl.BlockSpec((count, LANES), lambda f, s: (0, f)),
            pl.BlockSpec((count, LANES), lambda f, s: (0, s[0])),
        ]
        out = pl.BlockSpec((1, 1, nb, ROWS, LANES), lambda f, s: (lax.rem(f, 2), lax.div(f, 2), 0, 0, 0))
    else:
        nb = right.shape[1] // LANES // 2
        grid = (nb,)
        specs = [
            pl.BlockSpec((count, D), lambda j, s: (0, 0)),
            pl.BlockSpec((count, LANES), lambda j, s: (0, s[0] * nb + j)),
        ]
        out = pl.BlockSpec((2, 4, 1, ROWS, LANES), lambda j, s: (0, 0, j, 0, 0))
    return pl.pallas_call(
        functools.partial(weight_grad_kernel, down),
        grid_spec=pltpu.PrefetchScalarGridSpec(
            num_scalar_prefetch=1, grid=grid, in_specs=specs, out_specs=out
        ),
        out_shape=jax.ShapeDtypeStruct((2, 4, nb, ROWS, LANES), jnp.bfloat16),
        compiler_params=vmem(40),
        cost_estimate=pl.CostEstimate(
            flops=2 * count * D * nb * LANES, bytes_accessed=count * (D + nb * LANES) * 2, transcendentals=0
        ),
    )(side.reshape(1), left, right)


def small_to_blocks(grad_vectors, grad_b_in, place):
    vectors = jnp.pad(
        grad_vectors.reshape(8, 4, 2, ROWS).transpose(2, 1, 0, 3),
        ((0, 0), (0, 0), (0, 8), (0, LANES - ROWS)),
    )
    biases = jnp.pad(
        grad_b_in.reshape(4, 2, 1, LANES).transpose(1, 0, 2, 3), ((0, 0), (0, 0), (0, 15), (0, 0))
    )
    vectors, biases = vectors.astype(jnp.bfloat16), biases.astype(jnp.bfloat16)
    return (
        jnp.where(place.c == 0, biases, vectors),
        jnp.where(place.c == 0, vectors, biases),
    )


class Staged:
    def __init__(self, w_qkv, vectors, w_attn_out, w_in, b_in, w_down):
        self.place = place = Place()
        small = jnp.pad(
            jnp.concatenate([b_in[None], jnp.pad(vectors, ((0, 0), (0, LANES - ROWS)))]),
            ((0, 7), (0, 0)),
        )
        own = own_blocks(to_blocks(w_qkv, False), place, False)
        own = jnp.concatenate([own.reshape(-1, LANES), small])[None]
        near = gather_z(own)
        near_y = swap_y(near)
        self.qkv = gather_rest_of(place, [near, near_y], 3, (D, 3 * D), False, False)
        edge = [near[:, 0, 3 * ROWS :], near_y[:, 0, 3 * ROWS :]]
        edge = jnp.stack(
            [
                jnp.stack(
                    [
                        jnp.where(place.y == y, *(pick(e, (place.z - z) % 4) for e in edge))
                        for y in range(2)
                    ]
                )
                for z in range(4)
            ]
        )
        self.b_in = edge[:, :, 0].reshape(-1)
        self.vectors = edge[:, :, 1:9, :ROWS].transpose(2, 0, 1, 3).reshape(8, D)
        blocks = after(own_blocks(to_blocks(w_attn_out, False), place, False), near)
        near_out = gather_z(blocks)
        blocks = after(own_blocks(to_blocks(w_in, False), place, True), near)
        near_in = gather_z(blocks)
        blocks = after(own_blocks(to_blocks(w_down, True), place, True), near_out, near_in)
        near_down = gather_z(blocks)
        self.out = gather_rest(place, near_out, (D, D), False, False)
        self.w_in = gather_rest(place, near_in, (D, 4 * D), True, False)
        self.down = gather_rest(place, near_down, (4 * D, D), True, True)

    def reduce(self, left, right, down=False, split_x=False, small=None):
        place = self.place
        mate = weight_grad(1 - place.c, left, right, down)
        mine = weight_grad(place.c, left, right, down)
        if small is not None:
            nb = mate.shape[2]
            mate, mine = (
                jnp.concatenate([rows.reshape(2, 4, nb * ROWS, LANES), edge], axis=2)[:, :, None]
                for rows, edge in zip((mate, mine), small_to_blocks(*small, place), strict=True)
            )
        shard = reduce_blocks(place, mate, mine, split_x)
        if small is not None:
            edge = shard[:, nb * ROWS :]
            shard = shard[:, : nb * ROWS].reshape(2 * nb, ROWS, LANES)
        if down:
            shard = shard.reshape(2, 4, ROWS, LANES).transpose(1, 2, 0, 3).reshape(LANES, D)
        else:
            shard = shard.transpose(1, 0, 2).reshape(ROWS, -1)
        return shard if small is None else (shard, edge[0, :8, :ROWS], edge[1, 0])


class Plain:
    def __init__(self, w_qkv, vectors, w_attn_out, w_in, b_in, w_down):
        def whole(rows, axis=0):
            return lax.all_gather(rows, "fsdp", axis=axis, tiled=True)

        self.qkv, self.vectors, self.out = whole(w_qkv), whole(vectors, 1), whole(w_attn_out)
        self.w_in, self.b_in, self.down = whole(w_in), whole(b_in), whole(w_down)

    def own(self, total, axis=0):
        shard = lax.psum_scatter(total, "fsdp", scatter_dimension=axis, tiled=True)
        return lax.psum(shard.astype(jnp.bfloat16), "rep").astype(jnp.float32)

    def reduce(self, left, right, down=False, split_x=False, small=None):
        shard = self.own(wide_dot(left, right, TN))
        return shard if small is None else (shard, self.own(small[0], 1), self.own(small[1]))


def body(staged, tokens, lengths, w_qkv, vectors, w_attn_out, w_in, b_in, w_down, cotangent):
    row_count = tokens.shape[0]
    valid_rows, doc_ids = layout(lengths[0], row_count)
    doc_columns = document_columns(doc_ids)
    weights = (Staged if staged else Plain)(w_qkv, vectors, w_attn_out, w_in, b_in, w_down)
    vector_wide = weights.vectors.astype(jnp.float32)
    projected = jnp.dot(tokens, weights.qkv, preferred_element_type=jnp.float32)
    queries = (projected[:, :D] + vector_wide[0]).astype(jnp.bfloat16)
    key_rows = projected[:, D : 2 * D].astype(jnp.bfloat16)
    value_rows = (projected[:, 2 * D :] + vector_wide[1]).astype(jnp.bfloat16)
    context, log_total = attention_forward(queries, key_rows, value_rows, doc_columns)
    attn_branch = jnp.dot(context, weights.out, preferred_element_type=jnp.float32) + vector_wide[2]
    first_norm, normed_one, inverse_one = norm_forward(
        tokens.astype(jnp.float32) + attn_branch, vector_wide[3], vector_wide[4]
    )
    first_low = first_norm.astype(jnp.bfloat16)
    active, slope = gelu_forward(first_low, weights.w_in, weights.b_in)
    mlp_branch = jnp.dot(active, weights.down, preferred_element_type=jnp.float32) + vector_wide[5]
    second_norm, normed_two, inverse_two = norm_forward(
        first_norm + mlp_branch, vector_wide[6], vector_wide[7]
    )
    layer_out = jnp.where(valid_rows[:, None], second_norm, 0.0).astype(jnp.bfloat16)
    grad_out = jnp.where(valid_rows[:, None], cotangent.astype(jnp.float32), 0.0)
    grad_two, gain_two, shift_two = norm_backward(grad_out, normed_two, inverse_two, vector_wide[6])
    grad_mlp = grad_two.astype(jnp.bfloat16)
    down_shard = weights.reduce(active, grad_mlp, down=True, split_x=False)
    grad_inner, grad_b_in = inner_backward(grad_mlp, weights.down, slope)
    in_shard = weights.reduce(first_low, grad_inner, split_x=True)
    grad_b_down = jnp.sum(grad_mlp.astype(jnp.float32), axis=0)
    grad_first = grad_two + wide_dot(grad_inner, weights.w_in, NT)
    grad_one, gain_one, shift_one = norm_backward(
        grad_first, normed_one, inverse_one, vector_wide[3]
    )
    grad_attn = grad_one.astype(jnp.bfloat16)
    grad_context = wide_dot(grad_attn, weights.out, NT).astype(jnp.bfloat16)
    out_shard = weights.reduce(context, grad_attn)
    query_low, key_low, value_low, column_sums = attention_backward(
        queries, key_rows, value_rows, doc_columns, grad_context, context, log_total
    )
    grad_proj = jnp.concatenate([query_low, key_low, value_low], axis=1)
    grad_vectors = jnp.concatenate(
        [
            column_sums,
            jnp.stack(
                [
                    jnp.sum(grad_attn.astype(jnp.float32), axis=0),
                    gain_one,
                    shift_one,
                    grad_b_down,
                    gain_two,
                    shift_two,
                ]
            ),
        ]
    )
    qkv_shard, vector_shard, bias_shard = weights.reduce(
        tokens, grad_proj, small=(grad_vectors, grad_b_in.reshape(-1))
    )
    grad_tokens = (grad_one + wide_dot(grad_proj, weights.qkv, NT)).astype(jnp.bfloat16)
    return (
        layer_out,
        grad_tokens,
        qkv_shard,
        vector_shard,
        out_shard,
        in_shard,
        bias_shard,
        down_shard,
    )


def solution(mesh):
    staged = mesh.shape["fsdp"] == 8 and mesh.shape["rep"] == 4
    return jax.shard_map(
        functools.partial(body, staged),
        mesh=mesh,
        in_specs=(
            P(("fsdp", "rep"), None),
            P(("fsdp", "rep"), None),
            P("fsdp", None),
            P(None, "fsdp"),
            P("fsdp", None),
            P("fsdp", None),
            P("fsdp"),
            P("fsdp", None),
            P(("fsdp", "rep"), None),
        ),
        out_specs=(
            P(("fsdp", "rep"), None),
            P(("fsdp", "rep"), None),
            P("fsdp", None),
            P(None, "fsdp"),
            P("fsdp", None),
            P("fsdp", None),
            P("fsdp"),
            P("fsdp", None),
        ),
        check_vma=False,
    )
```

time: 1140 us -> 429 us (0.38)
  waiting for transfers between devices: 574 us -> 116 us
  matrix products: 306 us -> 30.4 us
  Pallas kernels: 0 us -> 131 us
  blocking collectives: 75.5 us -> 0 us
  other arithmetic: 102 us -> 32.1 us
  starting transfers between devices: 0.4 us -> 66.9 us
  local copies, waits for them, and re-layouts: 60.3 us -> 39.8 us
  between operations: 17 us -> 3.81 us
    reduce_scatter x3 -> x0, waiting for transfers between devices: 328 us -> none  [the longest x1 164 us: body(): lax.psum_scatter(grad_w_down, 'fsdp', scatter_dimension=0, tiled=True)]
    dot_general x26 -> x6, matrix products: 306 us -> 30.4 us  [the longest x3 17.7 us: wide_dot(): lax.dot_general(left, right, dims, preferred_element_type=jnp.float32)]
    pallas_call x0 -> x16, Pallas kernels: none -> 131 us  [the longest x1 39.7 us: attention_backward(): pl.pallas_call(attend_back_kernel, grid=(HEADS // 2,), out_shape=(like, l...]
    unnamed x12 -> x0, waiting for transfers between devices: 122 us -> none
    ppermute x0 -> x61, waiting for transfers between devices: none -> 116 us  [the longest x24 72.6 us: turn_z(): lax.ppermute(rows, 'fsdp', [(i, (i + 2 * step) % 8) for i in range(8)])]
    all_gather x4 -> x0, waiting for transfers between devices: 79.4 us -> none  [the longest x1 42.5 us: body(): lax.all_gather(w_down, 'fsdp', axis=0, tiled=True)]
    ppermute x0 -> x61, starting transfers between devices: none -> 66.9 us  [the longest x20 25.4 us: swap_core(): return lax.ppermute(rows, 'rep', [(i, i ^ 1) for i in range(4)])]
    convert_element_type x12 -> x19, other arithmetic: 58.2 us -> 10.9 us  [the longest x4 4.62 us: reduce_blocks(): came_y = swap_y(half_y(1 - place.y).astype(jnp.bfloat16))]
  transfers between devices with their start and end apart: 10 -> 61, of which waited for: 8 -> 17; matrix products, arithmetic and copies ran while one was open for 33% -> 9% of each run, Pallas kernels for 0% -> 18%
where the time goes in v1:
time: 429 us; the launch traced here: 421 us
  Pallas kernels  131 us (31%)
  waiting for transfers between devices  116 us (27%)
  starting transfers between devices  66.9 us (16%)
  local copies, waits for them, and re-layouts  39.8 us (9%)
  other arithmetic  32.1 us (7%)
  matrix products  30.4 us (7%)
    ppermute x24, waiting for transfers between devices, turn_z(): lax.ppermute(rows, 'fsdp', [(i, (i + 2 * step) % 8) for i in range(8)])  72.6 us
    pallas_call x1, Pallas kernels, attention_backward(): pl.pallas_call(attend_back_kernel, grid=(HEADS // 2,), out_shape=(like, l...  39.7 us
    pallas_call x8, Pallas kernels, weight_grad(): pl.pallas_call(functools.partial(weight_grad_kernel, down), grid_spec=plt...  32.7 us
    pallas_call x1, Pallas kernels, attention_forward(): pl.pallas_call(attend_kernel, grid=(HEADS // 2,), out_shape=(jax.ShapeDty...  31.4 us
    unnamed x131, local copies, waits for them, and re-layouts  28.4 us
    ppermute x9, waiting for transfers between devices, swap_x(): return lax.ppermute(rows, 'rep', [(i, i ^ 2) for i in range(4)])  27.3 us
    ppermute x20, starting transfers between devices, swap_core(): return lax.ppermute(rows, 'rep', [(i, i ^ 1) for i in range(4)])  25.4 us
    ppermute x24, starting transfers between devices, turn_z(): lax.ppermute(rows, 'fsdp', [(i, (i + 2 * step) % 8) for i in range(8)])  24.5 us
  transfers between devices with their start and end apart: 61, of which 17 were waited for; matrix products, arithmetic and copies ran while one was open for 9% of the time, Pallas kernels for 18%

profile of v1, /device:TPU:25, one launch (start us, length us, event | category | flops | bytes accessed | tf_op | source)
XLA Modules:
  0.0 420.8 jit_solution(13853713739325587976)
XLA Ops:
  0.7 1.6 reshape.588
  10.5 14.9 %collective-permute-done.1 = bf16[1,304,384]{2,1,0:T(8,128)(2,1)S(1)} collective-permute-done((bf16[1,304,384]{2,1,0:T(8,128)(2,1)S(1)}, bf16[1,304,384]{2,1,0:T(8,128)(2,1)S(1)}, u32[]{:S(2)}, u32[]{:S(2)}) %collective-permute-start.1) | collective-permute-done | bytes 233504 | tf_op jit(solution)/shard_map/ppermute | solution.py:87
  29.4 2.1 collective-permute-start.7
  32.0 1.5 collective-permute-start.12
  35.4 6.5 %collective-permute-start.8 = (bf16[1,96,384]{2,1,0:T(8,128)(2,1)S(1)}, bf16[1,96,384]{2,1,0:T(8,128)(2,1)S(1)}, u32[]{:S(2)}, u32[]{:S(2)}) collective-permute-start(bf16[1,96,384]{2,1,0:T(8,128)(2,1)S(1)} %bitcast.236), channel_id=1, source_target_pairs={{0,24},{4,28},{8,0},{12,4},{16,8},{20,12},{24,16},{28,20},{1,25},{... | collective-permute-start | bytes 221192 | tf_op jit(solution)/shard_map/ppermute | solution.py:87
  42.0 5.3 %collective-permute-done.8 = bf16[1,96,384]{2,1,0:T(8,128)(2,1)S(1)} collective-permute-done((bf16[1,96,384]{2,1,0:T(8,128)(2,1)S(1)}, bf16[1,96,384]{2,1,0:T(8,128)(2,1)S(1)}, u32[]{:S(2)}, u32[]{:S(2)}) %collective-permute-start.8) | collective-permute-done | bytes 73760 | tf_op jit(solution)/shard_map/ppermute | solution.py:87
  47.6 3.4 collective-permute-done.13
  51.2 2.7 collective-permute-start.23
  55.8 1.7 collective-permute-start.10
  57.5 6.1 %collective-permute-done.23 = bf16[2,96,384]{2,1,0:T(8,128)(2,1)S(1)} collective-permute-done((bf16[2,96,384]{2,1,0:T(8,128)(2,1)S(1)}, bf16[2,96,384]{2,1,0:T(8,128)(2,1)S(1)}, u32[]{:S(2)}, u32[]{:S(2)}) %collective-permute-start.23) | collective-permute-done | bytes 147488 | tf_op jit(solution)/shard_map/ppermute | solution.py:87
  65.8 3.5 collective-permute-done.24
  73.0 3.0 collective-permute-start.18
  79.9 1.9 collective-permute-done.15.refs_1_
  84.5 2.1 shard_map.152
  86.6 3.8 convolution_bitcast_fusion
  91.6 31.4 %shard_map.153 = (bf16[1024,768]{1,0:T(8,128)(2,1)S(1)}, f32[6,2,1024]{2,1,0:T(2,128)S(1)}) custom-call(bf16[1024,768]{1,0:T(8,128)(2,1)S(1)} %get-tuple-element.56.q_ref, bf16[1024,768]{1,0:T(8,128)(2,1)S(1)} %slice.129.k_ref, bf16[1024,768]{1,0:T(8,128)(2,1)S(1)} %get-tuple-element.55.v_ref, bf16[1024,128]{1,0:T(8,128)(2,1)S(1)} %copy-done.42, ...), custom_call_target="tpu_custom_call" | custom-call | flops 12884901888 | bytes 6291456 | tf_op jit(solution)/shard_map/pallas_call | solution.py:244
  123.1 1.6 fusion.58
  124.7 4.3 %collective-permute-start.19 = (bf16[4,2,96,384]{3,2,1,0:T(8,128)(2,1)S(1)}, bf16[4,2,96,384]{3,2,1,0:T(8,128)(2,1)S(1)}, u32[]{:S(2)}, u32[]{:S(2)}) collective-permute-start(bf16[4,2,96,384]{3,2,1,0:T(8,128)(2,1)S(1)} %collective-permute-done.15.refs_1_), channel_id=1, source_target_pairs={{0,1},{1,0},{2,3},{3,2},{4,5},{5,4},{6,7},{7,6},{8,9},{9,8},{10,11... | collective-permute-start | bytes 1769480 | tf_op jit(solution)/shard_map/ppermute | solution.py:75
  132.3 11.3 %collective-permute-done.27.refs_3_ = bf16[4,2,96,384]{3,2,1,0:T(8,128)(2,1)S(1)} collective-permute-done((bf16[4,2,96,384]{3,2,1,0:T(8,128)(2,1)S(1)}, bf16[4,2,96,384]{3,2,1,0:T(8,128)(2,1)S(1)}, u32[]{:S(2)}, u32[]{:S(2)}) %collective-permute-start.27) | collective-permute-done | bytes 589856 | tf_op jit(solution)/shard_map/ppermute | solution.py:79
  145.5 1.7 shard_map.155.w_ref
  147.2 11.9 %shard_map.156 = (bf16[1024,3072]{1,0:T(8,128)(2,1)S(1)}, bf16[1024,3072]{1,0:T(8,128)(2,1)}) custom-call(bf16[1024,768]{1,0:T(8,128)(2,1)S(1)} %fusion.5.x_ref.a_ref, bf16[768,3072]{1,0:T(8,128)(2,1)S(1)} %shard_map.155.w_ref, bf16[1,3072]{1,0:T(2,128)(2,1)S(1)} %bitcast.217), custom_call_target="tpu_custom_call" | custom-call | flops 4831838208 | bytes 12582912 | tf_op jit(solution)/shard_map/pallas_call | solution.py:341
  160.1 1.5 copy-done.39
  161.6 1.6 shard_map.157.w_ref
  163.2 7.3 %fusion.59 = (f32[1024]{0:T(1024)S(1)}, f32[1024,768]{1,0:T(8,128)S(1)}) fusion(f32[768]{0:T(1024)S(1)} %add.446, bf16[1024,3072]{1,0:T(8,128)(2,1)S(1)} %get-tuple-element.24.a_ref, bf16[3072,768]{1,0:T(8,128)(2,1)S(1)} %shard_map.157.w_ref, f32[768]{0:T(1024)S(1)} %add.441, f32[768]{0:T(1024)S(1)} %mul.114, f32[1024]{0:T(1024)S(1)} %add_rsqrt_fusion.1, ...), kind=kOutput, calls=%fused_computation.193 | convolution fusion | flops 4837342208 | bytes 17323008 | tf_op jit(solution)/shard_map/dot_general | solution.py:535
  171.1 2.0 copy-done.47
  173.1 3.1 multiply_reduce_fusion
  176.1 1.5 fusion.54
  177.7 9.0 %shard_map.158 = (bf16[1024,3072]{1,0:T(8,128)(2,1)S(1)}, f32[1,3072]{1,0:T(1,128)S(1)}) custom-call(bf16[1024,768]{1,0:T(8,128)(2,1)S(1)} %get-tuple-element.51.g_ref.b_ref, bf16[3072,768]{1,0:T(8,128)(2,1)S(1)} %shard_map.157.w_ref, bf16[1024,3072]{1,0:T(8,128)(2,1)} %get-tuple-element.26.slope_ref), custom_call_target="tpu_custom_call" | custom-call | flops 4831838208 | bytes 18874368 | tf_op jit(solution)/shard_map/pallas_call | solution.py:369
  186.7 11.3 %multiply_reduce_fusion.1 = (bf16[768]{0:T(1024)(128)(2,1)S(1)}, f32[1024]{0:T(1024)S(1)}, f32[1024]{0:T(1024)S(1)}, bf16[768]{0:T(1024)(128)(2,1)S(1)}, f32[1024,768]{1,0:T(8,128)}) fusion(f32[1024,768]{1,0:T(8,128)} %copy-done.44, f32[1024]{0:T(1024)S(1)} %add_rsqrt_fusion.1, f32[1024]{0:T(1024)S(1)} %broadcast_multiply_fusion.5, f32[768]{0:T(1024)S(1)} %mul.114, ...), kind=kOutput, calls=%fused_computation.7 | convolution fusion | flops 4846776320 | bytes 22063104 | tf_op jit(solution)/shard_map/dot_general | solution.py:26
  198.1 3.8 fusion.56
  201.9 1.4 convolution_convert_fusion.do_ref
  204.4 39.7 %shard_map.159 = (bf16[1024,768]{1,0:T(8,128)(2,1)S(1)}, bf16[1024,768]{1,0:T(8,128)(2,1)S(1)}, bf16[1024,768]{1,0:T(8,128)(2,1)S(1)}, f32[2,768]{1,0:T(2,128)S(1)}) custom-call(bf16[1024,768]{1,0:T(8,128)(2,1)S(1)} %copy-done.30, bf16[1024,768]{1,0:T(8,128)(2,1)S(1)} %slice.129.k_ref, bf16[1024,768]{1,0:T(8,128)(2,1)S(1)} %copy-done.28, ...), custom_call_target="tpu_custom_call" | custom-call | flops 32212254720 | bytes 14155776 | tf_op jit(solution)/shard_map/pallas_call | solution.py:314
  247.2 1.6 constant_dynamic-update-slice_fusion.2
  250.5 3.4 shard_map.161
  254.0 2.1 copy-done
  256.2 1.5 maximum_bitcast_fusion
  258.1 2.8 copy-done.2
  260.9 6.7 %shard_map.167 = bf16[2,4,4,96,384]{4,3,2,1,0:T(8,128)(2,1)} custom-call(s32[1]{0:T(128)} %bitcast.48.side_ref, bf16[1024,3072]{1,0:T(8,128)(2,1)S(1)} %copy-done.2, bf16[1024,768]{1,0:T(8,128)(2,1)S(1)} %copy-done.7), custom_call_target="tpu_custom_call" | custom-call | flops 2415919104 | bytes 4718592 | tf_op jit(solution)/shard_map/pallas_call | solution.py:416
  269.1 1.9 shard_map.163
  271.4 2.8 copy-done.4
  274.2 5.3 %shard_map.165 = bf16[2,4,4,96,384]{4,3,2,1,0:T(8,128)(2,1)} custom-call(s32[1]{0:T(128)} %bitcast.48.side_ref, bf16[1024,768]{1,0:T(8,128)(2,1)S(1)} %fusion.5.x_ref.a_ref, bf16[1024,3072]{1,0:T(8,128)(2,1)S(1)} %copy-done.4), custom_call_target="tpu_custom_call" | custom-call | flops 2415919104 | bytes 4718592 | tf_op jit(solution)/shard_map/pallas_call | solution.py:416
  281.5 3.5 shard_map.160
  285.0 2.8 copy-done.5
  287.8 4.9 %shard_map.164 = bf16[2,4,4,96,384]{4,3,2,1,0:T(8,128)(2,1)S(1)} custom-call(s32[1]{0:T(128)} %bitcast.5.side_ref, bf16[1024,768]{1,0:T(8,128)(2,1)S(1)} %fusion.5.x_ref.a_ref, bf16[1024,3072]{1,0:T(8,128)(2,1)S(1)} %copy-done.5), custom_call_target="tpu_custom_call" | custom-call | flops 2415919104 | bytes 4718592 | tf_op jit(solution)/shard_map/pallas_call | solution.py:416
  294.3 1.5 fusion.6
  297.4 5.9 %shard_map.166 = bf16[2,4,4,96,384]{4,3,2,1,0:T(8,128)(2,1)S(1)} custom-call(s32[1]{0:T(128)} %bitcast.5.side_ref, bf16[1024,3072]{1,0:T(8,128)(2,1)S(1)} %bitcast.210, bf16[1024,768]{1,0:T(8,128)(2,1)S(1)} %copy-done.8), custom_call_target="tpu_custom_call" | custom-call | flops 2415919104 | bytes 4718592 | tf_op jit(solution)/shard_map/pallas_call | solution.py:416
  306.1 1.6 fusion.9
  307.6 14.6 %collective-permute-done.33 = bf16[4,1,304,384]{3,2,1,0:T(8,128)(2,1)S(1)} collective-permute-done((bf16[4,1,304,384]{3,2,1,0:T(8,128)(2,1)S(1)}, bf16[4,1,304,384]{3,2,1,0:T(8,128)(2,1)S(1)}, u32[]{:S(2)}, u32[]{:S(2)}) %collective-permute-start.33) | collective-permute-done | bytes 933920 | tf_op jit(solution)/shard_map/ppermute | solution.py:83
  322.5 1.5 fusion.8
  327.0 1.6 add_convert_fusion.2
  328.6 2.3 collective-permute-done.34
  332.1 11.2 %collective-permute-done.35 = bf16[1,304,384]{2,1,0:T(8,128)(2,1)S(1)} collective-permute-done((bf16[1,304,384]{2,1,0:T(8,128)(2,1)S(1)}, bf16[1,304,384]{2,1,0:T(8,128)(2,1)S(1)}, u32[]{:S(2)}, u32[]{:S(2)}) %collective-permute-start.35) | collective-permute-done | bytes 233504 | tf_op jit(solution)/shard_map/ppermute | solution.py:87
  344.8 2.0 collective-permute-start.45
  346.8 1.5 dynamic-slice_convert_fusion
  348.4 12.3 %collective-permute-done.37 = bf16[1,304,384]{2,1,0:T(8,128)(2,1)S(1)} collective-permute-done((bf16[1,304,384]{2,1,0:T(8,128)(2,1)S(1)}, bf16[1,304,384]{2,1,0:T(8,128)(2,1)S(1)}, u32[]{:S(2)}, u32[]{:S(2)}) %collective-permute-start.37) | collective-permute-done | bytes 233504 | tf_op jit(solution)/shard_map/ppermute | solution.py:79
  360.7 3.7 collective-permute-start.38
  364.4 1.8 bitcast_add_fusion
  370.3 5.0 %add_convert_fusion = bf16[1024,768]{1,0:T(8,128)(2,1)} fusion(f32[1024,768]{1,0:T(8,128)S(1)} %copy-done.48, bf16[1024,2304]{1,0:T(8,128)(2,1)S(1)} %bitcast.208, bf16[768,2304]{1,0:T(8,128)(2,1)S(1)} %copy-done.21), kind=kOutput, calls=%fused_computation.8 | convolution fusion | flops 3625451520 | bytes 12976128 | tf_op jit(solution)/shard_map/dot_general | solution.py:26
  376.1 17.7 %collective-permute-done.57 = bf16[4,96,384]{2,1,0:T(8,128)(2,1)S(1)} collective-permute-done((bf16[4,96,384]{2,1,0:T(8,128)(2,1)S(1)}, bf16[4,96,384]{2,1,0:T(8,128)(2,1)S(1)}, u32[]{:S(2)}, u32[]{:S(2)}) %collective-permute-start.57) | collective-permute-done | bytes 294944 | tf_op jit(solution)/shard_map/ppermute | solution.py:87
  395.3 2.0 collective-permute-start.50
  398.7 3.1 collective-permute-done.59
  401.9 1.8 collective-permute-start.60
  403.7 6.2 %collective-permute-done.50 = bf16[2,96,384]{2,1,0:T(8,128)(2,1)S(1)} collective-permute-done((bf16[2,96,384]{2,1,0:T(8,128)(2,1)S(1)}, bf16[2,96,384]{2,1,0:T(8,128)(2,1)S(1)}, u32[]{:S(2)}, u32[]{:S(2)}) %collective-permute-start.50) | collective-permute-done | bytes 147488 | tf_op jit(solution)/shard_map/ppermute | solution.py:87
  414.0 2.9 collective-permute-start.53
  (326 shorter events, 73.0 us)
Async XLA Ops:
  3.9 6.6 %collective-permute-start = (bf16[1,304,384]{2,1,0:T(8,128)(2,1)S(1)}, bf16[1,304,384]{2,1,0:T(8,128)(2,1)S(1)}, u32[]{:S(2)}, u32[]{:S(2)}) collective-permute-start(bf16[1,304,384]{2,1,0:T(8,128)(2,1)S(1)} %get-tuple-element.70), channel_id=1, source_target_pairs={{0,8},{4,12},{8,16},{12,20},{16,24},{20,28},{24,0},{28,4},{1,9},{5... | collective-permute-start | bytes 700424 | tf_op jit(solution)/shard_map/ppermute | solution.py:87
  4.0 21.4 %collective-permute-start.1 = (bf16[1,304,384]{2,1,0:T(8,128)(2,1)S(1)}, bf16[1,304,384]{2,1,0:T(8,128)(2,1)S(1)}, u32[]{:S(2)}, u32[]{:S(2)}) collective-permute-start(bf16[1,304,384]{2,1,0:T(8,128)(2,1)S(1)} %get-tuple-element.70), channel_id=1, source_target_pairs={{0,16},{4,20},{8,24},{12,28},{16,0},{20,4},{24,8},{28,12},{1,17},{... | collective-permute-start | bytes 700424 | tf_op jit(solution)/shard_map/ppermute | solution.py:87
  5.3 20.1 %collective-permute-start.2 = (bf16[1,304,384]{2,1,0:T(8,128)(2,1)S(1)}, bf16[1,304,384]{2,1,0:T(8,128)(2,1)S(1)}, u32[]{:S(2)}, u32[]{:S(2)}) collective-permute-start(bf16[1,304,384]{2,1,0:T(8,128)(2,1)S(1)} %get-tuple-element.70), channel_id=1, source_target_pairs={{0,24},{4,28},{8,0},{12,4},{16,8},{20,12},{24,16},{28,20},{1,25},{... | collective-permute-start | bytes 700424 | tf_op jit(solution)/shard_map/ppermute | solution.py:87
  27.2 37.7 %collective-permute-start.3 = (bf16[4,1,304,384]{3,2,1,0:T(8,128)(2,1)S(1)}, bf16[4,1,304,384]{3,2,1,0:T(8,128)(2,1)}, u32[]{:S(2)}, u32[]{:S(2)}) collective-permute-start(bf16[4,1,304,384]{3,2,1,0:T(8,128)(2,1)S(1)} %pad_maximum_fusion.refs_0_), channel_id=1, source_target_pairs={{0,4},{4,0},{8,12},{12,8},{16,20},{20,16},{24,28},{28,24},{1,5},{5... | collective-permute-start | bytes 2801672 | tf_op jit(solution)/shard_map/ppermute | solution.py:83
  29.4 5.2 %collective-permute-start.6 = (bf16[1,96,384]{2,1,0:T(8,128)(2,1)S(1)}, bf16[1,96,384]{2,1,0:T(8,128)(2,1)S(1)}, u32[]{:S(2)}, u32[]{:S(2)}) collective-permute-start(bf16[1,96,384]{2,1,0:T(8,128)(2,1)S(1)} %bitcast.234), channel_id=1, source_target_pairs={{0,8},{4,12},{8,16},{12,20},{16,24},{20,28},{24,0},{28,4},{1,9},{5... | collective-permute-start | bytes 221192 | tf_op jit(solution)/shard_map/ppermute | solution.py:87
  29.4 6.0 %collective-permute-start.7 = (bf16[1,96,384]{2,1,0:T(8,128)(2,1)S(1)}, bf16[1,96,384]{2,1,0:T(8,128)(2,1)S(1)}, u32[]{:S(2)}, u32[]{:S(2)}) collective-permute-start(bf16[1,96,384]{2,1,0:T(8,128)(2,1)S(1)} %bitcast.235), channel_id=1, source_target_pairs={{0,16},{4,20},{8,24},{12,28},{16,0},{20,4},{24,8},{28,12},{1,17},{... | collective-permute-start | bytes 221192 | tf_op jit(solution)/shard_map/ppermute | solution.py:87
  32.0 15.6 %collective-permute-start.12 = (bf16[2,96,384]{2,1,0:T(8,128)(2,1)S(1)}, bf16[2,96,384]{2,1,0:T(8,128)(2,1)S(1)}, u32[]{:S(2)}, u32[]{:S(2)}) collective-permute-start(bf16[2,96,384]{2,1,0:T(8,128)(2,1)S(1)} %bitcast.229), channel_id=1, source_target_pairs={{0,8},{4,12},{8,16},{12,20},{16,24},{20,28},{24,0},{28,4},{1,9},{5... | collective-permute-start | bytes 442376 | tf_op jit(solution)/shard_map/ppermute | solution.py:87
  33.5 17.5 %collective-permute-start.13 = (bf16[2,96,384]{2,1,0:T(8,128)(2,1)S(1)}, bf16[2,96,384]{2,1,0:T(8,128)(2,1)S(1)}, u32[]{:S(2)}, u32[]{:S(2)}) collective-permute-start(bf16[2,96,384]{2,1,0:T(8,128)(2,1)S(1)} %bitcast.230), channel_id=1, source_target_pairs={{0,16},{4,20},{8,24},{12,28},{16,0},{20,4},{24,8},{28,12},{1,17},{... | collective-permute-start | bytes 442376 | tf_op jit(solution)/shard_map/ppermute | solution.py:87
  34.7 16.3 %collective-permute-start.14 = (bf16[2,96,384]{2,1,0:T(8,128)(2,1)S(1)}, bf16[2,96,384]{2,1,0:T(8,128)(2,1)S(1)}, u32[]{:S(2)}, u32[]{:S(2)}) collective-permute-start(bf16[2,96,384]{2,1,0:T(8,128)(2,1)S(1)} %bitcast.231), channel_id=1, source_target_pairs={{0,24},{4,28},{8,0},{12,4},{16,8},{20,12},{24,16},{28,20},{1,25},{... | collective-permute-start | bytes 442376 | tf_op jit(solution)/shard_map/ppermute | solution.py:87
  35.4 11.8 %collective-permute-start.8 = (bf16[1,96,384]{2,1,0:T(8,128)(2,1)S(1)}, bf16[1,96,384]{2,1,0:T(8,128)(2,1)S(1)}, u32[]{:S(2)}, u32[]{:S(2)}) collective-permute-start(bf16[1,96,384]{2,1,0:T(8,128)(2,1)S(1)} %bitcast.236), channel_id=1, source_target_pairs={{0,24},{4,28},{8,0},{12,4},{16,8},{20,12},{24,16},{28,20},{1,25},{... | collective-permute-start | bytes 221192 | tf_op jit(solution)/shard_map/ppermute | solution.py:87
  47.3 16.3 %collective-permute-start.9 = (bf16[4,1,96,384]{3,2,1,0:T(8,128)(2,1)S(1)}, bf16[4,1,96,384]{3,2,1,0:T(8,128)(2,1)S(1)}, u32[]{:S(2)}, u32[]{:S(2)}) collective-permute-start(bf16[4,1,96,384]{3,2,1,0:T(8,128)(2,1)S(1)} %pad_maximum_fusion.3.refs_0_), channel_id=1, source_target_pairs={{0,4},{4,0},{8,12},{12,8},{16,20},{20,16},{24,28},{28,24},{1,5},{5... | collective-permute-start | bytes 884744 | tf_op jit(solution)/shard_map/ppermute | solution.py:83
  51.1 4.7 %collective-permute-start.22 = (bf16[2,96,384]{2,1,0:T(8,128)(2,1)S(1)}, bf16[2,96,384]{2,1,0:T(8,128)(2,1)S(1)}, u32[]{:S(2)}, u32[]{:S(2)}) collective-permute-start(bf16[2,96,384]{2,1,0:T(8,128)(2,1)S(1)} %constant_dynamic-slice_fusion), channel_id=1, source_target_pairs={{0,8},{4,12},{8,16},{12,20},{16,24},{20,28},{24,0},{28,4},{1,9},{5... | collective-permute-start | bytes 442376 | tf_op jit(solution)/shard_map/ppermute | solution.py:87
  51.2 12.4 %collective-permute-start.23 = (bf16[2,96,384]{2,1,0:T(8,128)(2,1)S(1)}, bf16[2,96,384]{2,1,0:T(8,128)(2,1)S(1)}, u32[]{:S(2)}, u32[]{:S(2)}) collective-permute-start(bf16[2,96,384]{2,1,0:T(8,128)(2,1)S(1)} %constant_dynamic-slice_fusion), channel_id=1, source_target_pairs={{0,16},{4,20},{8,24},{12,28},{16,0},{20,4},{24,8},{28,12},{1,17},{... | collective-permute-start | bytes 442376 | tf_op jit(solution)/shard_map/ppermute | solution.py:87
  54.7 28.3 %collective-permute-start.4 = (bf16[4,1,304,384]{3,2,1,0:T(8,128)(2,1)S(1)}, bf16[4,1,304,384]{3,2,1,0:T(8,128)(2,1)}, u32[]{:S(2)}, u32[]{:S(2)}) collective-permute-start(bf16[4,1,304,384]{3,2,1,0:T(8,128)(2,1)S(1)} %pad_maximum_fusion.refs_0_), channel_id=1, source_target_pairs={{0,1},{1,0},{2,3},{3,2},{4,5},{5,4},{6,7},{7,6},{8,9},{9,8},{10,11... | collective-permute-start | bytes 2801672 | tf_op jit(solution)/shard_map/ppermute | solution.py:75
  55.8 15.9 %collective-permute-start.10 = (bf16[4,1,96,384]{3,2,1,0:T(8,128)(2,1)S(1)}, bf16[4,1,96,384]{3,2,1,0:T(8,128)(2,1)}, u32[]{:S(2)}, u32[]{:S(2)}) collective-permute-start(bf16[4,1,96,384]{3,2,1,0:T(8,128)(2,1)S(1)} %pad_maximum_fusion.3.refs_0_), channel_id=1, source_target_pairs={{0,1},{1,0},{2,3},{3,2},{4,5},{5,4},{6,7},{7,6},{8,9},{9,8},{10,11... | collective-permute-start | bytes 884744 | tf_op jit(solution)/shard_map/ppermute | solution.py:75
  63.5 5.8 %collective-permute-start.24 = (bf16[2,96,384]{2,1,0:T(8,128)(2,1)S(1)}, bf16[2,96,384]{2,1,0:T(8,128)(2,1)S(1)}, u32[]{:S(2)}, u32[]{:S(2)}) collective-permute-start(bf16[2,96,384]{2,1,0:T(8,128)(2,1)S(1)} %constant_dynamic-slice_fusion), channel_id=1, source_target_pairs={{0,24},{4,28},{8,0},{12,4},{16,8},{20,12},{24,16},{28,20},{1,25},{... | collective-permute-start | bytes 442376 | tf_op jit(solution)/shard_map/ppermute | solution.py:87
  63.5 9.5 %collective-permute-start.11 = (bf16[4,1,96,384]{3,2,1,0:T(8,128)(2,1)S(1)}, bf16[4,1,96,384]{3,2,1,0:T(8,128)(2,1)}, u32[]{:S(2)}, u32[]{:S(2)}) collective-permute-start(bf16[4,1,96,384]{3,2,1,0:T(8,128)(2,1)S(1)} %collective-permute-done.9.refs_1_), channel_id=1, source_target_pairs={{0,1},{1,0},{2,3},{3,2},{4,5},{5,4},{6,7},{7,6},{8,9},{9,8},{10,11... | collective-permute-start | bytes 884744 | tf_op jit(solution)/shard_map/ppermute | solution.py:75
  64.9 19.3 %collective-permute-start.5 = (bf16[4,1,304,384]{3,2,1,0:T(8,128)(2,1)}, bf16[4,1,304,384]{3,2,1,0:T(8,128)(2,1)}, u32[]{:S(2)}, u32[]{:S(2)}) collective-permute-start(bf16[4,1,304,384]{3,2,1,0:T(8,128)(2,1)} %collective-permute-done.3.refs_1_), channel_id=1, source_target_pairs={{0,1},{1,0},{2,3},{3,2},{4,5},{5,4},{6,7},{7,6},{8,9},{9,8},{10,11... | collective-permute-start | bytes 2801672 | tf_op jit(solution)/shard_map/ppermute | solution.py:75
  69.3 12.4 %collective-permute-start.15 = (bf16[4,2,96,384]{3,2,1,0:T(8,128)(2,1)S(1)}, bf16[4,2,96,384]{3,2,1,0:T(8,128)(2,1)S(1)}, u32[]{:S(2)}, u32[]{:S(2)}) collective-permute-start(bf16[4,2,96,384]{3,2,1,0:T(8,128)(2,1)S(1)} %pad_maximum_fusion.1.refs_0_), channel_id=1, source_target_pairs={{0,4},{4,0},{8,12},{12,8},{16,20},{20,16},{24,28},{28,24},{1,5},{5... | collective-permute-start | bytes 1769480 | tf_op jit(solution)/shard_map/ppermute | solution.py:83
  71.7 53.0 %collective-permute-start.16 = (bf16[4,2,96,384]{3,2,1,0:T(8,128)(2,1)S(1)}, bf16[4,2,96,384]{3,2,1,0:T(8,128)(2,1)}, u32[]{:S(2)}, u32[]{:S(2)}) collective-permute-start(bf16[4,2,96,384]{3,2,1,0:T(8,128)(2,1)S(1)} %pad_maximum_fusion.1.refs_0_), channel_id=1, source_target_pairs={{0,2},{1,3},{2,0},{3,1},{4,6},{5,7},{6,4},{7,5},{8,10},{9,11},{10,... | collective-permute-start | bytes 1769480 | tf_op jit(solution)/shard_map/ppermute | solution.py:79
  73.0 56.0 %collective-permute-start.18 = (bf16[4,2,96,384]{3,2,1,0:T(8,128)(2,1)S(1)}, bf16[4,2,96,384]{3,2,1,0:T(8,128)(2,1)}, u32[]{:S(2)}, u32[]{:S(2)}) collective-permute-start(bf16[4,2,96,384]{3,2,1,0:T(8,128)(2,1)S(1)} %pad_maximum_fusion.1.refs_0_), channel_id=1, source_target_pairs={{0,1},{1,0},{2,3},{3,2},{4,5},{5,4},{6,7},{7,6},{8,9},{9,8},{10,11... | collective-permute-start | bytes 1769480 | tf_op jit(solution)/shard_map/ppermute | solution.py:75
  81.8 47.4 %collective-permute-start.25 = (bf16[4,2,96,384]{3,2,1,0:T(8,128)(2,1)S(1)}, bf16[4,2,96,384]{3,2,1,0:T(8,128)(2,1)S(1)}, u32[]{:S(2)}, u32[]{:S(2)}) collective-permute-start(bf16[4,2,96,384]{3,2,1,0:T(8,128)(2,1)S(1)} %pad_maximum_fusion.2.refs_0_), channel_id=1, source_target_pairs={{0,4},{4,0},{8,12},{12,8},{16,20},{20,16},{24,28},{28,24},{1,5},{5... | collective-permute-start | bytes 1769480 | tf_op jit(solution)/shard_map/ppermute | solution.py:83
  83.0 48.6 %collective-permute-start.26 = (bf16[4,2,96,384]{3,2,1,0:T(8,128)(2,1)S(1)}, bf16[4,2,96,384]{3,2,1,0:T(8,128)(2,1)S(1)}, u32[]{:S(2)}, u32[]{:S(2)}) collective-permute-start(bf16[4,2,96,384]{3,2,1,0:T(8,128)(2,1)S(1)} %pad_maximum_fusion.2.refs_0_), channel_id=1, source_target_pairs={{0,2},{1,3},{2,0},{3,1},{4,6},{5,7},{6,4},{7,5},{8,10},{9,11},{10,... | collective-permute-start | bytes 1769480 | tf_op jit(solution)/shard_map/ppermute | solution.py:79
  84.2 46.1 %collective-permute-start.17 = (bf16[4,2,96,384]{3,2,1,0:T(8,128)(2,1)S(1)}, bf16[4,2,96,384]{3,2,1,0:T(8,128)(2,1)S(1)}, u32[]{:S(2)}, u32[]{:S(2)}) collective-permute-start(bf16[4,2,96,384]{3,2,1,0:T(8,128)(2,1)S(1)} %collective-permute-done.15.refs_1_), channel_id=1, source_target_pairs={{0,2},{1,3},{2,0},{3,1},{4,6},{5,7},{6,4},{7,5},{8,10},{9,11},{10,... | collective-permute-start | bytes 1769480 | tf_op jit(solution)/shard_map/ppermute | solution.py:79
  91.2 31.8 %copy-start.27 = (bf16[1024,768]{1,0:T(8,128)(2,1)}, bf16[1024,768]{1,0:T(8,128)(2,1)S(1)}, u32[]{:S(2)}) copy-start(bf16[1024,768]{1,0:T(8,128)(2,1)S(1)} %get-tuple-element.55.v_ref) | copy-start | bytes 4718596
  91.2 31.8 %copy-start.29 = (bf16[1024,768]{1,0:T(8,128)(2,1)}, bf16[1024,768]{1,0:T(8,128)(2,1)S(1)}, u32[]{:S(2)}) copy-start(bf16[1024,768]{1,0:T(8,128)(2,1)S(1)} %get-tuple-element.56.q_ref) | copy-start | bytes 4718596
  123.1 80.3 %copy-start.14 = (bf16[1024,768]{1,0:T(8,128)(2,1)}, bf16[1024,768]{1,0:T(8,128)(2,1)S(1)}, u32[]{:S(2)}) copy-start(bf16[1024,768]{1,0:T(8,128)(2,1)S(1)} %get-tuple-element.21.ctx_ref.a_ref) | copy-start | bytes 4718596
  124.7 7.0 %collective-permute-start.19 = (bf16[4,2,96,384]{3,2,1,0:T(8,128)(2,1)S(1)}, bf16[4,2,96,384]{3,2,1,0:T(8,128)(2,1)S(1)}, u32[]{:S(2)}, u32[]{:S(2)}) collective-permute-start(bf16[4,2,96,384]{3,2,1,0:T(8,128)(2,1)S(1)} %collective-permute-done.15.refs_1_), channel_id=1, source_target_pairs={{0,1},{1,0},{2,3},{3,2},{4,5},{5,4},{6,7},{7,6},{8,9},{9,8},{10,11... | collective-permute-start | bytes 1769480 | tf_op jit(solution)/shard_map/ppermute | solution.py:75
  129.0 3.1 collective-permute-start.20
  129.1 14.5 %collective-permute-start.27 = (bf16[4,2,96,384]{3,2,1,0:T(8,128)(2,1)S(1)}, bf16[4,2,96,384]{3,2,1,0:T(8,128)(2,1)S(1)}, u32[]{:S(2)}, u32[]{:S(2)}) collective-permute-start(bf16[4,2,96,384]{3,2,1,0:T(8,128)(2,1)S(1)} %collective-permute-done.25.refs_1_), channel_id=1, source_target_pairs={{0,2},{1,3},{2,0},{3,1},{4,6},{5,7},{6,4},{7,5},{8,10},{9,11},{10,... | collective-permute-start | bytes 1769480 | tf_op jit(solution)/shard_map/ppermute | solution.py:79
  130.3 15.1 %collective-permute-start.21 = (bf16[4,2,96,384]{3,2,1,0:T(8,128)(2,1)S(1)}, bf16[4,2,96,384]{3,2,1,0:T(8,128)(2,1)S(1)}, u32[]{:S(2)}, u32[]{:S(2)}) collective-permute-start(bf16[4,2,96,384]{3,2,1,0:T(8,128)(2,1)S(1)} %collective-permute-done.17.refs_3_), channel_id=1, source_target_pairs={{0,1},{1,0},{2,3},{3,2},{4,5},{5,4},{6,7},{7,6},{8,9},{9,8},{10,11... | collective-permute-start | bytes 1769480 | tf_op jit(solution)/shard_map/ppermute | solution.py:75
  131.6 27.6 %collective-permute-start.28 = (bf16[4,2,96,384]{3,2,1,0:T(8,128)(2,1)S(1)}, bf16[4,2,96,384]{3,2,1,0:T(8,128)(2,1)S(1)}, u32[]{:S(2)}, u32[]{:S(2)}) collective-permute-start(bf16[4,2,96,384]{3,2,1,0:T(8,128)(2,1)S(1)} %pad_maximum_fusion.2.refs_0_), channel_id=1, source_target_pairs={{0,1},{1,0},{2,3},{3,2},{4,5},{5,4},{6,7},{7,6},{8,9},{9,8},{10,11... | collective-permute-start | bytes 1769480 | tf_op jit(solution)/shard_map/ppermute | solution.py:75
  131.7 27.5 %collective-permute-start.29 = (bf16[4,2,96,384]{3,2,1,0:T(8,128)(2,1)S(1)}, bf16[4,2,96,384]{3,2,1,0:T(8,128)(2,1)S(1)}, u32[]{:S(2)}, u32[]{:S(2)}) collective-permute-start(bf16[4,2,96,384]{3,2,1,0:T(8,128)(2,1)S(1)} %collective-permute-done.25.refs_1_), channel_id=1, source_target_pairs={{0,1},{1,0},{2,3},{3,2},{4,5},{5,4},{6,7},{7,6},{8,9},{9,8},{10,11... | collective-permute-start | bytes 1769480 | tf_op jit(solution)/shard_map/ppermute | solution.py:75
  132.2 27.1 %collective-permute-start.30 = (bf16[4,2,96,384]{3,2,1,0:T(8,128)(2,1)S(1)}, bf16[4,2,96,384]{3,2,1,0:T(8,128)(2,1)S(1)}, u32[]{:S(2)}, u32[]{:S(2)}) collective-permute-start(bf16[4,2,96,384]{3,2,1,0:T(8,128)(2,1)S(1)} %collective-permute-done.26.refs_2_), channel_id=1, source_target_pairs={{0,1},{1,0},{2,3},{3,2},{4,5},{5,4},{6,7},{7,6},{8,9},{9,8},{10,11... | collective-permute-start | bytes 1769480 | tf_op jit(solution)/shard_map/ppermute | solution.py:75
  143.6 16.5 %collective-permute-start.31 = (bf16[4,2,96,384]{3,2,1,0:T(8,128)(2,1)S(1)}, bf16[4,2,96,384]{3,2,1,0:T(8,128)(2,1)}, u32[]{:S(2)}, u32[]{:S(2)}) collective-permute-start(bf16[4,2,96,384]{3,2,1,0:T(8,128)(2,1)S(1)} %collective-permute-done.27.refs_3_), channel_id=1, source_target_pairs={{0,1},{1,0},{2,3},{3,2},{4,5},{5,4},{6,7},{7,6},{8,9},{9,8},{10,11... | collective-permute-start | bytes 1769480 | tf_op jit(solution)/shard_map/ppermute | solution.py:75
  257.7 36.6 %collective-permute-start.32 = (bf16[2,4,1,304,384]{4,3,1,2,0:T(8,128)(2,1)}, bf16[2,4,1,304,384]{4,3,1,2,0:T(8,128)(2,1)}, u32[]{:S(2)}, u32[]{:S(2)}) collective-permute-start(bf16[2,4,1,304,384]{4,3,1,2,0:T(8,128)(2,1)} %maximum_bitcast_fusion), channel_id=1, source_target_pairs={{0,1},{1,0},{2,3},{3,2},{4,5},{5,4},{6,7},{7,6},{8,9},{9,8},{10,11... | collective-permute-start | bytes 5603336 | tf_op jit(solution)/shard_map/ppermute | solution.py:75
  267.6 37.4 %collective-permute-start.54 = (bf16[2,4,4,96,384]{4,3,2,1,0:T(8,128)(2,1)}, bf16[2,4,4,96,384]{4,3,2,1,0:T(8,128)(2,1)}, u32[]{:S(2)}, u32[]{:S(2)}) collective-permute-start(bf16[2,4,4,96,384]{4,3,2,1,0:T(8,128)(2,1)} %shard_map.167), channel_id=1, source_target_pairs={{0,1},{1,0},{2,3},{3,2},{4,5},{5,4},{6,7},{7,6},{8,9},{9,8},{10,11... | collective-permute-start | bytes 7077896 | tf_op jit(solution)/shard_map/ppermute | solution.py:75
  270.9 21.8 %collective-permute-start.39 = (bf16[2,4,1,96,384]{4,3,2,1,0:T(8,128)(2,1)}, bf16[2,4,1,96,384]{4,3,2,1,0:T(8,128)(2,1)}, u32[]{:S(2)}, u32[]{:S(2)}) collective-permute-start(bf16[2,4,1,96,384]{4,3,2,1,0:T(8,128)(2,1)} %shard_map.163), channel_id=1, source_target_pairs={{0,1},{1,0},{2,3},{3,2},{4,5},{5,4},{6,7},{7,6},{8,9},{9,8},{10,11... | collective-permute-start | bytes 1769480 | tf_op jit(solution)/shard_map/ppermute | solution.py:75
  279.5 46.2 %collective-permute-start.46 = (bf16[2,4,4,96,384]{4,3,2,1,0:T(8,128)(2,1)}, bf16[2,4,4,96,384]{4,3,2,1,0:T(8,128)(2,1)}, u32[]{:S(2)}, u32[]{:S(2)}) collective-permute-start(bf16[2,4,4,96,384]{4,3,2,1,0:T(8,128)(2,1)} %shard_map.165), channel_id=1, source_target_pairs={{0,1},{1,0},{2,3},{3,2},{4,5},{5,4},{6,7},{7,6},{8,9},{9,8},{10,11... | collective-permute-start | bytes 7077896 | tf_op jit(solution)/shard_map/ppermute | solution.py:75
  294.0 9.3 %collective-permute-start.40 = (bf16[4,1,96,384]{3,2,0,1:T(8,128)(2,1)S(1)}, bf16[4,1,96,384]{3,2,0,1:T(8,128)(2,1)S(1)}, u32[]{:S(2)}, u32[]{:S(2)}) collective-permute-start(bf16[4,1,96,384]{3,2,0,1:T(8,128)(2,1)S(1)} %fusion.27), channel_id=1, source_target_pairs={{0,4},{4,0},{8,12},{12,8},{16,20},{20,16},{24,28},{28,24},{1,5},{5... | collective-permute-start | bytes 884744 | tf_op jit(solution)/shard_map/ppermute | solution.py:83
  295.9 26.4 %collective-permute-start.33 = (bf16[4,1,304,384]{3,2,1,0:T(8,128)(2,1)S(1)}, bf16[4,1,304,384]{3,2,1,0:T(8,128)(2,1)S(1)}, u32[]{:S(2)}, u32[]{:S(2)}) collective-permute-start(bf16[4,1,304,384]{3,2,1,0:T(8,128)(2,1)S(1)} %fusion.6), channel_id=1, source_target_pairs={{0,4},{4,0},{8,12},{12,8},{16,20},{20,16},{24,28},{28,24},{1,5},{5... | collective-permute-start | bytes 2801672 | tf_op jit(solution)/shard_map/ppermute | solution.py:83
  304.5 19.6 %collective-permute-start.41 = (bf16[1,96,384]{2,1,0:T(8,128)(2,1)S(1)}, bf16[1,96,384]{2,1,0:T(8,128)(2,1)S(1)}, u32[]{:S(2)}, u32[]{:S(2)}) collective-permute-start(bf16[1,96,384]{2,1,0:T(8,128)(2,1)S(1)} %get-tuple-element.67), channel_id=1, source_target_pairs={{0,8},{4,12},{8,16},{12,20},{16,24},{20,28},{24,0},{28,4},{1,9},{5... | collective-permute-start | bytes 221192 | tf_op jit(solution)/shard_map/ppermute | solution.py:87
  305.0 19.7 %collective-permute-start.42 = (bf16[1,96,384]{2,1,0:T(8,128)(2,1)S(1)}, bf16[1,96,384]{2,1,0:T(8,128)(2,1)S(1)}, u32[]{:S(2)}, u32[]{:S(2)}) collective-permute-start(bf16[1,96,384]{2,1,0:T(8,128)(2,1)S(1)} %get-tuple-element.68), channel_id=1, source_target_pairs={{0,16},{4,20},{8,24},{12,28},{16,0},{20,4},{24,8},{28,12},{1,17},{... | collective-permute-start | bytes 221192 | tf_op jit(solution)/shard_map/ppermute | solution.py:87
  305.0 19.6 %collective-permute-start.43 = (bf16[1,96,384]{2,1,0:T(8,128)(2,1)S(1)}, bf16[1,96,384]{2,1,0:T(8,128)(2,1)S(1)}, u32[]{:S(2)}, u32[]{:S(2)}) collective-permute-start(bf16[1,96,384]{2,1,0:T(8,128)(2,1)S(1)} %fusion.48), channel_id=1, source_target_pairs={{0,24},{4,28},{8,0},{12,4},{16,8},{20,12},{24,16},{28,20},{1,25},{... | collective-permute-start | bytes 221192 | tf_op jit(solution)/shard_map/ppermute | solution.py:87
  322.3 42.1 %collective-permute-start.55 = (bf16[4,4,96,384]{3,2,1,0:T(8,128)(2,1)S(1)}, bf16[4,4,96,384]{3,2,1,0:T(8,128)(2,1)S(1)}, u32[]{:S(2)}, u32[]{:S(2)}) collective-permute-start(bf16[4,4,96,384]{3,2,1,0:T(8,128)(2,1)S(1)} %fusion.9), channel_id=1, source_target_pairs={{0,4},{4,0},{8,12},{12,8},{16,20},{20,16},{24,28},{28,24},{1,5},{5... | collective-permute-start | bytes 3538952 | tf_op jit(solution)/shard_map/ppermute | solution.py:83
  324.1 6.8 %collective-permute-start.34 = (bf16[1,304,384]{2,1,0:T(8,128)(2,1)S(1)}, bf16[1,304,384]{2,1,0:T(8,128)(2,1)S(1)}, u32[]{:S(2)}, u32[]{:S(2)}) collective-permute-start(bf16[1,304,384]{2,1,0:T(8,128)(2,1)S(1)} %get-tuple-element.61), channel_id=1, source_target_pairs={{0,8},{4,12},{8,16},{12,20},{16,24},{20,28},{24,0},{28,4},{1,9},{5... | collective-permute-start | bytes 700424 | tf_op jit(solution)/shard_map/ppermute | solution.py:87
  324.7 18.7 %collective-permute-start.35 = (bf16[1,304,384]{2,1,0:T(8,128)(2,1)S(1)}, bf16[1,304,384]{2,1,0:T(8,128)(2,1)S(1)}, u32[]{:S(2)}, u32[]{:S(2)}) collective-permute-start(bf16[1,304,384]{2,1,0:T(8,128)(2,1)S(1)} %get-tuple-element.63), channel_id=1, source_target_pairs={{0,16},{4,20},{8,24},{12,28},{16,0},{20,4},{24,8},{28,12},{1,17},{... | collective-permute-start | bytes 700424 | tf_op jit(solution)/shard_map/ppermute | solution.py:87
  324.7 18.7 %collective-permute-start.36 = (bf16[1,304,384]{2,1,0:T(8,128)(2,1)S(1)}, bf16[1,304,384]{2,1,0:T(8,128)(2,1)S(1)}, u32[]{:S(2)}, u32[]{:S(2)}) collective-permute-start(bf16[1,304,384]{2,1,0:T(8,128)(2,1)S(1)} %get-tuple-element.62), channel_id=1, source_target_pairs={{0,24},{4,28},{8,0},{12,4},{16,8},{20,12},{24,16},{28,20},{1,25},{... | collective-permute-start | bytes 700424 | tf_op jit(solution)/shard_map/ppermute | solution.py:87
  325.7 19.0 %collective-permute-start.44 = (bf16[1,96,384]{2,1,0:T(8,128)(2,1)S(1)}, bf16[1,96,384]{2,1,0:T(8,128)(2,1)S(1)}, u32[]{:S(2)}, u32[]{:S(2)}) collective-permute-start(bf16[1,96,384]{2,1,0:T(8,128)(2,1)S(1)} %fusion.43), channel_id=1, source_target_pairs={{0,2},{1,3},{2,0},{3,1},{4,6},{5,7},{6,4},{7,5},{8,10},{9,11},{10,... | collective-permute-start | bytes 221192 | tf_op jit(solution)/shard_map/ppermute | solution.py:79
  330.9 36.9 %collective-permute-start.47 = (bf16[2,4,2,96,384]{4,3,2,1,0:T(8,128)(2,1)S(1)}, bf16[2,4,2,96,384]{4,3,2,1,0:T(8,128)(2,1)S(1)}, u32[]{:S(2)}, u32[]{:S(2)}) collective-permute-start(bf16[2,4,2,96,384]{4,3,2,1,0:T(8,128)(2,1)S(1)} %add_convert_fusion.2), channel_id=1, source_target_pairs={{0,2},{1,3},{2,0},{3,1},{4,6},{5,7},{6,4},{7,5},{8,10},{9,11},{10,... | collective-permute-start | bytes 3538952 | tf_op jit(solution)/shard_map/ppermute | solution.py:79
  343.5 17.1 %collective-permute-start.37 = (bf16[1,304,384]{2,1,0:T(8,128)(2,1)S(1)}, bf16[1,304,384]{2,1,0:T(8,128)(2,1)S(1)}, u32[]{:S(2)}, u32[]{:S(2)}) collective-permute-start(bf16[1,304,384]{2,1,0:T(8,128)(2,1)S(1)} %fusion.25), channel_id=1, source_target_pairs={{0,2},{1,3},{2,0},{3,1},{4,6},{5,7},{6,4},{7,5},{8,10},{9,11},{10,... | collective-permute-start | bytes 700424 | tf_op jit(solution)/shard_map/ppermute | solution.py:79
  344.8 24.2 %collective-permute-start.45 = (bf16[1,96,384]{2,1,0:T(8,128)(2,1)S(1)}, bf16[1,96,384]{2,1,0:T(8,128)(2,1)S(1)}, u32[]{:S(2)}, u32[]{:S(2)}) collective-permute-start(bf16[1,96,384]{2,1,0:T(8,128)(2,1)S(1)} %add_convert_fusion.7), channel_id=1, source_target_pairs={{0,1},{1,0},{2,3},{3,2},{4,5},{5,4},{6,7},{7,6},{8,9},{9,8},{10,11... | collective-permute-start | bytes 221192 | tf_op jit(solution)/shard_map/ppermute | solution.py:75
  360.7 15.3 %collective-permute-start.38 = (bf16[1,304,384]{2,1,0:T(8,128)(2,1)S(1)}, bf16[1,304,384]{2,1,0:T(8,128)(2,1)S(1)}, u32[]{:S(2)}, u32[]{:S(2)}) collective-permute-start(bf16[1,304,384]{2,1,0:T(8,128)(2,1)S(1)} %add_convert_fusion.6), channel_id=1, source_target_pairs={{0,1},{1,0},{2,3},{3,2},{4,5},{5,4},{6,7},{7,6},{8,9},{9,8},{10,11... | collective-permute-start | bytes 700424 | tf_op jit(solution)/shard_map/ppermute | solution.py:75
  366.4 9.8 %collective-permute-start.56 = (bf16[4,96,384]{2,1,0:T(8,128)(2,1)S(1)}, bf16[4,96,384]{2,1,0:T(8,128)(2,1)S(1)}, u32[]{:S(2)}, u32[]{:S(2)}) collective-permute-start(bf16[4,96,384]{2,1,0:T(8,128)(2,1)S(1)} %get-tuple-element.58), channel_id=1, source_target_pairs={{0,8},{4,12},{8,16},{12,20},{16,24},{20,28},{24,0},{28,4},{1,9},{5... | collective-permute-start | bytes 884744 | tf_op jit(solution)/shard_map/ppermute | solution.py:87
  367.7 26.1 %collective-permute-start.57 = (bf16[4,96,384]{2,1,0:T(8,128)(2,1)S(1)}, bf16[4,96,384]{2,1,0:T(8,128)(2,1)S(1)}, u32[]{:S(2)}, u32[]{:S(2)}) collective-permute-start(bf16[4,96,384]{2,1,0:T(8,128)(2,1)S(1)} %get-tuple-element.60), channel_id=1, source_target_pairs={{0,16},{4,20},{8,24},{12,28},{16,0},{20,4},{24,8},{28,12},{1,17},{... | collective-permute-start | bytes 884744 | tf_op jit(solution)/shard_map/ppermute | solution.py:87
  367.8 26.1 %collective-permute-start.58 = (bf16[4,96,384]{2,1,0:T(8,128)(2,1)S(1)}, bf16[4,96,384]{2,1,0:T(8,128)(2,1)S(1)}, u32[]{:S(2)}, u32[]{:S(2)}) collective-permute-start(bf16[4,96,384]{2,1,0:T(8,128)(2,1)S(1)} %get-tuple-element.59), channel_id=1, source_target_pairs={{0,24},{4,28},{8,0},{12,4},{16,8},{20,12},{24,16},{28,20},{1,25},{... | collective-permute-start | bytes 884744 | tf_op jit(solution)/shard_map/ppermute | solution.py:87
  369.0 25.9 %collective-permute-start.48 = (bf16[4,2,96,384]{3,2,1,0:T(8,128)(2,1)S(1)}, bf16[4,2,96,384]{3,2,1,0:T(8,128)(2,1)S(1)}, u32[]{:S(2)}, u32[]{:S(2)}) collective-permute-start(bf16[4,2,96,384]{3,2,1,0:T(8,128)(2,1)S(1)} %fusion.14), channel_id=1, source_target_pairs={{0,4},{4,0},{8,12},{12,8},{16,20},{20,16},{24,28},{28,24},{1,5},{5... | collective-permute-start | bytes 1769480 | tf_op jit(solution)/shard_map/ppermute | solution.py:83
  394.0 7.8 %collective-permute-start.59 = (bf16[4,96,384]{2,1,0:T(8,128)(2,1)S(1)}, bf16[4,96,384]{2,1,0:T(8,128)(2,1)S(1)}, u32[]{:S(2)}, u32[]{:S(2)}) collective-permute-start(bf16[4,96,384]{2,1,0:T(8,128)(2,1)S(1)} %fusion.17), channel_id=1, source_target_pairs={{0,2},{1,3},{2,0},{3,1},{4,6},{5,7},{6,4},{7,5},{8,10},{9,11},{10,... | collective-permute-start | bytes 884744 | tf_op jit(solution)/shard_map/ppermute | solution.py:79
  395.3 8.4 %collective-permute-start.49 = (bf16[2,96,384]{2,1,0:T(8,128)(2,1)S(1)}, bf16[2,96,384]{2,1,0:T(8,128)(2,1)S(1)}, u32[]{:S(2)}, u32[]{:S(2)}) collective-permute-start(bf16[2,96,384]{2,1,0:T(8,128)(2,1)S(1)} %get-tuple-element.64), channel_id=1, source_target_pairs={{0,8},{4,12},{8,16},{12,20},{16,24},{20,28},{24,0},{28,4},{1,9},{5... | collective-permute-start | bytes 442376 | tf_op jit(solution)/shard_map/ppermute | solution.py:87
  395.3 14.5 %collective-permute-start.50 = (bf16[2,96,384]{2,1,0:T(8,128)(2,1)S(1)}, bf16[2,96,384]{2,1,0:T(8,128)(2,1)S(1)}, u32[]{:S(2)}, u32[]{:S(2)}) collective-permute-start(bf16[2,96,384]{2,1,0:T(8,128)(2,1)S(1)} %get-tuple-element.66), channel_id=1, source_target_pairs={{0,16},{4,20},{8,24},{12,28},{16,0},{20,4},{24,8},{28,12},{1,17},{... | collective-permute-start | bytes 442376 | tf_op jit(solution)/shard_map/ppermute | solution.py:87
  397.3 12.5 %collective-permute-start.51 = (bf16[2,96,384]{2,1,0:T(8,128)(2,1)S(1)}, bf16[2,96,384]{2,1,0:T(8,128)(2,1)S(1)}, u32[]{:S(2)}, u32[]{:S(2)}) collective-permute-start(bf16[2,96,384]{2,1,0:T(8,128)(2,1)S(1)} %get-tuple-element.65), channel_id=1, source_target_pairs={{0,24},{4,28},{8,0},{12,4},{16,8},{20,12},{24,16},{28,20},{1,25},{... | collective-permute-start | bytes 442376 | tf_op jit(solution)/shard_map/ppermute | solution.py:87
  401.9 15.1 %collective-permute-start.60 = (bf16[4,96,384]{2,1,0:T(8,128)(2,1)S(1)}, bf16[4,96,384]{2,1,0:T(8,128)(2,1)S(1)}, u32[]{:S(2)}, u32[]{:S(2)}) collective-permute-start(bf16[4,96,384]{2,1,0:T(8,128)(2,1)S(1)} %add_convert_fusion.4), channel_id=1, source_target_pairs={{0,1},{1,0},{2,3},{3,2},{4,5},{5,4},{6,7},{7,6},{8,9},{9,8},{10,11... | collective-permute-start | bytes 884744 | tf_op jit(solution)/shard_map/ppermute | solution.py:75
  409.9 4.1 collective-permute-start.52
  414.0 5.1 %collective-permute-start.53 = (bf16[4,96,384]{2,1,0:T(8,128)(2,1)S(1)}, bf16[4,96,384]{2,1,0:T(8,128)(2,1)S(1)}, u32[]{:S(2)}, u32[]{:S(2)}) collective-permute-start(bf16[4,96,384]{2,1,0:T(8,128)(2,1)S(1)} %maximum_select_fusion.3), channel_id=1, source_target_pairs={{0,1},{1,0},{2,3},{3,2},{4,5},{5,4},{6,7},{7,6},{8,9},{9,8},{10,11... | collective-permute-start | bytes 884744 | tf_op jit(solution)/shard_map/ppermute | solution.py:75
  (59 other events, 407.2 us)

commit v2 on v1

v2 whole, which is shorter than its diff:
```python
import functools
import math

import jax
import jax.numpy as jnp
from jax import lax
from jax.experimental import pallas as pl
from jax.experimental.pallas import tpu as pltpu
from jax.sharding import PartitionSpec as P

D = 768
HEADS = 12
HEAD_DIM = 64
BLOCK = 128

NORM_EPS = 1e-12
MASKED_SCORE = -1e30
SCALE_TWO = 0.125 * math.log2(math.e)
MIB = 1 << 20
CHEAP = 8

NT = (((1,), (1,)), ((), ()))
TN = (((0,), (0,)), ((), ()))


def wide_dot(left, right, dims=(((1,), (0,)), ((), ()))):
    return lax.dot_general(left, right, dims, preferred_element_type=jnp.float32)


def vmem(mib):
    return pltpu.CompilerParams(vmem_limit_bytes=mib * MIB)


def cost(flops, bytes_accessed, transcendentals=0):
    return pl.CostEstimate(
        flops=flops // CHEAP, bytes_accessed=bytes_accessed // CHEAP, transcendentals=transcendentals // CHEAP
    )


def layout(length_row, row_count):
    first_len = length_row[0]
    second_len = length_row[1]
    second_start = (first_len + BLOCK - 1) // BLOCK * BLOCK
    positions = jnp.arange(row_count, dtype=jnp.int32)
    in_first = positions < first_len
    in_second = (positions >= second_start) & (positions < second_start + second_len)
    doc_ids = jnp.where(in_first, 0, jnp.where(in_second, 1, 2)).astype(jnp.int32)
    return (in_first | in_second, doc_ids)


def norm_forward(hidden, gain_row, shift_row):
    centre = jnp.mean(hidden, axis=-1, keepdims=True)
    spread = jnp.mean(jnp.square(hidden - centre), axis=-1, keepdims=True)
    inverse = lax.rsqrt(spread + NORM_EPS)
    normed = (hidden - centre) * inverse
    return (normed * gain_row + shift_row, normed, inverse)


def norm_backward_rows(grad_rows, normed, inverse, gain_row):
    scaled = grad_rows * gain_row
    return inverse * (
        scaled
        - jnp.mean(scaled, axis=-1, keepdims=True)
        - normed * jnp.mean(scaled * normed, axis=-1, keepdims=True)
    )


def norm_backward(grad_rows, normed, inverse, gain_row):
    grad_in = norm_backward_rows(grad_rows, normed, inverse, gain_row)
    return (grad_in, jnp.sum(grad_rows * normed, axis=0), jnp.sum(grad_rows, axis=0))


LANES = 384
ROWS = 96
HALF = ROWS // 2


class Place:
    def __init__(self):
        fsdp, rep = lax.axis_index("fsdp"), lax.axis_index("rep")
        self.z, self.y = fsdp // 2, fsdp % 2
        self.x, self.c = rep // 2, rep % 2
        self.scalars = jnp.stack([self.z, self.y, self.x, self.c]).astype(jnp.int32)


def swap_core(rows):
    return lax.ppermute(rows, "rep", [(i, i ^ 1) for i in range(4)])


def swap_x(rows):
    return lax.ppermute(rows, "rep", [(i, i ^ 2) for i in range(4)])


def swap_y(rows):
    return lax.ppermute(rows, "fsdp", [(i, i ^ 1) for i in range(8)])


def turn_z(rows, step):
    return lax.ppermute(rows, "fsdp", [(i, (i + 2 * step) % 8) for i in range(8)])


def pick(rows, index):
    return lax.dynamic_index_in_dim(rows, index, 0, keepdims=False)


def after(rows, *others):
    return lax.optimization_barrier((rows, *others))[0]


def wide(rows):
    return rows.astype(jnp.float32)


def low(rows):
    return rows.astype(jnp.bfloat16)


def turned(own):
    return [turn_z(own, step) for step in (1, 2, 3)]


def to_blocks(shard, place, split_x=False, down=False):
    if down:
        blocks = shard.reshape(4, 2, HALF, 2, LANES).transpose(1, 3, 0, 2, 4).reshape(2, 8, HALF, LANES)
    else:
        blocks = shard.reshape(2, HALF, -1, LANES).transpose(0, 2, 1, 3)
    blocks = pick(blocks, place.c)
    if split_x:
        nb = blocks.shape[0] // 2
        blocks = lax.dynamic_slice_in_dim(blocks, place.x * nb, nb, 0)
    return blocks


def assemble(near_ref, pieces, full_ref, nb):
    z, y, c = near_ref[0], near_ref[1], near_ref[3]
    for p, piece in enumerate(pieces):
        core = 1 - c if p >> 1 else c
        for k in range(4):
            f = lax.rem(z + 4 - k, 4) * 2 + (1 - y if p & 1 else y)
            row = pl.multiple_of(f * ROWS + core * HALF, HALF)
            for j in range(nb):
                full_ref[pl.ds(row, HALF), j * LANES : (j + 1) * LANES] = piece[
                    k, j * HALF : (j + 1) * HALF
                ]


def assemble_down(near_ref, pieces, full_ref):
    z, y, c = near_ref[0], near_ref[1], near_ref[3]
    for p, piece in enumerate(pieces):
        core = 1 - c if p >> 1 else c
        for k in range(4):
            f = lax.rem(z + 4 - k, 4) * 2 + (1 - y if p & 1 else y)
            for j in range(8):
                row = pl.multiple_of(f * (4 * ROWS) + j % 4 * ROWS + core * HALF, HALF)
                col = j // 4 * LANES
                full_ref[pl.ds(row, HALF), col : col + LANES] = piece[k, j * HALF : (j + 1) * HALF]


def rest_kernel(near_ref, *refs):
    in_ref, out_ref = refs[-2:]
    z, y, x, c = near_ref[0], near_ref[1], near_ref[2], near_ref[3]
    for p, piece in enumerate(refs[:-2]):
        core = 1 - c if p >> 2 else c
        side = 1 - x if (p >> 1) & 1 else x
        for k in range(4):
            f = lax.rem(z + 4 - k, 4) * 2 + (1 - y if p & 1 else y)
            row = pl.ds(pl.multiple_of(f * ROWS + core * HALF, HALF), HALF)
            for j in range(4):
                col = pl.ds(pl.multiple_of((side * 4 + j) * LANES, LANES), LANES)
                in_ref[row, col] = piece[k, j * HALF : (j + 1) * HALF]
            col = pl.ds(pl.multiple_of(side * LANES, LANES), LANES)
            out_ref[row, col] = piece[k, 4 * HALF : 5 * HALF]


def down_kernel(near_ref, *refs):
    assemble_down(near_ref, refs[:-1], refs[-1])


def put_together(kernel, near, pieces, shapes):
    whole = pl.BlockSpec(memory_space=pltpu.VMEM)
    return pl.pallas_call(
        kernel,
        out_shape=tuple(jax.ShapeDtypeStruct(shape, jnp.bfloat16) for shape in shapes),
        in_specs=[pl.BlockSpec(memory_space=pltpu.SMEM)] + [whole] * len(pieces),
        out_specs=(whole,) * len(shapes),
        compiler_params=vmem(16),
        cost_estimate=cost(0, 4 * sum(math.prod(shape) for shape in shapes), 0),
    )(near, *pieces)


class Reduction:
    def __init__(self, place, mate, mine, split_x=False):
        self.place, self.split_x = place, split_x
        self.both = [mine, swap_core(mate)]
        self.others = []

    def part(self, rows, side):
        half = rows.shape[2] // 2
        return wide(lax.dynamic_slice_in_dim(rows, side * half, half, 2))

    def send_x(self):
        place = self.place
        if self.split_x:
            self.for_x = low(sum(self.part(rows, 1 - place.x) for rows in self.both))
            self.from_x = swap_x(self.for_x)
        return self

    def half_y(self, index):
        if not self.split_x:
            return sum(wide(pick(rows, index)) for rows in self.both)
        kept = sum(pick(self.part(rows, self.place.x), index) for rows in self.both)
        return kept + wide(pick(self.from_x, index))

    def send_y(self):
        self.for_y = low(self.half_y(1 - self.place.y))
        self.from_y = swap_y(self.for_y)
        return self

    def send_z(self):
        near = self.half_y(self.place.y) + wide(self.from_y)
        self.kept = pick(near, self.place.z)
        self.for_z = [low(pick(near, (self.place.z + step) % 4)) for step in (1, 2, 3)]
        self.from_z = [turn_z(rows, step) for step, rows in zip((1, 2, 3), self.for_z, strict=True)]
        return self

    def send_last_x(self):
        self.total = low(self.kept + sum(wide(rows) for rows in self.from_z))
        self.far = swap_x(self.total)
        return self

    def send_last_core(self):
        if self.split_x:
            both = jnp.concatenate([self.total, self.far]), jnp.concatenate([self.far, self.total])
            self.total = jnp.where(self.place.x == 0, *both)
        else:
            self.total = low(wide(self.total) + wide(self.far))
        self.far = swap_core(self.total)
        return self

    def send_last(self):
        self.total = low(self.kept + sum(wide(rows) for rows in self.from_z))
        self.others = [lax.ppermute(self.total, "rep", [(i, i ^ at) for i in range(4)]) for at in (2, 1, 3)]
        return self

    def finish(self):
        if self.others:
            x, core, both = (wide(rows) for rows in self.others)
            mine, theirs = wide(self.total) + x, core + both
            return jnp.where(self.place.c == 0, jnp.stack([mine, theirs]), jnp.stack([theirs, mine]))
        both = jnp.stack([self.total, self.far]), jnp.stack([self.far, self.total])
        return wide(jnp.where(self.place.c == 0, *both))


def from_blocks(parts, nb, down=False):
    if down:
        blocks = parts.reshape(2, 2, 4, HALF, LANES)
        return blocks.transpose(2, 0, 3, 1, 4).reshape(LANES, 2 * LANES)
    return parts.reshape(2, nb, HALF, LANES).transpose(0, 2, 1, 3).reshape(ROWS, nb * LANES)


def document_columns(doc_ids):
    hot = (doc_ids[:, None] == jnp.arange(128)[None, :]) & (jnp.arange(128) < 3)[None, :]
    other = (~hot) & (jnp.arange(128) < 3)[None, :]
    return (
        jnp.where(other, MASKED_SCORE, 0.0).astype(jnp.bfloat16),
        hot.astype(jnp.bfloat16),
    )


def head_part(rows, side):
    column = lax.broadcasted_iota(jnp.int32, rows.shape, 1)
    inside = column < HEAD_DIM if side == 0 else column >= HEAD_DIM
    return jnp.where(inside, rows, jnp.zeros_like(rows))


def attend_kernel(qkv_ref, qx_ref, kx_ref, ctx_ref, lse_ref, out_scr):
    rows = qkv_ref.shape[0]
    step = min(256, rows)
    keys = jnp.concatenate([qkv_ref[:, 128:256], kx_ref[...]], axis=1)
    values_t = qkv_ref[:, 256:].T
    for side in range(2):
        queries = jnp.concatenate([head_part(qkv_ref[:, :128], side), qx_ref[...]], axis=1)
        mine = slice(side * HEAD_DIM, (side + 1) * HEAD_DIM)
        for at in range(0, rows, step):
            scores = wide_dot(keys, queries[at : at + step], NT)
            top = jnp.max(scores, axis=0, keepdims=True)
            weights = jnp.exp2((scores - top) * SCALE_TWO)
            total = jnp.sum(weights, axis=0, keepdims=True)
            attended = wide_dot(values_t[mine], weights.astype(jnp.bfloat16))
            out_scr[mine, at : at + step] = attended * (1.0 / total)
            lse_ref[0, side : side + 1, at : at + step] = top * SCALE_TWO + jnp.log2(total)
    ctx_ref[...] = out_scr[...].T.astype(jnp.bfloat16)


def attention_forward(projected, doc_columns, first, pairs=3):
    rows = projected.shape[0]
    fixed = pl.BlockSpec((rows, 128), lambda h: (0, 0))
    return pl.pallas_call(
        attend_kernel,
        grid=(pairs,),
        out_shape=(
            jax.ShapeDtypeStruct((rows, pairs * 128), jnp.bfloat16),
            jax.ShapeDtypeStruct((pairs, 2, rows), jnp.float32),
        ),
        in_specs=[pl.BlockSpec((rows, 384), lambda h: (0, first + h)), fixed, fixed],
        out_specs=(
            pl.BlockSpec((rows, 128), lambda h: (0, h)),
            pl.BlockSpec((1, 2, rows), lambda h: (h, 0, 0)),
        ),
        scratch_shapes=[pltpu.VMEM((128, rows), jnp.float32)],
        compiler_params=vmem(32),
        cost_estimate=cost(16 * pairs * rows * rows * 128, 8 * rows * pairs * 128, 2 * pairs * rows * rows),
    )(projected, *doc_columns)


def attend_back_kernel(
    qkv_ref, do_ref, ctx_ref, lse_ref, qx_ref, kx_ref, out_ref, sums_ref, dq_scr
):
    rows = qkv_ref.shape[0]
    step = min(256, rows)
    grads = do_ref[...]
    product_t = (wide(grads) * wide(ctx_ref[...])).T
    keys_t = qkv_ref[:, 128:256].T
    heads = []
    for side in range(2):
        mine = slice(side * HEAD_DIM, (side + 1) * HEAD_DIM)
        q_side = head_part(qkv_ref[:, :128], side)
        heads.append((
            mine,
            q_side,
            jnp.concatenate([q_side, qx_ref[...]], axis=1),
            head_part(grads, side),
            jnp.sum(product_t[mine], axis=0, keepdims=True),
            lse_ref[0, side : side + 1, :],
        ))
    value_sum = jnp.zeros((1, 128), jnp.float32)
    for at in range(0, rows, step):
        here = slice(at, at + step)
        keys = jnp.concatenate([qkv_ref[here, 128:256], kx_ref[here]], axis=1)
        key_grad = jnp.zeros((step, 128), jnp.float32)
        value_grad = jnp.zeros((step, 128), jnp.float32)
        for mine, q_side, queries, do_side, delta, lse in heads:
            weights = jnp.exp2(wide_dot(keys, queries, NT) * SCALE_TWO - lse)
            grad_weights = wide_dot(qkv_ref[here, 256:], do_side, NT)
            grad_scores = (weights * (grad_weights - delta)).astype(jnp.bfloat16)
            value_grad += wide_dot(weights.astype(jnp.bfloat16), do_side)
            key_grad += wide_dot(grad_scores, q_side)
            query_grad = wide_dot(keys_t[mine, here], grad_scores)
            if at == 0:
                dq_scr[mine] = query_grad
            else:
                dq_scr[mine] += query_grad
        out_ref[here, 128:256] = low(key_grad * 0.125)
        value_low = low(value_grad)
        out_ref[here, 256:] = value_low
        value_sum += jnp.sum(wide(value_low), axis=0, keepdims=True)
    query_low = low(dq_scr[...].T * 0.125)
    out_ref[:, :128] = query_low
    query_sum = jnp.sum(wide(query_low), axis=0, keepdims=True)
    sums_ref[...] = jnp.concatenate([query_sum, value_sum], axis=0)


def attention_backward(projected, doc_columns, grad_context, context, log_total, pairs, own_first, first):
    rows = projected.shape[0]
    fixed = pl.BlockSpec((rows, 128), lambda h: (0, 0))
    return pl.pallas_call(
        attend_back_kernel,
        grid=(pairs,),
        out_shape=(
            jax.ShapeDtypeStruct((rows, pairs * 384), jnp.bfloat16),
            jax.ShapeDtypeStruct((2, pairs * 128), jnp.float32),
        ),
        in_specs=[
            pl.BlockSpec((rows, 384), lambda h: (0, first + h)),
            pl.BlockSpec((rows, 128), lambda h: (0, first + h)),
            pl.BlockSpec((rows, 128), lambda h: (0, own_first + h)),
            pl.BlockSpec((1, 2, rows), lambda h: (own_first + h, 0, 0)),
            fixed,
            fixed,
        ],
        out_specs=(
            pl.BlockSpec((rows, 384), lambda h: (0, h)),
            pl.BlockSpec((2, 128), lambda h: (0, h)),
        ),
        scratch_shapes=[pltpu.VMEM((128, rows), jnp.float32)],
        compiler_params=vmem(32),
        cost_estimate=cost(40 * pairs * rows * rows * 128, 18 * rows * pairs * 128, 2 * pairs * rows * rows),
    )(projected, grad_context, context, log_total, *doc_columns)


def gelu_tile(x_ref, w_ref, b_ref, act_ref, slope_ref):
    inner = wide_dot(x_ref[...], w_ref) + wide(b_ref[...])
    phi = 0.5 + 0.5 * lax.erf(inner * math.sqrt(0.5))
    bell = jnp.exp(inner * inner * -0.5) * (1.0 / math.sqrt(2.0 * math.pi))
    act_ref[...] = low(inner * phi)
    slope_ref[...] = low(phi + inner * bell)


def gelu_kernel(x_ref, w_ref, b_ref, act_ref, slope_ref):
    gelu_tile(x_ref, w_ref[...], b_ref, act_ref, slope_ref)


def gelu_forward(rows, w_in, b_in):
    count, units = rows.shape[0], w_in.shape[1]
    tile = 512
    column = pl.BlockSpec((count, tile), lambda j: (0, j))
    like = jax.ShapeDtypeStruct((count, units), jnp.bfloat16)
    return pl.pallas_call(
        gelu_kernel,
        grid=(units // tile,),
        out_shape=(like, like),
        in_specs=[
            pl.BlockSpec((count, D), lambda j: (0, 0)),
            pl.BlockSpec((D, tile), lambda j: (0, j)),
            pl.BlockSpec((1, tile), lambda j: (0, j)),
        ],
        out_specs=(column, column),
        compiler_params=vmem(32),
        cost_estimate=cost(2 * count * D * units, 4 * count * units, 2 * count * units),
    )(rows, w_in, b_in.reshape(1, -1))


def inner_grad_kernel(g_ref, w_ref, slope_ref, out_ref, sum_ref):
    grad = wide_dot(g_ref[...], w_ref[...], NT) * slope_ref[...].astype(jnp.float32)
    low = grad.astype(jnp.bfloat16)
    out_ref[...] = low
    sum_ref[...] = jnp.sum(low.astype(jnp.float32), axis=0, keepdims=True)


def inner_backward(grad_mlp, w_down, slope):
    count, units = slope.shape
    tile = 512
    column = pl.BlockSpec((count, tile), lambda j: (0, j))
    return pl.pallas_call(
        inner_grad_kernel,
        grid=(units // tile,),
        out_shape=(
            jax.ShapeDtypeStruct((count, units), jnp.bfloat16),
            jax.ShapeDtypeStruct((1, units), jnp.float32),
        ),
        in_specs=[
            pl.BlockSpec((count, D), lambda j: (0, 0)),
            pl.BlockSpec((tile, D), lambda j: (j, 0)),
            column,
        ],
        out_specs=(column, pl.BlockSpec((1, tile), lambda j: (0, j))),
        compiler_params=vmem(32),
        cost_estimate=cost(2 * count * D * units, 6 * count * units, 0),
    )(grad_mlp, w_down, slope)


def keep_halves(total, c, mate_ref, mine_ref, where_of):
    for part in range(total.shape[0] // ROWS):
        for j in range(total.shape[1] // LANES):
            first, second = (
                total[part * ROWS + at : part * ROWS + at + HALF, j * LANES : (j + 1) * LANES]
                for at in (0, HALF)
            )
            to = where_of(part, j)
            mate_ref[to] = jnp.where(c == 0, second, first)
            mine_ref[to] = jnp.where(c == 0, first, second)


def feed_back_kernel(
    near_ref, mlp_ref, low_ref, active_ref, slope_ref, down_ref, in_ref,
    first_ref, bias_ref, down_mate, down_mine, in_mate, in_mine, low_t,
):
    c = near_ref[3]
    start = pl.program_id(0) == 0

    @pl.when(start)
    def _():
        low_t[...] = low_ref[...].T

    grad_inner = low(wide_dot(mlp_ref[...], down_ref[...], NT) * wide(slope_ref[...]))
    bias_ref[...] = jnp.sum(wide(grad_inner), axis=0, keepdims=True)

    def of_in(part, j):
        return (part % 2, part // 2, slice(j * HALF, (j + 1) * HALF))

    def of_down(part, j):
        return (part // 4, 0, slice((j * 4 + part % 4) * HALF, (j * 4 + part % 4 + 1) * HALF))

    keep_halves(low(wide_dot(low_t[...], grad_inner)), c, in_mate, in_mine, of_in)
    keep_halves(low(wide_dot(active_ref[...], mlp_ref[...], TN)), c, down_mate, down_mine, of_down)
    back = wide_dot(grad_inner, in_ref[...], NT)

    @pl.when(start)
    def _():
        first_ref[...] = back

    @pl.when(jnp.logical_not(start))
    def _():
        first_ref[...] += back


def feed_backward(near, grad_mlp, first_low, active, slope, down_full, in_full):
    count, units = active.shape
    tile = 2 * LANES
    rows = 8 * HALF
    fixed = pl.BlockSpec((count, D), lambda u: (0, 0), pipeline_mode=pl.Buffered(1))
    column = pl.BlockSpec((count, tile), lambda u: (0, u))
    like = jax.ShapeDtypeStruct((2, 4, rows, LANES), jnp.bfloat16)
    down_out = pl.BlockSpec((2, 1, rows, LANES), lambda u: (0, u, 0, 0))
    in_out = pl.BlockSpec((2, 4, 2 * HALF, LANES), lambda u: (0, 0, u, 0))
    return pl.pallas_call(
        feed_back_kernel,
        grid=(units // tile,),
        in_specs=[
            pl.BlockSpec(memory_space=pltpu.SMEM),
            fixed,
            fixed,
            column,
            column,
            pl.BlockSpec((tile, D), lambda u: (u, 0)),
            pl.BlockSpec((D, tile), lambda u: (0, u)),
        ],
        out_specs=(
            pl.BlockSpec((count, D), lambda u: (0, 0)),
            pl.BlockSpec((1, tile), lambda u: (0, u)),
            down_out, down_out, in_out, in_out,
        ),
        out_shape=(
            jax.ShapeDtypeStruct((count, D), jnp.float32),
            jax.ShapeDtypeStruct((1, units), jnp.float32),
            like, like, like, like,
        ),
        scratch_shapes=[pltpu.VMEM((D, count), jnp.bfloat16)],
        compiler_params=vmem(48),
        cost_estimate=cost(8 * count * D * units, 8 * count * units),
    )(near, grad_mlp, first_low, active, slope, down_full, in_full)


def qkv_grad_kernel(many, near_ref, *refs):
    left_ref, rights, edges = refs[0], refs[1 : 1 + many], refs[1 + many : -2]
    mate_ref, mine_ref = refs[-2:]
    c = near_ref[3]
    right = jnp.concatenate([ref[...] for ref in rights], axis=1)
    blocks = right.shape[1] // LANES

    def where_of(part, j):
        return (part % 2, part // 2, slice(j * HALF, (j + 1) * HALF))

    keep_halves(low(wide_dot(left_ref[...], right, TN)), c, mate_ref, mine_ref, where_of)
    for ref, edge in zip((mate_ref, mine_ref), edges, strict=True):
        ref[:, :, blocks * HALF :] = edge[...]


def out_grad_kernel(near_ref, left_ref, right_ref, edge_left, edge_right, mate_ref, mine_ref):
    c = near_ref[3]

    def where_of(part, j):
        return (part % 2, part // 2, slice(j * HALF, (j + 1) * HALF))

    keep_halves(low(wide_dot(left_ref[...], right_ref[...], TN)), c, mate_ref, mine_ref, where_of)
    blocks = right_ref.shape[1] // LANES

    def edge_of(part, j):
        return (part % 2, part // 2, slice((blocks + j) * HALF, (blocks + j + 1) * HALF))

    keep_halves(low(wide_dot(edge_left[...], edge_right[...], TN)), c, mate_ref, mine_ref, edge_of)


def whole_grad(kernel, near, arrays, rows, flops):
    like = jax.ShapeDtypeStruct((2, 4, rows, LANES), jnp.bfloat16)
    whole = pl.BlockSpec(memory_space=pltpu.VMEM)
    return pl.pallas_call(
        kernel,
        in_specs=[pl.BlockSpec(memory_space=pltpu.SMEM)] + [whole] * len(arrays),
        out_specs=(whole, whole),
        out_shape=(like, like),
        compiler_params=vmem(32),
        cost_estimate=cost(flops, sum(2 * a.size for a in arrays), 0),
    )(near, *arrays)


def lo_and_out_grad(near, left, right, out_left, out_right):
    rows = (right.shape[1] + out_right.shape[1]) // LANES * HALF
    flops = 2 * left.shape[0] * D * (right.shape[1] + out_right.shape[1])
    return whole_grad(out_grad_kernel, near, [left, right, out_left, out_right], rows, flops)


def hi_grad(near, left, rights, edges):
    width = sum(right.shape[1] for right in rights)
    rows = width // LANES * HALF + edges[0].shape[2]
    kernel = functools.partial(qkv_grad_kernel, len(rights))
    return whole_grad(kernel, near, [left, *rights, *edges], rows, 2 * left.shape[0] * D * width)


def project_kernel(nb, near_ref, tokens_ref, *refs):
    pieces = refs[:4]
    full_ref, out_ref, vec_ref, b_ref = refs[4:]
    small = sum(
        wide(piece[k, nb * HALF : nb * HALF + 24]) for piece in pieces[:2] for k in range(4)
    )
    vec_ref[:, :LANES] = small[:8]
    vec_ref[:, LANES:] = small[8:16]
    for f in range(8):
        b_ref[:, f * LANES : (f + 1) * LANES] = small[16 + f : 17 + f]
    assemble(near_ref, pieces, full_ref, nb)
    for j in range(nb):
        here = slice(j * LANES, (j + 1) * LANES)
        pair = slice(j * 128, (j + 1) * 128)
        bias = jnp.concatenate(
            [vec_ref[0:1, pair], jnp.zeros((1, 128), jnp.float32), vec_ref[1:2, pair]], axis=1
        )
        out_ref[:, here] = low(wide_dot(tokens_ref[...], full_ref[:, here]) + bias)


def project(near, tokens, pieces, nb):
    count = tokens.shape[0]
    whole = pl.BlockSpec(memory_space=pltpu.VMEM)
    return pl.pallas_call(
        functools.partial(project_kernel, nb),
        out_shape=(
            jax.ShapeDtypeStruct((D, nb * LANES), jnp.bfloat16),
            jax.ShapeDtypeStruct((count, nb * LANES), jnp.bfloat16),
            jax.ShapeDtypeStruct((8, D), jnp.float32),
            jax.ShapeDtypeStruct((1, 4 * D), jnp.float32),
        ),
        in_specs=[pl.BlockSpec(memory_space=pltpu.SMEM)] + [whole] * (1 + len(pieces)),
        out_specs=(whole,) * 4,
        compiler_params=vmem(32),
        cost_estimate=cost(2 * count * D * nb * LANES, 6 * count * D),
    )(near, tokens, *pieces)


def pairs_of(rows):
    lead = rows.shape[:-1]
    return jnp.moveaxis(rows.reshape(*lead, 3, HEADS // 2, 128), -3, -2).reshape(*lead, 3 * D)


def of_pairs(rows):
    lead = rows.shape[:-1]
    return jnp.moveaxis(rows.reshape(*lead, HEADS // 2, 3, 128), -3, -2).reshape(*lead, 3 * D)


def small_to_blocks(grad_vectors, grad_b_in, place):
    vectors = jnp.pad(
        grad_vectors.reshape(8, 4, 2, ROWS).transpose(2, 1, 0, 3),
        ((0, 0), (0, 0), (0, 8), (0, LANES - ROWS)),
    )
    biases = jnp.pad(
        grad_b_in.reshape(4, 2, 1, LANES).transpose(1, 0, 2, 3), ((0, 0), (0, 0), (0, 15), (0, 0))
    )
    vectors, biases = low(vectors), low(biases)
    return (
        jnp.where(place.c == 0, biases, vectors),
        jnp.where(place.c == 0, vectors, biases),
    )


def layer_front(tokens, context, out_weight, vector_wide):
    attn_branch = wide_dot(context, out_weight) + vector_wide[2]
    return norm_forward(wide(tokens) + attn_branch, vector_wide[3], vector_wide[4])


def layer_end(active, down, first_norm, vector_wide, valid_rows, cotangent):
    mlp_branch = wide_dot(active, down) + vector_wide[5]
    second_norm, normed_two, inverse_two = norm_forward(
        first_norm + mlp_branch, vector_wide[6], vector_wide[7]
    )
    layer_out = low(jnp.where(valid_rows[:, None], second_norm, 0.0))
    grad_out = jnp.where(valid_rows[:, None], wide(cotangent), 0.0)
    return (layer_out, *norm_backward(grad_out, normed_two, inverse_two, vector_wide[6]))


def staged_body(tokens, lengths, w_qkv, vectors, w_attn_out, w_in, b_in, w_down, cotangent):
    place = Place()
    near = place.scalars
    valid_rows, doc_ids = layout(lengths[0], tokens.shape[0])
    doc_columns = document_columns(doc_ids)

    fsdp = lax.axis_index("fsdp")
    small = lax.dynamic_update_slice(jnp.zeros((8, D), jnp.bfloat16), vectors, (0, fsdp * ROWS))
    small = jnp.concatenate([small[:, :LANES], small[:, LANES:]])
    own_b = lax.dynamic_update_slice(jnp.zeros((16, LANES), jnp.bfloat16), b_in[None], (fsdp, 0))
    own = jnp.concatenate([to_blocks(pairs_of(w_qkv), place).reshape(-1, LANES), small, own_b])
    qkv = jnp.stack([own, *turned(own)])
    qkv_y = swap_y(qkv)
    qkv_pieces = [qkv, qkv_y, swap_core(qkv), swap_core(qkv_y)]
    own = jnp.concatenate(
        [
            to_blocks(w_in, place, True).reshape(-1, LANES),
            to_blocks(w_attn_out, place, True).reshape(-1, LANES),
            to_blocks(w_down, place, down=True).reshape(-1, LANES),
        ]
    )
    own = after(own, qkv)
    came = turned(own)
    w_qkv_full, projected, vector_wide, b_full = project(
        near, after(tokens, came[0], came[2]), qkv_pieces, HEADS // 2
    )
    context_lo, total_lo = attention_forward(projected, doc_columns, 0)
    both = [own, came[0], after(came[1], context_lo), came[2]]
    rest = [jnp.stack([rows[: 5 * HALF] for rows in both])]
    down = jnp.stack([rows[5 * HALF :] for rows in both])
    rest += [swap_y(rest[0]), swap_x(rest[0])]
    context_hi, total_hi = attention_forward(after(projected, context_lo, rest[0], down), doc_columns, 3)
    rest[1:] = after(rest[1:], context_hi)
    down_y = swap_y(after(down, rest[1]))
    rest.append(swap_x(rest[1]))
    rest += [swap_core(piece) for piece in rest]
    in_full, out_full = put_together(rest_kernel, near, rest, [(D, 4 * D), (D, D)])
    context = jnp.concatenate([context_lo, context_hi], axis=1)
    first_norm, normed_one, inverse_one = layer_front(tokens, context, out_full, vector_wide)
    first_low = low(first_norm)
    active, slope = gelu_forward(first_low, in_full, b_full.reshape(-1))
    down_y = after(down_y, active)
    down_pieces = [down, down_y, swap_core(down), swap_core(down_y)]
    (down_full,) = put_together(down_kernel, near, down_pieces, [(4 * D, D)])
    layer_out, grad_two, gain_two, shift_two = layer_end(
        active, down_full, first_norm, vector_wide, valid_rows, cotangent
    )

    grad_mlp = low(grad_two)
    back_first, grad_b_in, *parts = feed_backward(
        near, grad_mlp, first_low, active, slope, down_full, in_full
    )
    down_sum = Reduction(place, *parts[:2])
    in_sum = Reduction(place, *parts[2:], split_x=True)
    grad_one, gain_one, shift_one = norm_backward(
        grad_two + back_first, normed_one, inverse_one, vector_wide[3]
    )
    grad_attn = low(grad_one)
    grad_context = low(wide_dot(grad_attn, out_full, NT))
    down_sum.send_x().send_y()
    in_sum.send_x()

    def back_of(projected, context, total, pairs, own_first, first, *others):
        return attention_backward(
            projected, doc_columns, after(grad_context, *others), context, total, pairs, own_first, first
        )

    back_a, sums_a = back_of(projected, context_lo, total_lo, 2, 0, 0, in_sum.for_x, down_sum.for_y)
    down_sum.from_y = after(down_sum.from_y, back_a)
    down_sum.send_z()
    back_b, sums_b = back_of(projected, context_lo, total_lo, 1, 2, 2, back_a, down_sum.for_z)
    in_sum.from_x = after(in_sum.from_x, back_b)
    in_sum.send_y()
    back_lo = jnp.concatenate([back_a, back_b], axis=1)
    lo_sum = Reduction(
        place, *lo_and_out_grad(near, tokens, after(back_lo, in_sum.for_y), context, grad_attn)
    )
    back_3, sums_3 = back_of(projected, context_hi, total_hi, 1, 0, 3, lo_sum.both[0], in_sum.for_y)
    lo_sum.both[1], in_sum.from_y = after((lo_sum.both[1], in_sum.from_y), back_3)
    lo_sum.send_y()
    in_sum.send_z()
    back_4, sums_4 = back_of(
        projected, context_hi, total_hi, 1, 1, 4, back_3, lo_sum.for_y, in_sum.for_z
    )
    down_sum.from_z = after(down_sum.from_z, back_4)
    down_sum.send_last_x()
    back_5, sums_5 = back_of(projected, context_hi, total_hi, 1, 2, 5, back_4, down_sum.total)
    lo_sum.from_y, down_sum.far = after((lo_sum.from_y, down_sum.far), back_5)
    grad_vectors = jnp.concatenate(
        [
            jnp.concatenate([sums_a, sums_b, sums_3, sums_4, sums_5], axis=1),
            jnp.stack(
                [
                    jnp.sum(wide(grad_attn), axis=0),
                    gain_one,
                    shift_one,
                    jnp.sum(wide(grad_mlp), axis=0),
                    gain_two,
                    shift_two,
                ]
            ),
        ]
    )
    hi_sum = Reduction(
        place,
        *hi_grad(
            near, tokens, [back_3, back_4, back_5], small_to_blocks(grad_vectors, grad_b_in, place)
        ),
    )
    lo_sum.from_y = after(lo_sum.from_y, hi_sum.both[0])
    lo_sum.send_z()
    hi_sum.both[1] = after(hi_sum.both[1], lo_sum.for_z)
    hi_sum.send_y()
    in_sum.from_z, down_sum.far = after((in_sum.from_z, down_sum.far), hi_sum.for_y)
    in_sum.send_last_x()
    down_sum.send_last_core()
    back = jnp.concatenate([back_lo, back_3, back_4, back_5], axis=1)
    grad_tokens = low(
        grad_one + wide_dot(after(back, in_sum.total, down_sum.total), w_qkv_full, NT)
    )
    hi_sum.from_y = after(hi_sum.from_y, grad_tokens)
    hi_sum.send_z()
    lo_sum.from_z, in_sum.far = after((lo_sum.from_z, in_sum.far), hi_sum.for_z)
    in_sum.send_last_core()
    lo_sum.send_last()
    hi_sum.from_z = after(hi_sum.from_z, lo_sum.total, in_sum.total)
    hi_sum.send_last()
    in_part, down_part, lo_part, hi_part = (
        total.finish() for total in (in_sum, down_sum, lo_sum, hi_sum)
    )
    qkv_shard = jnp.concatenate(
        [from_blocks(lo_part[:, : 3 * HALF], 3), from_blocks(hi_part[:, : 3 * HALF], 3)], axis=1
    )
    small = hi_part[:, 3 * HALF :]
    return (
        layer_out,
        grad_tokens,
        of_pairs(qkv_shard),
        small[0, :8, :ROWS],
        from_blocks(lo_part[:, 3 * HALF :], 2),
        from_blocks(in_part, 8),
        small[1, 0],
        from_blocks(down_part, 8, True),
    )


def plain_body(tokens, lengths, w_qkv, vectors, w_attn_out, w_in, b_in, w_down, cotangent):
    def whole(rows, axis=0):
        return lax.all_gather(rows, "fsdp", axis=axis, tiled=True)

    def own(total, axis=0):
        shard = lax.psum_scatter(total, "fsdp", scatter_dimension=axis, tiled=True)
        return wide(lax.psum(low(shard), "rep"))

    valid_rows, doc_ids = layout(lengths[0], tokens.shape[0])
    doc_columns = document_columns(doc_ids)
    qkv_full, out_full, in_full, down_full = whole(w_qkv), whole(w_attn_out), whole(w_in), whole(w_down)
    vector_wide = wide(whole(vectors, 1))
    bias = jnp.concatenate([vector_wide[0], jnp.zeros((D,), jnp.float32), vector_wide[1]])
    projected = pairs_of(low(wide_dot(tokens, qkv_full) + bias))
    context, log_total = attention_forward(projected, doc_columns, 0, HEADS // 2)
    first_norm, normed_one, inverse_one = layer_front(tokens, context, out_full, vector_wide)
    first_low = low(first_norm)
    active, slope = gelu_forward(first_low, in_full, whole(b_in))
    layer_out, grad_two, gain_two, shift_two = layer_end(
        active, down_full, first_norm, vector_wide, valid_rows, cotangent
    )
    grad_mlp = low(grad_two)
    grad_inner, grad_b_in = inner_backward(grad_mlp, down_full, slope)
    grad_first = grad_two + wide_dot(grad_inner, in_full, NT)
    grad_one, gain_one, shift_one = norm_backward(
        grad_first, normed_one, inverse_one, vector_wide[3]
    )
    grad_attn = low(grad_one)
    grad_context = low(wide_dot(grad_attn, out_full, NT))
    back, column_sums = attention_backward(
        projected, doc_columns, grad_context, context, log_total, HEADS // 2, 0, 0
    )
    back = of_pairs(back)
    edge = [
        jnp.sum(wide(grad_attn), axis=0), gain_one, shift_one, jnp.sum(wide(grad_mlp), axis=0), gain_two, shift_two
    ]
    return (
        layer_out,
        low(grad_one + wide_dot(back, qkv_full, NT)),
        own(wide_dot(tokens, back, TN)),
        own(jnp.concatenate([column_sums, jnp.stack(edge)]), 1),
        own(wide_dot(context, grad_attn, TN)),
        own(wide_dot(first_low, grad_inner, TN)),
        own(grad_b_in.reshape(-1)),
        own(wide_dot(active, grad_mlp, TN)),
    )


def solution(mesh):
    staged = mesh.shape["fsdp"] == 8 and mesh.shape["rep"] == 4
    return jax.shard_map(
        staged_body if staged else plain_body,
        mesh=mesh,
        in_specs=(
            P(("fsdp", "rep"), None),
            P(("fsdp", "rep"), None),
            P("fsdp", None),
            P(None, "fsdp"),
            P("fsdp", None),
            P("fsdp", None),
            P("fsdp"),
            P("fsdp", None),
            P(("fsdp", "rep"), None),
        ),
        out_specs=(
            P(("fsdp", "rep"), None),
            P(("fsdp", "rep"), None),
            P("fsdp", None),
            P(None, "fsdp"),
            P("fsdp", None),
            P("fsdp", None),
            P("fsdp"),
            P("fsdp", None),
        ),
        check_vma=False,
    )
```

time: 429 us -> 373 us (0.87)
  waiting for transfers between devices: 116 us -> 89.6 us
  matrix products: 30.4 us -> 13.3 us
  starting transfers between devices: 66.9 us -> 55.6 us
    ppermute x24 -> x18, waiting for transfers between devices: 72.6 us -> 38 us  [turn_z(): lax.ppermute(rows, 'fsdp', [(i, (i + 2 * step) % 8) for i in range(8)])]
    dot_general x3 -> x0, matrix products: 12.7 us -> none  [the longest x1 7.28 us: body(): jnp.dot(active, weights.down, preferred_element_type=jnp.float32)]
    ppermute x8 -> x7, waiting for transfers between devices: 16.5 us -> 26.7 us  [swap_y(): return lax.ppermute(rows, 'fsdp', [(i, i ^ 1) for i in range(8)])]
    ppermute x9 -> x5, waiting for transfers between devices: 27.3 us -> 17.2 us  [swap_x(): return lax.ppermute(rows, 'rep', [(i, i ^ 2) for i in range(4)])]
    ppermute x20 -> x14, starting transfers between devices: 25.4 us -> 17.3 us  [swap_core(): return lax.ppermute(rows, 'rep', [(i, i ^ 1) for i in range(4)])]
    reduce_sum x1 -> x2, other arithmetic: 3.06 us -> 9.58 us  [norm_backward(): jnp.sum(grad_rows * normed, axis=0)]
    ppermute x9 -> x5, starting transfers between devices: 9.85 us -> 3.4 us  [swap_x(): return lax.ppermute(rows, 'rep', [(i, i ^ 2) for i in range(4)])]
    ppermute x0 -> x6, starting transfers between devices: none -> 5.05 us  [send_last(): lax.ppermute(self.total, 'rep', [(i, i ^ at) for i in range(4)])]
  transfers between devices with their start and end apart: 61 -> 50, of which waited for: 17 -> 16; matrix products, arithmetic and copies ran while one was open for 9% -> 14% of each run, Pallas kernels for 18% -> 25%
where the time goes in v2:
time: 373 us; the launch traced here: 366 us
  Pallas kernels  127 us (34%)
  waiting for transfers between devices  89.6 us (24%)
  starting transfers between devices  55.6 us (15%)
  local copies, waits for them, and re-layouts  42.1 us (11%)
  other arithmetic  34.6 us (9%)
  matrix products  13.3 us (4%)
  between operations  3.91 us (1%)
    pallas_call x5, Pallas kernels, attention_backward(): pl.pallas_call(attend_back_kernel, grid=(pairs,), out_shape=(jax.ShapeDty...  38.9 us
    ppermute x18, waiting for transfers between devices, turn_z(): lax.ppermute(rows, 'fsdp', [(i, (i + 2 * step) % 8) for i in range(8)])  38 us
    pallas_call x2, Pallas kernels, attention_forward(): pl.pallas_call(attend_kernel, grid=(pairs,), out_shape=(jax.ShapeDtypeStr...  31.4 us
    unnamed x133, local copies, waits for them, and re-layouts  28.1 us
    pallas_call x1, Pallas kernels, feed_backward(): pl.pallas_call(feed_back_kernel, grid=(units // tile,), in_specs=[pl.Bloc...  27.4 us
    ppermute x7, waiting for transfers between devices, swap_y(): return lax.ppermute(rows, 'fsdp', [(i, i ^ 1) for i in range(8)])  26.7 us
    ppermute x18, starting transfers between devices, turn_z(): lax.ppermute(rows, 'fsdp', [(i, (i + 2 * step) % 8) for i in range(8)])  21.4 us
    ppermute x14, starting transfers between devices, swap_core(): return lax.ppermute(rows, 'rep', [(i, i ^ 1) for i in range(4)])  17.3 us
  transfers between devices with their start and end apart: 50, of which 16 were waited for; matrix products, arithmetic and copies ran while one was open for 14% of the time, Pallas kernels for 25%

profile of v2, /device:TPU:25, one launch (start us, length us, event | category | flops | bytes accessed | tf_op | source)
XLA Modules:
  0.0 366.0 jit_solution(5022001669384217704)
XLA Ops:
  0.7 1.6 reshape.270
  5.3 5.0 %collective-permute-done = bf16[320,384]{1,0:T(8,128)(2,1)S(1)} collective-permute-done((bf16[320,384]{1,0:T(8,128)(2,1)S(1)}, bf16[320,384]{1,0:T(8,128)(2,1)S(1)}, u32[]{:S(2)}, u32[]{:S(2)}) %collective-permute-start) | collective-permute-done | bytes 245792 | tf_op jit(solution)/shard_map/ppermute | solution.py:99
  10.3 15.5 %collective-permute-done.1 = bf16[320,384]{1,0:T(8,128)(2,1)S(1)} collective-permute-done((bf16[320,384]{1,0:T(8,128)(2,1)S(1)}, bf16[320,384]{1,0:T(8,128)(2,1)S(1)}, u32[]{:S(2)}, u32[]{:S(2)}) %collective-permute-start.1) | collective-permute-done | bytes 245792 | tf_op jit(solution)/shard_map/ppermute | solution.py:99
  31.8 1.9 collective-permute-start.6
  33.7 1.5 collective-permute-start.4
  35.2 13.8 %collective-permute-done.5.refs_1_ = bf16[4,320,384]{2,1,0:T(8,128)(2,1)} collective-permute-done((bf16[4,320,384]{2,1,0:T(8,128)(2,1)}, bf16[4,320,384]{2,1,0:T(8,128)(2,1)}, u32[]{:S(2)}, u32[]{:S(2)}) %collective-permute-start.5) | collective-permute-done | bytes 983072 | tf_op jit(solution)/shard_map/ppermute | solution.py:95
  49.0 2.5 collective-permute-start.7
  51.5 2.2 collective-permute-start.8
  53.8 3.5 collective-permute-done.4
  57.4 6.9 %shard_map.152 = (bf16[768,2304]{1,0:T(8,128)(2,1)S(1)}, bf16[1024,2304]{1,0:T(8,128)(2,1)S(1)}, f32[8,768]{1,0:T(8,128)S(1)}, f32[1,3072]{1,0:T(1,128)S(1)}) custom-call(s32[4]{0:T(128)S(1)} %pad_add_fusion.near_ref, bf16[1024,768]{1,0:T(8,128)(2,1)S(1)} %copy-done.4, bf16[4,320,384]{2,1,0:T(8,128)(2,1)} %pad_maximum_fusion.2.refs_0_, ...), custom_call_target="tpu_custom_call" | custom-call | flops 452984832 | bytes 589824 | tf_op jit(solution)/shard_map/pallas_call | solution.py:613
  64.3 1.9 copy-done.25
  66.1 15.6 %shard_map.153 = (bf16[1024,384]{1,0:T(8,128)(2,1)S(1)}, f32[3,2,1024]{2,1,0:T(2,128)S(1)}) custom-call(bf16[1024,2304]{1,0:T(8,128)(2,1)S(1)} %get-tuple-element.83.qkv_ref, bf16[1024,128]{1,0:T(8,128)(2,1)S(1)} %select_convert_fusion.1.qx_ref, bf16[1024,128]{1,0:T(8,128)(2,1)S(1)} %fusion.9.kx_ref), custom_call_target="tpu_custom_call" | custom-call | flops 805306368 | bytes 393216 | tf_op jit(solution)/shard_map/pallas_call | solution.py:298
  83.7 15.8 %shard_map.154 = (bf16[1024,384]{1,0:T(8,128)(2,1)S(1)}, f32[3,2,1024]{2,1,0:T(2,128)S(1)}) custom-call(bf16[1024,2304]{1,0:T(8,128)(2,1)S(1)} %get-tuple-element.83.qkv_ref, bf16[1024,128]{1,0:T(8,128)(2,1)S(1)} %select_convert_fusion.1.qx_ref, bf16[1024,128]{1,0:T(8,128)(2,1)S(1)} %fusion.9.kx_ref), custom_call_target="tpu_custom_call" | custom-call | flops 805306368 | bytes 393216 | tf_op jit(solution)/shard_map/pallas_call | solution.py:298
  99.8 2.8 collective-permute-start.12
  103.1 12.0 %collective-permute-done.11.refs_3_ = bf16[4,240,384]{2,1,0:T(8,128)(2,1)S(1)} collective-permute-done((bf16[4,240,384]{2,1,0:T(8,128)(2,1)S(1)}, bf16[4,240,384]{2,1,0:T(8,128)(2,1)S(1)}, u32[]{:S(2)}, u32[]{:S(2)}) %collective-permute-start.11) | collective-permute-done | bytes 737312 | tf_op jit(solution)/shard_map/ppermute | solution.py:91
  115.1 3.4 collective-permute-start.15
  122.5 1.6 fusion.40
  125.2 11.3 %shard_map.156 = (bf16[1024,3072]{1,0:T(8,128)(2,1)S(1)}, bf16[1024,3072]{1,0:T(8,128)(2,1)S(1)}) custom-call(bf16[1024,768]{1,0:T(8,128)(2,1)S(1)} %fusion.3.x_ref.low_ref, bf16[768,3072]{1,0:T(8,128)(2,1)S(1)} %get-tuple-element.89.w_ref.in_ref, f32[1,3072]{1,0:T(1,128)S(1)} %get-tuple-element.90.b_ref), custom_call_target="tpu_custom_call" | custom-call | flops 603979776 | bytes 1572864 | tf_op jit(solution)/shard_map/pallas_call | solution.py:408
  136.5 2.7 copy-done.11
  139.2 6.8 %collective-permute-done.16.refs_1_ = bf16[4,384,384]{2,1,0:T(8,128)(2,1)} collective-permute-done((bf16[4,384,384]{2,1,0:T(8,128)(2,1)S(1)}, bf16[4,384,384]{2,1,0:T(8,128)(2,1)}, u32[]{:S(2)}, u32[]{:S(2)}) %collective-permute-start.16) | collective-permute-done | bytes 1179680 | tf_op jit(solution)/shard_map/ppermute | solution.py:95
  148.1 2.0 collective-permute-done.18.refs_3_
  150.1 2.1 shard_map.157.down_ref
  152.2 5.4 %fusion.37 = (f32[1024]{0:T(1024)S(1)}, f32[1024,768]{1,0:T(8,128)S(1)}) fusion(f32[768]{0:T(1024)S(1)} %get-tuple-element.158, f32[768]{0:T(1024)S(1)} %get-tuple-element.159, f32[768]{0:T(1024)S(1)} %get-tuple-element.160, f32[1024]{0:T(1024)S(1)} %add_rsqrt_fusion.1, f32[1024,768]{1,0:T(8,128)S(1)} %get-tuple-element.192, ...), kind=kOutput, calls=%fused_computation.155 | convolution fusion | flops 4837342208 | bytes 17323008 | tf_op jit(solution)/shard_map/dot_general | solution.py:27
  158.1 2.0 copy-done.32
  160.2 2.4 multiply_reduce_fusion
  162.5 2.0 fusion.33
  164.6 27.4 %shard_map.158 = (f32[1024,768]{1,0:T(8,128)}, f32[1,3072]{1,0:T(1,128)S(1)}, bf16[2,4,384,384]{3,2,1,0:T(8,128)(2,1)}, bf16[2,4,384,384]{3,2,1,0:T(8,128)(2,1)}...) custom-call(s32[4]{0:T(128)S(1)} %pad_add_fusion.near_ref, ...), custom_call_target="tpu_custom_call" | custom-call | flops 2415919104 | bytes 3145728 | tf_op jit(solution)/shard_map/pallas_call | solution.py:506
  192.4 7.2 %multiply_reduce_fusion.1 = (bf16[768]{0:T(1024)(128)(2,1)S(1)}, f32[1024]{0:T(1024)S(1)}, f32[1024]{0:T(1024)S(1)}, bf16[768]{0:T(1024)(128)(2,1)}, f32[1024,768]{1,0:T(8,128)S(1)}, /*index=5*/bf16[1024,768]{1,0:T(8,128)(2,1)}) fusion(f32[1024,768]{1,0:T(8,128)} %copy-done.29, f32[1024]{0:T(1024)S(1)} %add_rsqrt_fusion.1, ...), kind=kLoop, calls=%fused_computation.2 | loop fusion | flops 18084352 | bytes 15774720 | tf_op jit(solution)/shard_map/reduce_sum | solution.py:70
  199.7 1.7 fusion.4
  202.7 2.3 fusion.35
  205.1 1.4 convolution_convert_fusion.do_ref
  207.1 1.6 add_convert_fusion.2
  209.8 13.4 %shard_map.159 = (bf16[1024,768]{1,0:T(8,128)(2,1)S(1)}, f32[2,256]{1,0:T(2,128)S(1)}) custom-call(bf16[1024,2304]{1,0:T(8,128)(2,1)S(1)} %bitcast.164, bf16[1024,768]{1,0:T(8,128)(2,1)S(1)} %convolution_convert_fusion.do_ref, bf16[1024,384]{1,0:T(8,128)(2,1)S(1)} %copy-done.8, f32[3,2,1024]{2,1,0:T(2,128)S(1)} %get-tuple-element.101.lse_ref, ...), custom_call_target="tpu_custom_call" | custom-call | flops 1342177280 | bytes 589824 | tf_op jit(solution)/shard_map/pallas_call | solution.py:366
  223.2 2.0 dynamic-slice_convert_fusion
  225.2 3.4 collective-permute-done.21
  228.6 1.7 bitcast_add_fusion
  232.0 6.3 %shard_map.160 = (bf16[1024,384]{1,0:T(8,128)(2,1)S(1)}, f32[2,128]{1,0:T(2,128)S(1)}) custom-call(bf16[1024,2304]{1,0:T(8,128)(2,1)S(1)} %bitcast.164, bf16[1024,768]{1,0:T(8,128)(2,1)S(1)} %convolution_convert_fusion.do_ref, bf16[1024,384]{1,0:T(8,128)(2,1)S(1)} %copy-done.8, f32[3,2,1024]{2,1,0:T(2,128)S(1)} %get-tuple-element.101.lse_ref, ...), custom_call_target="tpu_custom_call" | custom-call | flops 671088640 | bytes 294912 | tf_op jit(solution)/shard_map/pallas_call | solution.py:366
  239.4 1.6 copy-done.5
  241.5 5.2 %shard_map.161 = (bf16[2,4,240,384]{3,2,1,0:T(8,128)(2,1)}, bf16[2,4,240,384]{3,2,1,0:T(8,128)(2,1)S(1)}) custom-call(s32[4]{0:T(128)S(1)} %pad_add_fusion.near_ref, bf16[1024,768]{1,0:T(8,128)(2,1)S(1)} %copy-done.5, bf16[1024,1152]{1,0:T(8,128)(2,1)S(1)} %pad_maximum_fusion.right_ref, bf16[1024,768]{1,0:T(8,128)(2,1)S(1)} %copy-done.13, ...), custom_call_target="tpu_custom_call" | custom-call | flops 377487360 | bytes 884736 | tf_op jit(solution)/shard_map/pallas_call | solution.py:567
  253.4 1.4 collective-permute-start.25
  255.7 2.3 copy-done.1
  258.0 6.3 %shard_map.162 = (bf16[1024,384]{1,0:T(8,128)(2,1)S(1)}, f32[2,128]{1,0:T(2,128)S(1)}) custom-call(bf16[1024,2304]{1,0:T(8,128)(2,1)S(1)} %copy-done.1, bf16[1024,768]{1,0:T(8,128)(2,1)S(1)} %convolution_convert_fusion.do_ref, bf16[1024,384]{1,0:T(8,128)(2,1)S(1)} %get-tuple-element.84.ctx_ref, f32[3,2,1024]{2,1,0:T(2,128)S(1)} %get-tuple-element.110.lse_ref, ...), custom_call_target="tpu_custom_call" | custom-call | flops 671088640 | bytes 294912 | tf_op jit(solution)/shard_map/pallas_call | solution.py:366
  264.4 2.7 collective-permute-done.24
  268.5 2.6 fusion.5
  273.1 6.5 %shard_map.163 = (bf16[1024,384]{1,0:T(8,128)(2,1)S(1)}, f32[2,128]{1,0:T(2,128)S(1)}) custom-call(bf16[1024,2304]{1,0:T(8,128)(2,1)S(1)} %copy-done.1, bf16[1024,768]{1,0:T(8,128)(2,1)S(1)} %convolution_convert_fusion.do_ref, bf16[1024,384]{1,0:T(8,128)(2,1)S(1)} %get-tuple-element.84.ctx_ref, f32[3,2,1024]{2,1,0:T(2,128)S(1)} %get-tuple-element.110.lse_ref, ...), custom_call_target="tpu_custom_call" | custom-call | flops 671088640 | bytes 294912 | tf_op jit(solution)/shard_map/pallas_call | solution.py:366
  281.8 6.3 %shard_map.164 = (bf16[1024,384]{1,0:T(8,128)(2,1)S(1)}, f32[2,128]{1,0:T(2,128)S(1)}) custom-call(bf16[1024,2304]{1,0:T(8,128)(2,1)S(1)} %copy-done.1, bf16[1024,768]{1,0:T(8,128)(2,1)S(1)} %convolution_convert_fusion.do_ref, bf16[1024,384]{1,0:T(8,128)(2,1)S(1)} %get-tuple-element.84.ctx_ref, f32[3,2,1024]{2,1,0:T(2,128)S(1)} %get-tuple-element.110.lse_ref, ...), custom_call_target="tpu_custom_call" | custom-call | flops 671088640 | bytes 294912 | tf_op jit(solution)/shard_map/pallas_call | solution.py:366
  289.3 1.4 copy-done.6
  294.1 2.8 shard_map.165
  298.0 1.5 constant_dynamic-update-slice_fusion.6
  300.4 1.4 collective-permute-start.28
  303.1 5.3 %collective-permute-done.32 = bf16[384,384]{1,0:T(8,128)(2,1)S(1)} collective-permute-done((bf16[384,384]{1,0:T(8,128)(2,1)S(1)}, bf16[384,384]{1,0:T(8,128)(2,1)S(1)}, u32[]{:S(2)}, u32[]{:S(2)}) %collective-permute-start.32) | collective-permute-done | bytes 294944 | tf_op jit(solution)/shard_map/ppermute | solution.py:91
  308.8 1.8 bitcast_add_fusion.1
  310.7 2.8 collective-permute-start.34
  315.6 1.6 collective-permute-start.38
  317.3 1.4 collective-permute-start.49
  319.8 5.0 %add_convert_fusion = bf16[1024,768]{1,0:T(8,128)(2,1)} fusion(f32[1024,768]{1,0:T(8,128)S(1)} %copy-done.38, bf16[1024,2304]{1,0:T(8,128)(2,1)S(1)} %constant_dynamic-update-slice_fusion.2, bf16[768,2304]{1,0:T(8,128)(2,1)S(1)} %copy-done.26), kind=kOutput, calls=%fused_computation | convolution fusion | flops 3625451520 | bytes 12976128 | tf_op jit(solution)/shard_map/dot_general | solution.py:27
  328.3 3.7 %collective-permute-done.35 = bf16[240,384]{1,0:T(8,128)(2,1)S(1)} collective-permute-done((bf16[240,384]{1,0:T(8,128)(2,1)S(1)}, bf16[240,384]{1,0:T(8,128)(2,1)S(1)}, u32[]{:S(2)}, u32[]{:S(2)}) %collective-permute-start.35) | collective-permute-done | bytes 184352 | tf_op jit(solution)/shard_map/ppermute | solution.py:99
  334.3 3.0 collective-permute-start.42
  337.3 3.1 collective-permute-start.43
  340.4 1.5 collective-permute-start.44
  342.8 9.1 %collective-permute-done.43 = bf16[160,384]{1,0:T(8,128)(2,1)S(1)} collective-permute-done((bf16[160,384]{1,0:T(8,128)(2,1)S(1)}, bf16[160,384]{1,0:T(8,128)(2,1)S(1)}, u32[]{:S(2)}, u32[]{:S(2)}) %collective-permute-start.43) | collective-permute-done | bytes 122912 | tf_op jit(solution)/shard_map/ppermute | solution.py:99
  353.1 1.6 collective-permute-start.47
  356.0 1.7 collective-permute-done.45
  357.7 2.7 collective-permute-done.47
  (311 shorter events, 63.4 us)
Async XLA Ops:
  3.3 25.0 %copy-start.57 = (s32[1,2]{1,0:T(1,128)S(1)}, s32[1,2]{1,0:T(1,128)}, u32[]{:S(2)}) copy-start(s32[1,2]{1,0:T(1,128)} %param.10) | copy-start | bytes 28
  3.4 26.2 %copy-start.45 = (bf16[384,768]{1,0:T(8,128)(2,1)S(1)}, bf16[384,768]{1,0:T(8,128)(2,1)}, u32[]{:S(2)}) copy-start(bf16[384,768]{1,0:T(8,128)(2,1)} %param.16) | copy-start | bytes 1769476
  3.4 6.9 %collective-permute-start = (bf16[320,384]{1,0:T(8,128)(2,1)S(1)}, bf16[320,384]{1,0:T(8,128)(2,1)S(1)}, u32[]{:S(2)}, u32[]{:S(2)}) collective-permute-start(bf16[320,384]{1,0:T(8,128)(2,1)S(1)} %get-tuple-element.184), channel_id=1, source_target_pairs={{0,8},{4,12},{8,16},{12,20},{16,24},{20,28},{24,0},{28,4},{1,9},{5... | collective-permute-start | bytes 737288 | tf_op jit(solution)/shard_map/ppermute | solution.py:99
  3.4 22.4 %collective-permute-start.1 = (bf16[320,384]{1,0:T(8,128)(2,1)S(1)}, bf16[320,384]{1,0:T(8,128)(2,1)S(1)}, u32[]{:S(2)}, u32[]{:S(2)}) collective-permute-start(bf16[320,384]{1,0:T(8,128)(2,1)S(1)} %get-tuple-element.184), channel_id=1, source_target_pairs={{0,16},{4,20},{8,24},{12,28},{16,0},{20,4},{24,8},{28,12},{1,17},{... | collective-permute-start | bytes 737288 | tf_op jit(solution)/shard_map/ppermute | solution.py:99
  4.7 21.2 %collective-permute-start.2 = (bf16[320,384]{1,0:T(8,128)(2,1)S(1)}, bf16[320,384]{1,0:T(8,128)(2,1)S(1)}, u32[]{:S(2)}, u32[]{:S(2)}) collective-permute-start(bf16[320,384]{1,0:T(8,128)(2,1)S(1)} %get-tuple-element.184), channel_id=1, source_target_pairs={{0,24},{4,28},{8,0},{12,4},{16,8},{20,12},{24,16},{28,20},{1,25},{... | collective-permute-start | bytes 737288 | tf_op jit(solution)/shard_map/ppermute | solution.py:99
  27.0 22.0 %collective-permute-start.5 = (bf16[4,320,384]{2,1,0:T(8,128)(2,1)}, bf16[4,320,384]{2,1,0:T(8,128)(2,1)}, u32[]{:S(2)}, u32[]{:S(2)}) collective-permute-start(bf16[4,320,384]{2,1,0:T(8,128)(2,1)} %pad_maximum_fusion.2.refs_0_), channel_id=1, source_target_pairs={{0,4},{4,0},{8,12},{12,8},{16,20},{20,16},{24,28},{28,24},{1,5},{5... | collective-permute-start | bytes 2949128 | tf_op jit(solution)/shard_map/ppermute | solution.py:95
  29.7 27.7 %copy-start.4 = (bf16[1024,768]{1,0:T(8,128)(2,1)S(1)}, bf16[1024,768]{1,0:T(8,128)(2,1)}, u32[]{:S(2)}) copy-start(bf16[1024,768]{1,0:T(8,128)(2,1)} %refs_0_.1) | copy-start | bytes 4718596
  31.8 25.5 %collective-permute-start.6 = (bf16[4,320,384]{2,1,0:T(8,128)(2,1)}, bf16[4,320,384]{2,1,0:T(8,128)(2,1)S(1)}, u32[]{:S(2)}, u32[]{:S(2)}) collective-permute-start(bf16[4,320,384]{2,1,0:T(8,128)(2,1)} %pad_maximum_fusion.2.refs_0_), channel_id=1, source_target_pairs={{0,1},{1,0},{2,3},{3,2},{4,5},{5,4},{6,7},{7,6},{8,9},{9,8},{10,11... | collective-permute-start | bytes 2949128 | tf_op jit(solution)/shard_map/ppermute | solution.py:87
  33.7 20.1 %collective-permute-start.3 = (bf16[624,384]{1,0:T(8,128)(2,1)S(1)}, bf16[624,384]{1,0:T(8,128)(2,1)S(1)}, u32[]{:S(2)}, u32[]{:S(2)}) collective-permute-start(bf16[624,384]{1,0:T(8,128)(2,1)S(1)} %pad_maximum_fusion.4), channel_id=1, source_target_pairs={{0,8},{4,12},{8,16},{12,20},{16,24},{20,28},{24,0},{28,4},{1,9},{5... | collective-permute-start | bytes 1437704 | tf_op jit(solution)/shard_map/ppermute | solution.py:99
  33.7 23.6 %collective-permute-start.4 = (bf16[624,384]{1,0:T(8,128)(2,1)S(1)}, bf16[624,384]{1,0:T(8,128)(2,1)S(1)}, u32[]{:S(2)}, u32[]{:S(2)}) collective-permute-start(bf16[624,384]{1,0:T(8,128)(2,1)S(1)} %pad_maximum_fusion.4), channel_id=1, source_target_pairs={{0,24},{4,28},{8,0},{12,4},{16,8},{20,12},{24,16},{28,20},{1,25},{... | collective-permute-start | bytes 1437704 | tf_op jit(solution)/shard_map/ppermute | solution.py:99
  49.0 8.4 %collective-permute-start.7 = (bf16[4,320,384]{2,1,0:T(8,128)(2,1)}, bf16[4,320,384]{2,1,0:T(8,128)(2,1)S(1)}, u32[]{:S(2)}, u32[]{:S(2)}) collective-permute-start(bf16[4,320,384]{2,1,0:T(8,128)(2,1)} %collective-permute-done.5.refs_1_), channel_id=1, source_target_pairs={{0,1},{1,0},{2,3},{3,2},{4,5},{5,4},{6,7},{7,6},{8,9},{9,8},{10,11... | collective-permute-start | bytes 2949128 | tf_op jit(solution)/shard_map/ppermute | solution.py:87
  51.5 30.2 %collective-permute-start.8 = (bf16[624,384]{1,0:T(8,128)(2,1)S(1)}, bf16[624,384]{1,0:T(8,128)(2,1)S(1)}, u32[]{:S(2)}, u32[]{:S(2)}) collective-permute-start(bf16[624,384]{1,0:T(8,128)(2,1)S(1)} %pad_maximum_fusion.4), channel_id=1, source_target_pairs={{0,16},{4,20},{8,24},{12,28},{16,0},{20,4},{24,8},{28,12},{1,17},{... | collective-permute-start | bytes 1437704 | tf_op jit(solution)/shard_map/ppermute | solution.py:99
  66.1 17.5 %copy-start = (bf16[1024,2304]{1,0:T(8,128)(2,1)}, bf16[1024,2304]{1,0:T(8,128)(2,1)S(1)}, u32[]{:S(2)}) copy-start(bf16[1024,2304]{1,0:T(8,128)(2,1)S(1)} %get-tuple-element.83.qkv_ref) | copy-start | bytes 14155780
  81.7 36.8 %copy-start.7 = (bf16[1024,384]{1,0:T(8,128)(2,1)}, bf16[1024,384]{1,0:T(8,128)(2,1)S(1)}, u32[]{:S(2)}) copy-start(bf16[1024,384]{1,0:T(8,128)(2,1)S(1)} %get-tuple-element.81.ctx_ref) | copy-start | bytes 2359300
  81.9 17.6 %collective-permute-start.10 = (bf16[4,240,384]{2,1,0:T(8,128)(2,1)S(1)}, bf16[4,240,384]{2,1,0:T(8,128)(2,1)S(1)}, u32[]{:S(2)}, u32[]{:S(2)}) collective-permute-start(bf16[4,240,384]{2,1,0:T(8,128)(2,1)S(1)} %pad_maximum_fusion.3.refs_0_), channel_id=1, source_target_pairs={{0,2},{1,3},{2,0},{3,1},{4,6},{5,7},{6,4},{7,5},{8,10},{9,11},{10,... | collective-permute-start | bytes 2211848 | tf_op jit(solution)/shard_map/ppermute | solution.py:91
  83.2 16.3 %collective-permute-start.9 = (bf16[4,240,384]{2,1,0:T(8,128)(2,1)S(1)}, bf16[4,240,384]{2,1,0:T(8,128)(2,1)S(1)}, u32[]{:S(2)}, u32[]{:S(2)}) collective-permute-start(bf16[4,240,384]{2,1,0:T(8,128)(2,1)S(1)} %pad_maximum_fusion.3.refs_0_), channel_id=1, source_target_pairs={{0,4},{4,0},{8,12},{12,8},{16,20},{20,16},{24,28},{28,24},{1,5},{5... | collective-permute-start | bytes 2211848 | tf_op jit(solution)/shard_map/ppermute | solution.py:95
  99.5 15.6 %collective-permute-start.11 = (bf16[4,240,384]{2,1,0:T(8,128)(2,1)S(1)}, bf16[4,240,384]{2,1,0:T(8,128)(2,1)S(1)}, u32[]{:S(2)}, u32[]{:S(2)}) collective-permute-start(bf16[4,240,384]{2,1,0:T(8,128)(2,1)S(1)} %collective-permute-done.9.refs_1_), channel_id=1, source_target_pairs={{0,2},{1,3},{2,0},{3,1},{4,6},{5,7},{6,4},{7,5},{8,10},{9,11},{10,... | collective-permute-start | bytes 2211848 | tf_op jit(solution)/shard_map/ppermute | solution.py:91
  99.8 19.0 %collective-permute-start.12 = (bf16[4,240,384]{2,1,0:T(8,128)(2,1)S(1)}, bf16[4,240,384]{2,1,0:T(8,128)(2,1)S(1)}, u32[]{:S(2)}, u32[]{:S(2)}) collective-permute-start(bf16[4,240,384]{2,1,0:T(8,128)(2,1)S(1)} %pad_maximum_fusion.3.refs_0_), channel_id=1, source_target_pairs={{0,1},{1,0},{2,3},{3,2},{4,5},{5,4},{6,7},{7,6},{8,9},{9,8},{10,11... | collective-permute-start | bytes 2211848 | tf_op jit(solution)/shard_map/ppermute | solution.py:87
  102.6 17.6 %collective-permute-start.13 = (bf16[4,240,384]{2,1,0:T(8,128)(2,1)S(1)}, bf16[4,240,384]{2,1,0:T(8,128)(2,1)S(1)}, u32[]{:S(2)}, u32[]{:S(2)}) collective-permute-start(bf16[4,240,384]{2,1,0:T(8,128)(2,1)S(1)} %collective-permute-done.9.refs_1_), channel_id=1, source_target_pairs={{0,1},{1,0},{2,3},{3,2},{4,5},{5,4},{6,7},{7,6},{8,9},{9,8},{10,11... | collective-permute-start | bytes 2211848 | tf_op jit(solution)/shard_map/ppermute | solution.py:87
  102.6 17.6 %collective-permute-start.14 = (bf16[4,240,384]{2,1,0:T(8,128)(2,1)S(1)}, bf16[4,240,384]{2,1,0:T(8,128)(2,1)S(1)}, u32[]{:S(2)}, u32[]{:S(2)}) collective-permute-start(bf16[4,240,384]{2,1,0:T(8,128)(2,1)S(1)} %collective-permute-done.10.refs_2_), channel_id=1, source_target_pairs={{0,1},{1,0},{2,3},{3,2},{4,5},{5,4},{6,7},{7,6},{8,9},{9,8},{10,11... | collective-permute-start | bytes 2211848 | tf_op jit(solution)/shard_map/ppermute | solution.py:87
  115.1 6.3 %collective-permute-start.15 = (bf16[4,240,384]{2,1,0:T(8,128)(2,1)S(1)}, bf16[4,240,384]{2,1,0:T(8,128)(2,1)S(1)}, u32[]{:S(2)}, u32[]{:S(2)}) collective-permute-start(bf16[4,240,384]{2,1,0:T(8,128)(2,1)S(1)} %collective-permute-done.11.refs_3_), channel_id=1, source_target_pairs={{0,1},{1,0},{2,3},{3,2},{4,5},{5,4},{6,7},{7,6},{8,9},{9,8},{10,11... | collective-permute-start | bytes 2211848 | tf_op jit(solution)/shard_map/ppermute | solution.py:87
  118.5 29.6 %collective-permute-start.17 = (bf16[4,384,384]{2,1,0:T(8,128)(2,1)S(1)}, bf16[4,384,384]{2,1,0:T(8,128)(2,1)}, u32[]{:S(2)}, u32[]{:S(2)}) collective-permute-start(bf16[4,384,384]{2,1,0:T(8,128)(2,1)S(1)} %pad_maximum_fusion.1.refs_0_), channel_id=1, source_target_pairs={{0,1},{1,0},{2,3},{3,2},{4,5},{5,4},{6,7},{7,6},{8,9},{9,8},{10,11... | collective-permute-start | bytes 3538952 | tf_op jit(solution)/shard_map/ppermute | solution.py:87
  118.8 27.2 %collective-permute-start.16 = (bf16[4,384,384]{2,1,0:T(8,128)(2,1)S(1)}, bf16[4,384,384]{2,1,0:T(8,128)(2,1)}, u32[]{:S(2)}, u32[]{:S(2)}) collective-permute-start(bf16[4,384,384]{2,1,0:T(8,128)(2,1)S(1)} %pad_maximum_fusion.1.refs_0_), channel_id=1, source_target_pairs={{0,4},{4,0},{8,12},{12,8},{16,20},{20,16},{24,28},{28,24},{1,5},{5... | collective-permute-start | bytes 3538952 | tf_op jit(solution)/shard_map/ppermute | solution.py:95
  124.1 28.1 %copy-start.29 = (f32[1024,768]{1,0:T(8,128)}, f32[1024,768]{1,0:T(8,128)S(1)}, u32[]{:S(2)}) copy-start(f32[1024,768]{1,0:T(8,128)S(1)} %get-tuple-element.192) | copy-start | bytes 9437188
  139.2 13.0 %copy-start.10 = (bf16[1024,3072]{1,0:T(8,128)(2,1)}, bf16[1024,3072]{1,0:T(8,128)(2,1)S(1)}, u32[]{:S(2)}) copy-start(bf16[1024,3072]{1,0:T(8,128)(2,1)S(1)} %get-tuple-element.91.active_ref) | copy-start | bytes 18874372
  146.0 4.0 %collective-permute-start.18 = (bf16[4,384,384]{2,1,0:T(8,128)(2,1)}, bf16[4,384,384]{2,1,0:T(8,128)(2,1)S(1)}, u32[]{:S(2)}, u32[]{:S(2)}) collective-permute-start(bf16[4,384,384]{2,1,0:T(8,128)(2,1)} %collective-permute-done.16.refs_1_), channel_id=1, source_target_pairs={{0,1},{1,0},{2,3},{3,2},{4,5},{5,4},{6,7},{7,6},{8,9},{9,8},{10,11... | collective-permute-start | bytes 3538952 | tf_op jit(solution)/shard_map/ppermute | solution.py:87
  191.9 7.7 %collective-permute-start.20 = (bf16[2,4,384,384]{3,2,1,0:T(8,128)(2,1)}, bf16[2,4,384,384]{3,2,1,0:T(8,128)(2,1)}, u32[]{:S(2)}, u32[]{:S(2)}) collective-permute-start(bf16[2,4,384,384]{3,2,1,0:T(8,128)(2,1)} %get-tuple-element.99), channel_id=1, source_target_pairs={{0,1},{1,0},{2,3},{3,2},{4,5},{5,4},{6,7},{7,6},{8,9},{9,8},{10,11... | collective-permute-start | bytes 7077896 | tf_op jit(solution)/shard_map/ppermute | solution.py:87
  192.3 14.2 %collective-permute-start.19 = (bf16[2,4,384,384]{3,2,1,0:T(8,128)(2,1)}, bf16[2,4,384,384]{3,2,1,0:T(8,128)(2,1)}, u32[]{:S(2)}, u32[]{:S(2)}) collective-permute-start(bf16[2,4,384,384]{3,2,1,0:T(8,128)(2,1)} %get-tuple-element.97), channel_id=1, source_target_pairs={{0,1},{1,0},{2,3},{3,2},{4,5},{5,4},{6,7},{7,6},{8,9},{9,8},{10,11... | collective-permute-start | bytes 7077896 | tf_op jit(solution)/shard_map/ppermute | solution.py:87
  201.4 27.2 %collective-permute-start.21 = (bf16[4,384,384]{2,1,0:T(8,128)(2,1)S(1)}, bf16[4,384,384]{2,1,0:T(8,128)(2,1)S(1)}, u32[]{:S(2)}, u32[]{:S(2)}) collective-permute-start(bf16[4,384,384]{2,1,0:T(8,128)(2,1)S(1)} %fusion.4), channel_id=1, source_target_pairs={{0,4},{4,0},{8,12},{12,8},{16,20},{20,16},{24,28},{28,24},{1,5},{5... | collective-permute-start | bytes 3538952 | tf_op jit(solution)/shard_map/ppermute | solution.py:95
  208.7 30.5 %collective-permute-start.22 = (bf16[2,4,192,384]{3,2,1,0:T(8,128)(2,1)S(1)}, bf16[2,4,192,384]{3,2,1,0:T(8,128)(2,1)S(1)}, u32[]{:S(2)}, u32[]{:S(2)}) collective-permute-start(bf16[2,4,192,384]{3,2,1,0:T(8,128)(2,1)S(1)} %add_convert_fusion.2), channel_id=1, source_target_pairs={{0,2},{1,3},{2,0},{3,1},{4,6},{5,7},{6,4},{7,5},{8,10},{9,11},{10,... | collective-permute-start | bytes 3538952 | tf_op jit(solution)/shard_map/ppermute | solution.py:91
  209.2 30.1 %copy-start.33 = (f32[2,4,192,384]{3,2,1,0:T(8,128)}, f32[2,4,192,384]{3,2,1,0:T(8,128)S(1)}, u32[]{:S(2)}) copy-start(f32[2,4,192,384]{3,2,1,0:T(8,128)S(1)} %dynamic-slice_convert_fusion.1) | copy-start | bytes 7077892
  223.2 15.2 %copy-start.9 = (bf16[1024,768]{1,0:T(8,128)(2,1)}, bf16[1024,768]{1,0:T(8,128)(2,1)S(1)}, u32[]{:S(2)}) copy-start(bf16[1024,768]{1,0:T(8,128)(2,1)S(1)} %get-tuple-element.102) | copy-start | bytes 4718596
  225.2 14.0 %copy-start.35 = (f32[2,4,192,384]{3,2,1,0:T(8,128)}, f32[2,4,192,384]{3,2,1,0:T(8,128)S(1)}, u32[]{:S(2)}) copy-start(f32[2,4,192,384]{3,2,1,0:T(8,128)S(1)} %dynamic-slice_convert_fusion) | copy-start | bytes 7077892
  241.5 9.8 %copy-start.52 = (bf16[768]{0:T(1024)(128)(2,1)S(1)}, bf16[768]{0:T(1024)(128)(2,1)}, u32[]{:S(2)}) copy-start(bf16[768]{0:T(1024)(128)(2,1)} %get-tuple-element.155) | copy-start | bytes 4612
  247.8 19.3 %collective-permute-start.23 = (bf16[2,4,240,384]{3,2,1,0:T(8,128)(2,1)}, bf16[2,4,240,384]{3,2,1,0:T(8,128)(2,1)}, u32[]{:S(2)}, u32[]{:S(2)}) collective-permute-start(bf16[2,4,240,384]{3,2,1,0:T(8,128)(2,1)} %get-tuple-element.112), channel_id=1, source_target_pairs={{0,1},{1,0},{2,3},{3,2},{4,5},{5,4},{6,7},{7,6},{8,9},{9,8},{10,11... | collective-permute-start | bytes 4423688 | tf_op jit(solution)/shard_map/ppermute | solution.py:87
  252.1 15.0 %collective-permute-start.24 = (bf16[4,192,384]{2,1,0:T(8,128)(2,1)S(1)}, bf16[4,192,384]{2,1,0:T(8,128)(2,1)S(1)}, u32[]{:S(2)}, u32[]{:S(2)}) collective-permute-start(bf16[4,192,384]{2,1,0:T(8,128)(2,1)S(1)} %fusion.6), channel_id=1, source_target_pairs={{0,4},{4,0},{8,12},{12,8},{16,20},{20,16},{24,28},{28,24},{1,5},{5... | collective-permute-start | bytes 1769480 | tf_op jit(solution)/shard_map/ppermute | solution.py:95
  253.4 27.1 %collective-permute-start.25 = (bf16[384,384]{1,0:T(8,128)(2,1)}, bf16[384,384]{1,0:T(8,128)(2,1)S(1)}, u32[]{:S(2)}, u32[]{:S(2)}) collective-permute-start(bf16[384,384]{1,0:T(8,128)(2,1)} %get-tuple-element.173), channel_id=1, source_target_pairs={{0,8},{4,12},{8,16},{12,20},{16,24},{20,28},{24,0},{28,4},{1,9},{5... | collective-permute-start | bytes 884744 | tf_op jit(solution)/shard_map/ppermute | solution.py:99
  254.8 25.7 %collective-permute-start.26 = (bf16[384,384]{1,0:T(8,128)(2,1)}, bf16[384,384]{1,0:T(8,128)(2,1)S(1)}, u32[]{:S(2)}, u32[]{:S(2)}) collective-permute-start(bf16[384,384]{1,0:T(8,128)(2,1)} %get-tuple-element.172), channel_id=1, source_target_pairs={{0,16},{4,20},{8,24},{12,28},{16,0},{20,4},{24,8},{28,12},{1,17},{... | collective-permute-start | bytes 884744 | tf_op jit(solution)/shard_map/ppermute | solution.py:99
  254.8 25.7 %collective-permute-start.27 = (bf16[384,384]{1,0:T(8,128)(2,1)}, bf16[384,384]{1,0:T(8,128)(2,1)S(1)}, u32[]{:S(2)}, u32[]{:S(2)}) collective-permute-start(bf16[384,384]{1,0:T(8,128)(2,1)} %get-tuple-element.171), channel_id=1, source_target_pairs={{0,24},{4,28},{8,0},{12,4},{16,8},{20,12},{24,16},{28,20},{1,25},{... | collective-permute-start | bytes 884744 | tf_op jit(solution)/shard_map/ppermute | solution.py:99
  271.1 37.7 %collective-permute-start.31 = (bf16[4,240,384]{2,1,0:T(8,128)(2,1)}, bf16[4,240,384]{2,1,0:T(8,128)(2,1)}, u32[]{:S(2)}, u32[]{:S(2)}) collective-permute-start(bf16[4,240,384]{2,1,0:T(8,128)(2,1)} %fusion.5), channel_id=1, source_target_pairs={{0,4},{4,0},{8,12},{12,8},{16,20},{20,16},{24,28},{28,24},{1,5},{5... | collective-permute-start | bytes 2211848 | tf_op jit(solution)/shard_map/ppermute | solution.py:95
  296.9 16.7 %collective-permute-start.33 = (bf16[2,4,160,384]{3,2,1,0:T(8,128)(2,1)S(1)}, bf16[2,4,160,384]{3,2,1,0:T(8,128)(2,1)S(1)}, u32[]{:S(2)}, u32[]{:S(2)}) collective-permute-start(bf16[2,4,160,384]{3,2,1,0:T(8,128)(2,1)S(1)} %get-tuple-element.130), channel_id=1, source_target_pairs={{0,1},{1,0},{2,3},{3,2},{4,5},{5,4},{6,7},{7,6},{8,9},{9,8},{10,11... | collective-permute-start | bytes 2949128 | tf_op jit(solution)/shard_map/ppermute | solution.py:87
  299.7 9.1 %copy-start.24 = (bf16[2,4,240,384]{3,2,1,0:T(8,128)(2,1)S(1)}, bf16[2,4,240,384]{3,2,1,0:T(8,128)(2,1)}, u32[]{:S(2)}) copy-start(bf16[2,4,240,384]{3,2,1,0:T(8,128)(2,1)} %copy-done.22) | copy-start | bytes 4423684
  299.7 8.6 %collective-permute-start.32 = (bf16[384,384]{1,0:T(8,128)(2,1)S(1)}, bf16[384,384]{1,0:T(8,128)(2,1)S(1)}, u32[]{:S(2)}, u32[]{:S(2)}) collective-permute-start(bf16[384,384]{1,0:T(8,128)(2,1)S(1)} %fusion.7), channel_id=1, source_target_pairs={{0,2},{1,3},{2,0},{3,1},{4,6},{5,7},{6,4},{7,5},{8,10},{9,11},{10,... | collective-permute-start | bytes 884744 | tf_op jit(solution)/shard_map/ppermute | solution.py:91
  300.4 13.7 %collective-permute-start.28 = (bf16[192,384]{1,0:T(8,128)(2,1)S(1)}, bf16[192,384]{1,0:T(8,128)(2,1)S(1)}, u32[]{:S(2)}, u32[]{:S(2)}) collective-permute-start(bf16[192,384]{1,0:T(8,128)(2,1)S(1)} %copy-done.47), channel_id=1, source_target_pairs={{0,8},{4,12},{8,16},{12,20},{16,24},{20,28},{24,0},{28,4},{1,9},{5... | collective-permute-start | bytes 442376 | tf_op jit(solution)/shard_map/ppermute | solution.py:99
  301.8 13.8 %collective-permute-start.29 = (bf16[192,384]{1,0:T(8,128)(2,1)S(1)}, bf16[192,384]{1,0:T(8,128)(2,1)S(1)}, u32[]{:S(2)}, u32[]{:S(2)}) collective-permute-start(bf16[192,384]{1,0:T(8,128)(2,1)S(1)} %get-tuple-element.178), channel_id=1, source_target_pairs={{0,16},{4,20},{8,24},{12,28},{16,0},{20,4},{24,8},{28,12},{1,17},{... | collective-permute-start | bytes 442376 | tf_op jit(solution)/shard_map/ppermute | solution.py:99
  308.3 8.9 %collective-permute-start.30 = (bf16[192,384]{1,0:T(8,128)(2,1)S(1)}, bf16[192,384]{1,0:T(8,128)(2,1)S(1)}, u32[]{:S(2)}, u32[]{:S(2)}) collective-permute-start(bf16[192,384]{1,0:T(8,128)(2,1)S(1)} %get-tuple-element.177), channel_id=1, source_target_pairs={{0,24},{4,28},{8,0},{12,4},{16,8},{20,12},{24,16},{28,20},{1,25},{... | collective-permute-start | bytes 442376 | tf_op jit(solution)/shard_map/ppermute | solution.py:99
  308.8 11.0 %copy-start.38 = (f32[1024,768]{1,0:T(8,128)S(1)}, f32[1024,768]{1,0:T(8,128)}, u32[]{:S(2)}) copy-start(f32[1024,768]{1,0:T(8,128)} %get-tuple-element.166) | copy-start | bytes 9437188
  310.6 9.2 %copy-start.26 = (bf16[768,2304]{1,0:T(8,128)(2,1)S(1)}, bf16[768,2304]{1,0:T(8,128)(2,1)}, u32[]{:S(2)}) copy-start(bf16[768,2304]{1,0:T(8,128)(2,1)} %copy-done.25) | copy-start | bytes 10616836
  310.7 17.6 %collective-permute-start.34 = (bf16[240,384]{1,0:T(8,128)(2,1)S(1)}, bf16[240,384]{1,0:T(8,128)(2,1)S(1)}, u32[]{:S(2)}, u32[]{:S(2)}) collective-permute-start(bf16[240,384]{1,0:T(8,128)(2,1)S(1)} %get-tuple-element.176), channel_id=1, source_target_pairs={{0,8},{4,12},{8,16},{12,20},{16,24},{20,28},{24,0},{28,4},{1,9},{5... | collective-permute-start | bytes 552968 | tf_op jit(solution)/shard_map/ppermute | solution.py:99
  313.6 18.4 %collective-permute-start.35 = (bf16[240,384]{1,0:T(8,128)(2,1)S(1)}, bf16[240,384]{1,0:T(8,128)(2,1)S(1)}, u32[]{:S(2)}, u32[]{:S(2)}) collective-permute-start(bf16[240,384]{1,0:T(8,128)(2,1)S(1)} %get-tuple-element.175), channel_id=1, source_target_pairs={{0,16},{4,20},{8,24},{12,28},{16,0},{20,4},{24,8},{28,12},{1,17},{... | collective-permute-start | bytes 552968 | tf_op jit(solution)/shard_map/ppermute | solution.py:99
  314.2 17.8 %collective-permute-start.36 = (bf16[240,384]{1,0:T(8,128)(2,1)S(1)}, bf16[240,384]{1,0:T(8,128)(2,1)S(1)}, u32[]{:S(2)}, u32[]{:S(2)}) collective-permute-start(bf16[240,384]{1,0:T(8,128)(2,1)S(1)} %get-tuple-element.174), channel_id=1, source_target_pairs={{0,24},{4,28},{8,0},{12,4},{16,8},{20,12},{24,16},{28,20},{1,25},{... | collective-permute-start | bytes 552968 | tf_op jit(solution)/shard_map/ppermute | solution.py:99
  315.6 12.4 %collective-permute-start.38 = (bf16[4,160,384]{2,1,0:T(8,128)(2,1)S(1)}, bf16[4,160,384]{2,1,0:T(8,128)(2,1)S(1)}, u32[]{:S(2)}, u32[]{:S(2)}) collective-permute-start(bf16[4,160,384]{2,1,0:T(8,128)(2,1)S(1)} %fusion.12), channel_id=1, source_target_pairs={{0,4},{4,0},{8,12},{12,8},{16,20},{20,16},{24,28},{28,24},{1,5},{5... | collective-permute-start | bytes 1474568 | tf_op jit(solution)/shard_map/ppermute | solution.py:95
  317.3 7.4 %collective-permute-start.49 = (bf16[384,384]{1,0:T(8,128)(2,1)S(1)}, bf16[384,384]{1,0:T(8,128)(2,1)S(1)}, u32[]{:S(2)}, u32[]{:S(2)}) collective-permute-start(bf16[384,384]{1,0:T(8,128)(2,1)S(1)} %add_convert_fusion.6), channel_id=1, source_target_pairs={{0,1},{1,0},{2,3},{3,2},{4,5},{5,4},{6,7},{7,6},{8,9},{9,8},{10,11... | collective-permute-start | bytes 884744 | tf_op jit(solution)/shard_map/ppermute | solution.py:87
  324.7 7.2 %collective-permute-start.37 = (bf16[192,384]{1,0:T(8,128)(2,1)S(1)}, bf16[192,384]{1,0:T(8,128)(2,1)S(1)}, u32[]{:S(2)}, u32[]{:S(2)}) collective-permute-start(bf16[192,384]{1,0:T(8,128)(2,1)S(1)} %fusion.17), channel_id=1, source_target_pairs={{0,2},{1,3},{2,0},{3,1},{4,6},{5,7},{6,4},{7,5},{8,10},{9,11},{10,... | collective-permute-start | bytes 442376 | tf_op jit(solution)/shard_map/ppermute | solution.py:91
  332.1 20.7 %collective-permute-start.39 = (bf16[240,384]{1,0:T(8,128)(2,1)S(1)}, bf16[240,384]{1,0:T(8,128)(2,1)S(1)}, u32[]{:S(2)}, u32[]{:S(2)}) collective-permute-start(bf16[240,384]{1,0:T(8,128)(2,1)S(1)} %fusion.13), channel_id=1, source_target_pairs={{0,2},{1,3},{2,0},{3,1},{4,6},{5,7},{6,4},{7,5},{8,10},{9,11},{10,... | collective-permute-start | bytes 552968 | tf_op jit(solution)/shard_map/ppermute | solution.py:242
  333.2 19.9 %collective-permute-start.40 = (bf16[240,384]{1,0:T(8,128)(2,1)S(1)}, bf16[240,384]{1,0:T(8,128)(2,1)S(1)}, u32[]{:S(2)}, u32[]{:S(2)}) collective-permute-start(bf16[240,384]{1,0:T(8,128)(2,1)S(1)} %fusion.13), channel_id=1, source_target_pairs={{0,1},{1,0},{2,3},{3,2},{4,5},{5,4},{6,7},{7,6},{8,9},{9,8},{10,11... | collective-permute-start | bytes 552968 | tf_op jit(solution)/shard_map/ppermute | solution.py:242
  334.3 7.7 %collective-permute-start.42 = (bf16[160,384]{1,0:T(8,128)(2,1)S(1)}, bf16[160,384]{1,0:T(8,128)(2,1)S(1)}, u32[]{:S(2)}, u32[]{:S(2)}) collective-permute-start(bf16[160,384]{1,0:T(8,128)(2,1)S(1)} %get-tuple-element.182), channel_id=1, source_target_pairs={{0,8},{4,12},{8,16},{12,20},{16,24},{20,28},{24,0},{28,4},{1,9},{5... | collective-permute-start | bytes 368648 | tf_op jit(solution)/shard_map/ppermute | solution.py:99
  337.3 14.7 %collective-permute-start.43 = (bf16[160,384]{1,0:T(8,128)(2,1)S(1)}, bf16[160,384]{1,0:T(8,128)(2,1)S(1)}, u32[]{:S(2)}, u32[]{:S(2)}) collective-permute-start(bf16[160,384]{1,0:T(8,128)(2,1)S(1)} %get-tuple-element.181), channel_id=1, source_target_pairs={{0,16},{4,20},{8,24},{12,28},{16,0},{20,4},{24,8},{28,12},{1,17},{... | collective-permute-start | bytes 368648 | tf_op jit(solution)/shard_map/ppermute | solution.py:99
  340.4 12.2 %collective-permute-start.44 = (bf16[160,384]{1,0:T(8,128)(2,1)S(1)}, bf16[160,384]{1,0:T(8,128)(2,1)S(1)}, u32[]{:S(2)}, u32[]{:S(2)}) collective-permute-start(bf16[160,384]{1,0:T(8,128)(2,1)S(1)} %get-tuple-element.180), channel_id=1, source_target_pairs={{0,24},{4,28},{8,0},{12,4},{16,8},{20,12},{24,16},{28,20},{1,25},{... | collective-permute-start | bytes 368648 | tf_op jit(solution)/shard_map/ppermute | solution.py:99
  342.1 12.6 %collective-permute-start.41 = (bf16[240,384]{1,0:T(8,128)(2,1)S(1)}, bf16[240,384]{1,0:T(8,128)(2,1)S(1)}, u32[]{:S(2)}, u32[]{:S(2)}) collective-permute-start(bf16[240,384]{1,0:T(8,128)(2,1)S(1)} %fusion.13), channel_id=1, source_target_pairs={{0,3},{1,2},{2,1},{3,0},{4,7},{5,6},{6,5},{7,4},{8,11},{9,10},{10,... | collective-permute-start | bytes 552968 | tf_op jit(solution)/shard_map/ppermute | solution.py:242
  352.0 11.9 %collective-permute-start.48 = (bf16[384,384]{1,0:T(8,128)(2,1)S(1)}, bf16[384,384]{1,0:T(8,128)(2,1)S(1)}, u32[]{:S(2)}, u32[]{:S(2)}) collective-permute-start(bf16[384,384]{1,0:T(8,128)(2,1)S(1)} %maximum_select_fusion.4), channel_id=1, source_target_pairs={{0,1},{1,0},{2,3},{3,2},{4,5},{5,4},{6,7},{7,6},{8,9},{9,8},{10,11... | collective-permute-start | bytes 884744 | tf_op jit(solution)/shard_map/ppermute | solution.py:87
  352.6 5.0 %collective-permute-start.45 = (bf16[160,384]{1,0:T(8,128)(2,1)S(1)}, bf16[160,384]{1,0:T(8,128)(2,1)S(1)}, u32[]{:S(2)}, u32[]{:S(2)}) collective-permute-start(bf16[160,384]{1,0:T(8,128)(2,1)S(1)} %fusion.18), channel_id=1, source_target_pairs={{0,2},{1,3},{2,0},{3,1},{4,6},{5,7},{6,4},{7,5},{8,10},{9,11},{10,... | collective-permute-start | bytes 368648 | tf_op jit(solution)/shard_map/ppermute | solution.py:242
  352.7 5.0 %collective-permute-start.46 = (bf16[160,384]{1,0:T(8,128)(2,1)S(1)}, bf16[160,384]{1,0:T(8,128)(2,1)S(1)}, u32[]{:S(2)}, u32[]{:S(2)}) collective-permute-start(bf16[160,384]{1,0:T(8,128)(2,1)S(1)} %fusion.18), channel_id=1, source_target_pairs={{0,1},{1,0},{2,3},{3,2},{4,5},{5,4},{6,7},{7,6},{8,9},{9,8},{10,11... | collective-permute-start | bytes 368648 | tf_op jit(solution)/shard_map/ppermute | solution.py:242
  353.1 7.3 %collective-permute-start.47 = (bf16[160,384]{1,0:T(8,128)(2,1)S(1)}, bf16[160,384]{1,0:T(8,128)(2,1)S(1)}, u32[]{:S(2)}, u32[]{:S(2)}) collective-permute-start(bf16[160,384]{1,0:T(8,128)(2,1)S(1)} %fusion.18), channel_id=1, source_target_pairs={{0,3},{1,2},{2,1},{3,0},{4,7},{5,6},{6,5},{7,4},{8,11},{9,10},{10,... | collective-permute-start | bytes 368648 | tf_op jit(solution)/shard_map/ppermute | solution.py:242
  (47 other events, 182.7 us)

commit v3 on v2

--- a/solution.py
+++ b/solution.py
@@ -35,6 +35,10 @@
     return pl.CostEstimate(
         flops=flops // CHEAP, bytes_accessed=bytes_accessed // CHEAP, transcendentals=transcendentals // CHEAP
     )
+
+
+def at_once(shape):
+    return pl.BlockSpec(shape, lambda i: (0,) * len(shape), pipeline_mode=pl.Buffered(1))
 
 
 def layout(length_row, row_count):
@@ -177,12 +181,12 @@
 
 
 def put_together(kernel, near, pieces, shapes):
-    whole = pl.BlockSpec(memory_space=pltpu.VMEM)
     return pl.pallas_call(
         kernel,
+        grid=(1,),
         out_shape=tuple(jax.ShapeDtypeStruct(shape, jnp.bfloat16) for shape in shapes),
-        in_specs=[pl.BlockSpec(memory_space=pltpu.SMEM)] + [whole] * len(pieces),
-        out_specs=(whole,) * len(shapes),
+        in_specs=[pl.BlockSpec(memory_space=pltpu.SMEM)] + [at_once(piece.shape) for piece in pieces],
+        out_specs=tuple(at_once(shape) for shape in shapes),
         compiler_params=vmem(16),
         cost_estimate=cost(0, 4 * sum(math.prod(shape) for shape in shapes), 0),
     )(near, *pieces)
@@ -192,7 +196,6 @@
     def __init__(self, place, mate, mine, split_x=False):
         self.place, self.split_x = place, split_x
         self.both = [mine, swap_core(mate)]
-        self.others = []
 
     def part(self, rows, side):
         half = rows.shape[2] // 2
@@ -243,10 +246,6 @@
         return self
 
     def finish(self):
-        if self.others:
-            x, core, both = (wide(rows) for rows in self.others)
-            mine, theirs = wide(self.total) + x, core + both
-            return jnp.where(self.place.c == 0, jnp.stack([mine, theirs]), jnp.stack([theirs, mine]))
         both = jnp.stack([self.total, self.far]), jnp.stack([self.far, self.total])
         return wide(jnp.where(self.place.c == 0, *both))
 
@@ -561,15 +560,15 @@
     keep_halves(low(wide_dot(edge_left[...], edge_right[...], TN)), c, mate_ref, mine_ref, edge_of)
 
 
-def whole_grad(kernel, near, arrays, rows, flops):
+def whole_grad(kernel, near, arrays, rows, flops, mib=32):
     like = jax.ShapeDtypeStruct((2, 4, rows, LANES), jnp.bfloat16)
-    whole = pl.BlockSpec(memory_space=pltpu.VMEM)
     return pl.pallas_call(
         kernel,
-        in_specs=[pl.BlockSpec(memory_space=pltpu.SMEM)] + [whole] * len(arrays),
-        out_specs=(whole, whole),
+        grid=(1,),
+        in_specs=[pl.BlockSpec(memory_space=pltpu.SMEM)] + [at_once(a.shape) for a in arrays],
+        out_specs=(at_once(like.shape),) * 2,
         out_shape=(like, like),
-        compiler_params=vmem(32),
+        compiler_params=vmem(mib),
         cost_estimate=cost(flops, sum(2 * a.size for a in arrays), 0),
     )(near, *arrays)
 
@@ -584,7 +583,7 @@
     width = sum(right.shape[1] for right in rights)
     rows = width // LANES * HALF + edges[0].shape[2]
     kernel = functools.partial(qkv_grad_kernel, len(rights))
-    return whole_grad(kernel, near, [left, *rights, *edges], rows, 2 * left.shape[0] * D * width)
+    return whole_grad(kernel, near, [left, *rights, *edges], rows, 2 * left.shape[0] * D * width, 60)
 
 
 def project_kernel(nb, near_ref, tokens_ref, *refs):
@@ -609,20 +608,61 @@
 
 def project(near, tokens, pieces, nb):
     count = tokens.shape[0]
-    whole = pl.BlockSpec(memory_space=pltpu.VMEM)
+    out_shape = (
+        jax.ShapeDtypeStruct((D, nb * LANES), jnp.bfloat16),
+        jax.ShapeDtypeStruct((count, nb * LANES), jnp.bfloat16),
+        jax.ShapeDtypeStruct((8, D), jnp.float32),
+        jax.ShapeDtypeStruct((1, 4 * D), jnp.float32),
+    )
     return pl.pallas_call(
         functools.partial(project_kernel, nb),
-        out_shape=(
-            jax.ShapeDtypeStruct((D, nb * LANES), jnp.bfloat16),
-            jax.ShapeDtypeStruct((count, nb * LANES), jnp.bfloat16),
-            jax.ShapeDtypeStruct((8, D), jnp.float32),
-            jax.ShapeDtypeStruct((1, 4 * D), jnp.float32),
-        ),
-        in_specs=[pl.BlockSpec(memory_space=pltpu.SMEM)] + [whole] * (1 + len(pieces)),
-        out_specs=(whole,) * 4,
+        grid=(1,),
+        out_shape=out_shape,
+        in_specs=[pl.BlockSpec(memory_space=pltpu.SMEM)]
+        + [at_once(a.shape) for a in (tokens, *pieces)],
+        out_specs=tuple(at_once(like.shape) for like in out_shape),
         compiler_params=vmem(32),
         cost_estimate=cost(2 * count * D * nb * LANES, 6 * count * D),
     )(near, tokens, *pieces)
+
+
+def last_kernel(near_ref, *refs):
+    qkv_ref, out_ref, vec_ref, b_ref = refs[-4:]
+    c = near_ref[3]
+    first_pair = 0
+    for total, x, core, both in (refs[:4], refs[4:8]):
+        mine, theirs = wide(total[...]) + wide(x[...]), wide(core[...]) + wide(both[...])
+        parts = jnp.where(c == 0, mine, theirs), jnp.where(c == 0, theirs, mine)
+        for at, part in enumerate(parts):
+            rows = slice(at * HALF, (at + 1) * HALF)
+            for j in range(3):
+                for kind in range(3):
+                    col = kind * D + (first_pair + j) * 128
+                    qkv_ref[rows, col : col + 128] = part[
+                        j * HALF : (j + 1) * HALF, kind * 128 : (kind + 1) * 128
+                    ]
+            if first_pair == 0:
+                for j in range(2):
+                    out_ref[rows, j * LANES : (j + 1) * LANES] = part[(3 + j) * HALF : (4 + j) * HALF]
+            elif at == 0:
+                vec_ref[...] = part[3 * HALF : 3 * HALF + 8, :ROWS]
+            else:
+                b_ref[...] = part[3 * HALF : 3 * HALF + 1]
+        first_pair += 3
+
+
+def last_sums(near, lo_sum, hi_sum):
+    arrays = [lo_sum.total, *lo_sum.others, hi_sum.total, *hi_sum.others]
+    shapes = [(ROWS, 3 * D), (ROWS, D), (8, ROWS), (1, LANES)]
+    return pl.pallas_call(
+        last_kernel,
+        grid=(1,),
+        in_specs=[pl.BlockSpec(memory_space=pltpu.SMEM)] + [at_once(a.shape) for a in arrays],
+        out_specs=tuple(at_once(shape) for shape in shapes),
+        out_shape=tuple(jax.ShapeDtypeStruct(shape, jnp.float32) for shape in shapes),
+        compiler_params=vmem(16),
+        cost_estimate=cost(0, 10 * ROWS * 3 * D),
+    )(near, *arrays)
 
 
 def pairs_of(rows):
@@ -683,23 +723,26 @@
         [
             to_blocks(w_in, place, True).reshape(-1, LANES),
             to_blocks(w_attn_out, place, True).reshape(-1, LANES),
-            to_blocks(w_down, place, down=True).reshape(-1, LANES),
         ]
     )
     own = after(own, qkv)
     came = turned(own)
+    own_down = to_blocks(w_down, place, down=True).reshape(-1, LANES)
     w_qkv_full, projected, vector_wide, b_full = project(
-        near, after(tokens, came[0], came[2]), qkv_pieces, HEADS // 2
-    )
-    context_lo, total_lo = attention_forward(projected, doc_columns, 0)
-    both = [own, came[0], after(came[1], context_lo), came[2]]
-    rest = [jnp.stack([rows[: 5 * HALF] for rows in both])]
-    down = jnp.stack([rows[5 * HALF :] for rows in both])
-    rest += [swap_y(rest[0]), swap_x(rest[0])]
-    context_hi, total_hi = attention_forward(after(projected, context_lo, rest[0], down), doc_columns, 3)
-    rest[1:] = after(rest[1:], context_hi)
-    down_y = swap_y(after(down, rest[1]))
-    rest.append(swap_x(rest[1]))
+        near, after(tokens, came, own_down), qkv_pieces, HEADS // 2
+    )
+    rest = [jnp.stack([own, *came])]
+    own_down = after(own_down, came)
+    came_down = turned(own_down)
+    context_lo, total_lo = attention_forward(after(projected, rest[0]), doc_columns, 0)
+    rest += after([swap_y(rest[0]), swap_x(rest[0])], context_lo)
+    context_hi, total_hi = attention_forward(
+        after(projected, context_lo, rest[1], rest[2]), doc_columns, 3
+    )
+    rest.append(after(swap_x(rest[1]), context_hi))
+    came_down = after(came_down, context_hi)
+    down = jnp.stack([own_down, *came_down])
+    down_y = swap_y(down)
     rest += [swap_core(piece) for piece in rest]
     in_full, out_full = put_together(rest_kernel, near, rest, [(D, 4 * D), (D, D)])
     context = jnp.concatenate([context_lo, context_hi], axis=1)
@@ -792,22 +835,16 @@
     lo_sum.send_last()
     hi_sum.from_z = after(hi_sum.from_z, lo_sum.total, in_sum.total)
     hi_sum.send_last()
-    in_part, down_part, lo_part, hi_part = (
-        total.finish() for total in (in_sum, down_sum, lo_sum, hi_sum)
-    )
-    qkv_shard = jnp.concatenate(
-        [from_blocks(lo_part[:, : 3 * HALF], 3), from_blocks(hi_part[:, : 3 * HALF], 3)], axis=1
-    )
-    small = hi_part[:, 3 * HALF :]
+    qkv_shard, out_shard, vector_shard, bias_shard = last_sums(near, lo_sum, hi_sum)
     return (
         layer_out,
         grad_tokens,
-        of_pairs(qkv_shard),
-        small[0, :8, :ROWS],
-        from_blocks(lo_part[:, 3 * HALF :], 2),
-        from_blocks(in_part, 8),
-        small[1, 0],
-        from_blocks(down_part, 8, True),
+        qkv_shard,
+        vector_shard,
+        out_shard,
+        from_blocks(in_sum.finish(), 8),
+        bias_shard.reshape(-1),
+        from_blocks(down_sum.finish(), 8, True),
     )
 
 

time: 373 us -> 353 us (0.946)
  local copies, waits for them, and re-layouts: 42.1 us -> 30.4 us
  waiting for transfers between devices: 89.6 us -> 81.9 us
  starting transfers between devices: 55.6 us -> 50.6 us
  Pallas kernels: 127 us -> 131 us
    ppermute x5, waiting for transfers between devices: 17.2 us -> 4.06 us  [swap_x(): return lax.ppermute(rows, 'rep', [(i, i ^ 2) for i in range(4)])]
    unnamed x133 -> x126, local copies, waits for them, and re-layouts: 28.1 us -> 17.2 us
    pallas_call x5 -> x6, Pallas kernels: 18 us -> 22.9 us  [the longest x2 10.9 us: whole_grad(): pl.pallas_call(kernel, grid=(1,), in_specs=[pl.BlockSpec(memory_space=plt...]
    ppermute x14, starting transfers between devices: 17.3 us -> 13.3 us  [swap_core(): return lax.ppermute(rows, 'rep', [(i, i ^ 1) for i in range(4)])]
    ppermute x18 -> x21, waiting for transfers between devices: 38 us -> 39.8 us  [turn_z(): lax.ppermute(rows, 'fsdp', [(i, (i + 2 * step) % 8) for i in range(8)])]
    ppermute x18 -> x21, starting transfers between devices: 21.4 us -> 20.4 us  [turn_z(): lax.ppermute(rows, 'fsdp', [(i, (i + 2 * step) % 8) for i in range(8)])]
  transfers between devices with their start and end apart: 50 -> 53, of which waited for: 16 -> 18; matrix products, arithmetic and copies ran while one was open for 14% -> 15% of each run, Pallas kernels for 25% -> 28%
where the time goes in v3:
time: 353 us; the launch traced here: 349 us
  Pallas kernels  131 us (37%)
  waiting for transfers between devices  81.9 us (23%)
  starting transfers between devices  50.6 us (14%)
  other arithmetic  38 us (11%)
  local copies, waits for them, and re-layouts  30.4 us (9%)
  matrix products  13.4 us (4%)
    ppermute x21, waiting for transfers between devices, turn_z(): lax.ppermute(rows, 'fsdp', [(i, (i + 2 * step) % 8) for i in range(8)])  39.8 us
    pallas_call x5, Pallas kernels, attention_backward(): pl.pallas_call(attend_back_kernel, grid=(pairs,), out_shape=(jax.ShapeDty...  38.6 us
    pallas_call x2, Pallas kernels, attention_forward(): pl.pallas_call(attend_kernel, grid=(pairs,), out_shape=(jax.ShapeDtypeStr...  30.6 us
    ppermute x7, waiting for transfers between devices, swap_y(): return lax.ppermute(rows, 'fsdp', [(i, i ^ 1) for i in range(8)])  29.7 us
    pallas_call x1, Pallas kernels, feed_backward(): pl.pallas_call(feed_back_kernel, grid=(units // tile,), in_specs=[pl.Bloc...  27.2 us
    ppermute x21, starting transfers between devices, turn_z(): lax.ppermute(rows, 'fsdp', [(i, (i + 2 * step) % 8) for i in range(8)])  20.4 us
    unnamed x126, local copies, waits for them, and re-layouts  17.2 us
    dot_general x4, matrix products, wide_dot(): lax.dot_general(left, right, dims, preferred_element_type=jnp.float32)  13.4 us
  transfers between devices with their start and end apart: 53, of which 18 were waited for; matrix products, arithmetic and copies ran while one was open for 15% of the time, Pallas kernels for 28%

profile of v3, /device:TPU:25, one launch (start us, length us, event | category | flops | bytes accessed | tf_op | source)
XLA Modules:
  0.0 348.6 jit_solution(10098624290391153639)
XLA Ops:
  0.7 1.6 reshape.248
  4.9 5.4 %collective-permute-done = bf16[320,384]{1,0:T(8,128)(2,1)S(1)} collective-permute-done((bf16[320,384]{1,0:T(8,128)(2,1)S(1)}, bf16[320,384]{1,0:T(8,128)(2,1)S(1)}, u32[]{:S(2)}, u32[]{:S(2)}) %collective-permute-start) | collective-permute-done | bytes 245792 | tf_op jit(solution)/shard_map/ppermute | solution.py:103
  10.3 15.5 %collective-permute-done.1 = bf16[320,384]{1,0:T(8,128)(2,1)S(1)} collective-permute-done((bf16[320,384]{1,0:T(8,128)(2,1)S(1)}, bf16[320,384]{1,0:T(8,128)(2,1)S(1)}, u32[]{:S(2)}, u32[]{:S(2)}) %collective-permute-start.1) | collective-permute-done | bytes 245792 | tf_op jit(solution)/shard_map/ppermute | solution.py:103
  28.5 2.2 collective-permute-start.4
  30.7 1.7 collective-permute-start.5
  32.3 1.6 collective-permute-start.7
  33.9 14.0 %collective-permute-done.6.refs_1_ = bf16[4,320,384]{2,1,0:T(8,128)(2,1)} collective-permute-done((bf16[4,320,384]{2,1,0:T(8,128)(2,1)S(1)}, bf16[4,320,384]{2,1,0:T(8,128)(2,1)}, u32[]{:S(2)}, u32[]{:S(2)}) %collective-permute-start.6) | collective-permute-done | bytes 983072 | tf_op jit(solution)/shard_map/ppermute | solution.py:99
  47.9 2.5 collective-permute-start.8
  56.0 2.5 reshape.250
  60.1 7.2 %shard_map.152 = (bf16[768,2304]{1,0:T(8,128)(2,1)S(1)}, bf16[1024,2304]{1,0:T(8,128)(2,1)S(1)}, f32[8,768]{1,0:T(8,128)S(1)}, f32[1,3072]{1,0:T(1,128)S(1)}) custom-call(s32[4]{0:T(128)S(1)} %pad_add_fusion.near_ref, bf16[1024,768]{1,0:T(8,128)(2,1)S(1)} %copy-done.4, bf16[4,320,384]{2,1,0:T(8,128)(2,1)S(1)} %pad_maximum_fusion.2.refs_0_, ...), custom_call_target="tpu_custom_call" | custom-call | flops 452984832 | bytes 589824 | tf_op jit(solution)/shard_map/pallas_call | solution.py:617
  67.3 1.9 copy-done.27
  69.2 15.3 %shard_map.153 = (bf16[1024,384]{1,0:T(8,128)(2,1)S(1)}, f32[3,2,1024]{2,1,0:T(2,128)S(1)}) custom-call(bf16[1024,2304]{1,0:T(8,128)(2,1)S(1)} %get-tuple-element.93.qkv_ref, bf16[1024,128]{1,0:T(8,128)(2,1)S(1)} %select_convert_fusion.1.qx_ref, bf16[1024,128]{1,0:T(8,128)(2,1)S(1)} %fusion.9.kx_ref), custom_call_target="tpu_custom_call" | custom-call | flops 805306368 | bytes 393216 | tf_op jit(solution)/shard_map/pallas_call | solution.py:297
  84.9 2.1 collective-permute-start.17
  87.0 2.0 collective-permute-start.18
  88.9 1.7 collective-permute-start.12
  90.6 15.3 %shard_map.154 = (bf16[1024,384]{1,0:T(8,128)(2,1)S(1)}, f32[3,2,1024]{2,1,0:T(2,128)S(1)}) custom-call(bf16[1024,2304]{1,0:T(8,128)(2,1)S(1)} %get-tuple-element.93.qkv_ref, bf16[1024,128]{1,0:T(8,128)(2,1)S(1)} %select_convert_fusion.1.qx_ref, bf16[1024,128]{1,0:T(8,128)(2,1)S(1)} %fusion.9.kx_ref), custom_call_target="tpu_custom_call" | custom-call | flops 805306368 | bytes 393216 | tf_op jit(solution)/shard_map/pallas_call | solution.py:297
  106.5 5.9 %collective-permute-done.17 = bf16[384,384]{1,0:T(8,128)(2,1)S(1)} collective-permute-done((bf16[384,384]{1,0:T(8,128)(2,1)S(1)}, bf16[384,384]{1,0:T(8,128)(2,1)S(1)}, u32[]{:S(2)}, u32[]{:S(2)}) %collective-permute-start.17) | collective-permute-done | bytes 294944 | tf_op jit(solution)/shard_map/ppermute | solution.py:103
  115.7 2.1 shard_map.155
  117.9 1.6 fusion.38
  120.6 11.5 %shard_map.156 = (bf16[1024,3072]{1,0:T(8,128)(2,1)S(1)}, bf16[1024,3072]{1,0:T(8,128)(2,1)S(1)}) custom-call(bf16[1024,768]{1,0:T(8,128)(2,1)S(1)} %fusion.3.x_ref.low_ref, bf16[768,3072]{1,0:T(8,128)(2,1)S(1)} %get-tuple-element.98.w_ref.in_ref, f32[1,3072]{1,0:T(1,128)S(1)} %get-tuple-element.99.b_ref), custom_call_target="tpu_custom_call" | custom-call | flops 603979776 | bytes 1572864 | tf_op jit(solution)/shard_map/pallas_call | solution.py:407
  132.1 2.7 copy-done.11
  134.8 6.9 %collective-permute-done.19.refs_1_ = bf16[4,384,384]{2,1,0:T(8,128)(2,1)S(1)} collective-permute-done((bf16[4,384,384]{2,1,0:T(8,128)(2,1)S(1)}, bf16[4,384,384]{2,1,0:T(8,128)(2,1)S(1)}, u32[]{:S(2)}, u32[]{:S(2)}) %collective-permute-start.19) | collective-permute-done | bytes 1179680 | tf_op jit(solution)/shard_map/ppermute | solution.py:99
  143.2 1.8 collective-permute-done.21.refs_3_
  146.0 5.4 %fusion.37 = (f32[1024]{0:T(1024)S(1)}, f32[1024,768]{1,0:T(8,128)S(1)}) fusion(f32[768]{0:T(1024)S(1)} %get-tuple-element.174, f32[768]{0:T(1024)S(1)} %get-tuple-element.175, f32[768]{0:T(1024)S(1)} %get-tuple-element.176, f32[1024]{0:T(1024)S(1)} %add_rsqrt_fusion.1, f32[1024,768]{1,0:T(8,128)S(1)} %get-tuple-element.187, ...), kind=kOutput, calls=%fused_computation.136 | convolution fusion | flops 4837342208 | bytes 17323008 | tf_op jit(solution)/shard_map/dot_general | solution.py:27
  152.0 2.0 copy-done.34
  154.0 1.9 multiply_reduce_fusion
  155.9 1.5 fusion.33
  157.4 27.2 %shard_map.158 = (f32[1024,768]{1,0:T(8,128)}, f32[1,3072]{1,0:T(1,128)S(1)}, bf16[2,4,384,384]{3,2,1,0:T(8,128)(2,1)}, bf16[2,4,384,384]{3,2,1,0:T(8,128)(2,1)}...) custom-call(s32[4]{0:T(128)S(1)} %pad_add_fusion.near_ref, ...), custom_call_target="tpu_custom_call" | custom-call | flops 2415919104 | bytes 3145728 | tf_op jit(solution)/shard_map/pallas_call | solution.py:505
  185.1 7.2 %multiply_reduce_fusion.1 = (bf16[768]{0:T(1024)(128)(2,1)S(1)}, f32[1024]{0:T(1024)S(1)}, f32[1024]{0:T(1024)S(1)}, bf16[768]{0:T(1024)(128)(2,1)S(1)}, f32[1024,768]{1,0:T(8,128)S(1)}, /*index=5*/bf16[1024,768]{1,0:T(8,128)(2,1)}) fusion(f32[1024,768]{1,0:T(8,128)} %copy-done.31, f32[1024]{0:T(1024)S(1)} %add_rsqrt_fusion.1, ...), kind=kLoop, calls=%fused_computation.2 | loop fusion | flops 18084352 | bytes 15774720 | tf_op jit(solution)/shard_map/reduce_sum | solution.py:74
  192.3 1.7 fusion.4
  194.5 2.3 fusion.35
  196.8 1.4 convolution_convert_fusion.do_ref
  198.9 1.6 add_convert_fusion.2
  202.1 13.3 %shard_map.159 = (bf16[1024,768]{1,0:T(8,128)(2,1)S(1)}, f32[2,256]{1,0:T(2,128)S(1)}) custom-call(bf16[1024,2304]{1,0:T(8,128)(2,1)S(1)} %bitcast.122, bf16[1024,768]{1,0:T(8,128)(2,1)S(1)} %convolution_convert_fusion.do_ref, bf16[1024,384]{1,0:T(8,128)(2,1)S(1)} %copy-done.7, f32[3,2,1024]{2,1,0:T(2,128)S(1)} %get-tuple-element.113.lse_ref, ...), custom_call_target="tpu_custom_call" | custom-call | flops 1342177280 | bytes 589824 | tf_op jit(solution)/shard_map/pallas_call | solution.py:365
  215.4 2.0 dynamic-slice_convert_fusion
  217.4 3.9 %collective-permute-done.24 = bf16[4,384,384]{2,1,0:T(8,128)(2,1)S(1)} collective-permute-done((bf16[4,384,384]{2,1,0:T(8,128)(2,1)S(1)}, bf16[4,384,384]{2,1,0:T(8,128)(2,1)S(1)}, u32[]{:S(2)}, u32[]{:S(2)}) %collective-permute-start.24) | collective-permute-done | bytes 1179680 | tf_op jit(solution)/shard_map/ppermute | solution.py:99
  221.3 1.7 bitcast_add_fusion
  224.6 6.3 %shard_map.160 = (bf16[1024,384]{1,0:T(8,128)(2,1)S(1)}, f32[2,128]{1,0:T(2,128)S(1)}) custom-call(bf16[1024,2304]{1,0:T(8,128)(2,1)S(1)} %bitcast.122, bf16[1024,768]{1,0:T(8,128)(2,1)S(1)} %convolution_convert_fusion.do_ref, bf16[1024,384]{1,0:T(8,128)(2,1)S(1)} %copy-done.7, f32[3,2,1024]{2,1,0:T(2,128)S(1)} %get-tuple-element.113.lse_ref, ...), custom_call_target="tpu_custom_call" | custom-call | flops 671088640 | bytes 294912 | tf_op jit(solution)/shard_map/pallas_call | solution.py:365
  233.7 5.2 %shard_map.161 = (bf16[2,4,240,384]{3,2,1,0:T(8,128)(2,1)}, bf16[2,4,240,384]{3,2,1,0:T(8,128)(2,1)S(1)}) custom-call(s32[4]{0:T(128)S(1)} %pad_add_fusion.near_ref, bf16[1024,768]{1,0:T(8,128)(2,1)S(1)} %copy-done.5, bf16[1024,1152]{1,0:T(8,128)(2,1)S(1)} %pad_maximum_fusion.right_ref, bf16[1024,768]{1,0:T(8,128)(2,1)S(1)} %copy-done.13, ...), custom_call_target="tpu_custom_call" | custom-call | flops 377487360 | bytes 884736 | tf_op jit(solution)/shard_map/pallas_call | solution.py:565
  244.0 1.6 collective-permute-start.30
  245.6 2.3 copy-done.1
  247.9 6.3 %shard_map.162 = (bf16[1024,384]{1,0:T(8,128)(2,1)S(1)}, f32[2,128]{1,0:T(2,128)S(1)}) custom-call(bf16[1024,2304]{1,0:T(8,128)(2,1)S(1)} %copy-done.1, bf16[1024,768]{1,0:T(8,128)(2,1)S(1)} %convolution_convert_fusion.do_ref, bf16[1024,384]{1,0:T(8,128)(2,1)S(1)} %get-tuple-element.94.ctx_ref, f32[3,2,1024]{2,1,0:T(2,128)S(1)} %get-tuple-element.122.lse_ref, ...), custom_call_target="tpu_custom_call" | custom-call | flops 671088640 | bytes 294912 | tf_op jit(solution)/shard_map/pallas_call | solution.py:365
  255.4 2.9 collective-permute-done.27
  258.6 2.7 fusion.5
  262.3 6.5 %shard_map.163 = (bf16[1024,384]{1,0:T(8,128)(2,1)S(1)}, f32[2,128]{1,0:T(2,128)S(1)}) custom-call(bf16[1024,2304]{1,0:T(8,128)(2,1)S(1)} %copy-done.1, bf16[1024,768]{1,0:T(8,128)(2,1)S(1)} %convolution_convert_fusion.do_ref, bf16[1024,384]{1,0:T(8,128)(2,1)S(1)} %get-tuple-element.94.ctx_ref, f32[3,2,1024]{2,1,0:T(2,128)S(1)} %get-tuple-element.122.lse_ref, ...), custom_call_target="tpu_custom_call" | custom-call | flops 671088640 | bytes 294912 | tf_op jit(solution)/shard_map/pallas_call | solution.py:365
  271.3 6.3 %shard_map.164 = (bf16[1024,384]{1,0:T(8,128)(2,1)S(1)}, f32[2,128]{1,0:T(2,128)S(1)}) custom-call(bf16[1024,2304]{1,0:T(8,128)(2,1)S(1)} %copy-done.1, bf16[1024,768]{1,0:T(8,128)(2,1)S(1)} %convolution_convert_fusion.do_ref, bf16[1024,384]{1,0:T(8,128)(2,1)S(1)} %get-tuple-element.94.ctx_ref, f32[3,2,1024]{2,1,0:T(2,128)S(1)} %get-tuple-element.122.lse_ref, ...), custom_call_target="tpu_custom_call" | custom-call | flops 671088640 | bytes 294912 | tf_op jit(solution)/shard_map/pallas_call | solution.py:365
  281.0 5.7 %shard_map.165 = (bf16[2,4,160,384]{3,2,1,0:T(8,128)(2,1)}, bf16[2,4,160,384]{3,2,1,0:T(8,128)(2,1)}) custom-call(s32[4]{0:T(128)} %copy-done.25, bf16[1024,768]{1,0:T(8,128)(2,1)} %refs_0_.1, bf16[1024,384]{1,0:T(8,128)(2,1)} %copy-done.16, bf16[1024,384]{1,0:T(8,128)(2,1)} %copy-done.18, bf16[1024,384]{1,0:T(8,128)(2,1)} %copy-done.20, ...), custom_call_target="tpu_custom_call" | custom-call | flops 226492416 | bytes 516096 | tf_op jit(solution)/shard_map/pallas_call | solution.py:565
  289.5 2.8 collective-permute-start.32
  292.6 4.0 %collective-permute-done.35 = bf16[384,384]{1,0:T(8,128)(2,1)S(1)} collective-permute-done((bf16[384,384]{1,0:T(8,128)(2,1)S(1)}, bf16[384,384]{1,0:T(8,128)(2,1)S(1)}, u32[]{:S(2)}, u32[]{:S(2)}) %collective-permute-start.35) | collective-permute-done | bytes 294944 | tf_op jit(solution)/shard_map/ppermute | solution.py:95
  297.4 1.8 bitcast_add_fusion.1
  299.2 2.6 collective-permute-start.37
  303.0 2.5 collective-permute-done.32
  306.8 1.9 collective-permute-start.52
  309.7 5.0 %add_convert_fusion = bf16[1024,768]{1,0:T(8,128)(2,1)} fusion(f32[1024,768]{1,0:T(8,128)S(1)} %copy-done.40, bf16[1024,2304]{1,0:T(8,128)(2,1)S(1)} %constant_dynamic-update-slice_fusion.2, bf16[768,2304]{1,0:T(8,128)(2,1)S(1)} %copy-done.28), kind=kOutput, calls=%fused_computation | convolution fusion | flops 3625451520 | bytes 12976128 | tf_op jit(solution)/shard_map/dot_general | solution.py:27
  314.7 2.0 collective-permute-done.41
  316.9 1.5 collective-permute-start.45
  318.4 2.9 collective-permute-done.38
  322.0 1.5 collective-permute-start.42
  323.6 2.1 collective-permute-start.43
  325.7 6.4 %collective-permute-done.46 = bf16[160,384]{1,0:T(8,128)(2,1)S(1)} collective-permute-done((bf16[160,384]{1,0:T(8,128)(2,1)S(1)}, bf16[160,384]{1,0:T(8,128)(2,1)S(1)}, u32[]{:S(2)}, u32[]{:S(2)}) %collective-permute-start.46) | collective-permute-done | bytes 122912 | tf_op jit(solution)/shard_map/ppermute | solution.py:103
  332.1 1.9 collective-permute-start.44
  339.1 3.0 collective-permute-done.48.refs_5_
  342.1 2.3 collective-permute-done.50.refs_7_
  344.4 1.7 shard_map.166
  (285 shorter events, 55.9 us)
Async XLA Ops:
  0.7 26.7 %copy-start.47 = (bf16[96,3072]{1,0:T(8,128)(2,1)S(1)}, bf16[96,3072]{1,0:T(8,128)(2,1)}, u32[]{:S(2)}) copy-start(bf16[96,3072]{1,0:T(8,128)(2,1)} %param.14) | copy-start | bytes 1769476
  2.5 25.1 %copy-start.48 = (bf16[96,768]{1,0:T(8,128)(2,1)S(1)}, bf16[96,768]{1,0:T(8,128)(2,1)}, u32[]{:S(2)}) copy-start(bf16[96,768]{1,0:T(8,128)(2,1)} %param.13) | copy-start | bytes 442372
  2.5 25.3 %copy-start.54 = (s32[1,2]{1,0:T(1,128)S(1)}, s32[1,2]{1,0:T(1,128)}, u32[]{:S(2)}) copy-start(s32[1,2]{1,0:T(1,128)} %param.10) | copy-start | bytes 28
  3.4 6.9 %collective-permute-start = (bf16[320,384]{1,0:T(8,128)(2,1)S(1)}, bf16[320,384]{1,0:T(8,128)(2,1)S(1)}, u32[]{:S(2)}, u32[]{:S(2)}) collective-permute-start(bf16[320,384]{1,0:T(8,128)(2,1)S(1)} %get-tuple-element.202), channel_id=1, source_target_pairs={{0,8},{4,12},{8,16},{12,20},{16,24},{20,28},{24,0},{28,4},{1,9},{5... | collective-permute-start | bytes 737288 | tf_op jit(solution)/shard_map/ppermute | solution.py:103
  3.4 22.4 %collective-permute-start.1 = (bf16[320,384]{1,0:T(8,128)(2,1)S(1)}, bf16[320,384]{1,0:T(8,128)(2,1)S(1)}, u32[]{:S(2)}, u32[]{:S(2)}) collective-permute-start(bf16[320,384]{1,0:T(8,128)(2,1)S(1)} %get-tuple-element.202), channel_id=1, source_target_pairs={{0,16},{4,20},{8,24},{12,28},{16,0},{20,4},{24,8},{28,12},{1,17},{... | collective-permute-start | bytes 737288 | tf_op jit(solution)/shard_map/ppermute | solution.py:103
  4.7 21.2 %collective-permute-start.2 = (bf16[320,384]{1,0:T(8,128)(2,1)S(1)}, bf16[320,384]{1,0:T(8,128)(2,1)S(1)}, u32[]{:S(2)}, u32[]{:S(2)}) collective-permute-start(bf16[320,384]{1,0:T(8,128)(2,1)S(1)} %get-tuple-element.202), channel_id=1, source_target_pairs={{0,24},{4,28},{8,0},{12,4},{16,8},{20,12},{24,16},{28,20},{1,25},{... | collective-permute-start | bytes 737288 | tf_op jit(solution)/shard_map/ppermute | solution.py:103
  26.0 21.9 %collective-permute-start.6 = (bf16[4,320,384]{2,1,0:T(8,128)(2,1)S(1)}, bf16[4,320,384]{2,1,0:T(8,128)(2,1)}, u32[]{:S(2)}, u32[]{:S(2)}) collective-permute-start(bf16[4,320,384]{2,1,0:T(8,128)(2,1)S(1)} %pad_maximum_fusion.2.refs_0_), channel_id=1, source_target_pairs={{0,4},{4,0},{8,12},{12,8},{16,20},{20,16},{24,28},{28,24},{1,5},{5... | collective-permute-start | bytes 2949128 | tf_op jit(solution)/shard_map/ppermute | solution.py:99
  27.6 32.5 %copy-start.4 = (bf16[1024,768]{1,0:T(8,128)(2,1)S(1)}, bf16[1024,768]{1,0:T(8,128)(2,1)}, u32[]{:S(2)}) copy-start(bf16[1024,768]{1,0:T(8,128)(2,1)} %refs_0_.1) | copy-start | bytes 4718596
  28.4 23.9 %collective-permute-start.3 = (bf16[240,384]{1,0:T(8,128)(2,1)S(1)}, bf16[240,384]{1,0:T(8,128)(2,1)S(1)}, u32[]{:S(2)}, u32[]{:S(2)}) collective-permute-start(bf16[240,384]{1,0:T(8,128)(2,1)S(1)} %pad_maximum_fusion.5), channel_id=1, source_target_pairs={{0,8},{4,12},{8,16},{12,20},{16,24},{20,28},{24,0},{28,4},{1,9},{5... | collective-permute-start | bytes 552968 | tf_op jit(solution)/shard_map/ppermute | solution.py:103
  28.5 23.9 %collective-permute-start.4 = (bf16[240,384]{1,0:T(8,128)(2,1)S(1)}, bf16[240,384]{1,0:T(8,128)(2,1)S(1)}, u32[]{:S(2)}, u32[]{:S(2)}) collective-permute-start(bf16[240,384]{1,0:T(8,128)(2,1)S(1)} %pad_maximum_fusion.5), channel_id=1, source_target_pairs={{0,16},{4,20},{8,24},{12,28},{16,0},{20,4},{24,8},{28,12},{1,17},{... | collective-permute-start | bytes 552968 | tf_op jit(solution)/shard_map/ppermute | solution.py:103
  30.7 21.7 %collective-permute-start.5 = (bf16[240,384]{1,0:T(8,128)(2,1)S(1)}, bf16[240,384]{1,0:T(8,128)(2,1)S(1)}, u32[]{:S(2)}, u32[]{:S(2)}) collective-permute-start(bf16[240,384]{1,0:T(8,128)(2,1)S(1)} %pad_maximum_fusion.5), channel_id=1, source_target_pairs={{0,24},{4,28},{8,0},{12,4},{16,8},{20,12},{24,16},{28,20},{1,25},{... | collective-permute-start | bytes 552968 | tf_op jit(solution)/shard_map/ppermute | solution.py:103
  32.3 27.8 %collective-permute-start.7 = (bf16[4,320,384]{2,1,0:T(8,128)(2,1)S(1)}, bf16[4,320,384]{2,1,0:T(8,128)(2,1)}, u32[]{:S(2)}, u32[]{:S(2)}) collective-permute-start(bf16[4,320,384]{2,1,0:T(8,128)(2,1)S(1)} %pad_maximum_fusion.2.refs_0_), channel_id=1, source_target_pairs={{0,1},{1,0},{2,3},{3,2},{4,5},{5,4},{6,7},{7,6},{8,9},{9,8},{10,11... | collective-permute-start | bytes 2949128 | tf_op jit(solution)/shard_map/ppermute | solution.py:91
  47.9 12.2 %collective-permute-start.8 = (bf16[4,320,384]{2,1,0:T(8,128)(2,1)}, bf16[4,320,384]{2,1,0:T(8,128)(2,1)}, u32[]{:S(2)}, u32[]{:S(2)}) collective-permute-start(bf16[4,320,384]{2,1,0:T(8,128)(2,1)} %collective-permute-done.6.refs_1_), channel_id=1, source_target_pairs={{0,1},{1,0},{2,3},{3,2},{4,5},{5,4},{6,7},{7,6},{8,9},{9,8},{10,11... | collective-permute-start | bytes 2949128 | tf_op jit(solution)/shard_map/ppermute | solution.py:91
  53.4 31.1 %collective-permute-start.10 = (bf16[4,240,384]{2,1,0:T(8,128)(2,1)}, bf16[4,240,384]{2,1,0:T(8,128)(2,1)}, u32[]{:S(2)}, u32[]{:S(2)}) collective-permute-start(bf16[4,240,384]{2,1,0:T(8,128)(2,1)} %pad_maximum_fusion.3.refs_0_), channel_id=1, source_target_pairs={{0,2},{1,3},{2,0},{3,1},{4,6},{5,7},{6,4},{7,5},{8,10},{9,11},{10,... | collective-permute-start | bytes 2211848 | tf_op jit(solution)/shard_map/ppermute | solution.py:95
  54.6 29.9 %collective-permute-start.9 = (bf16[4,240,384]{2,1,0:T(8,128)(2,1)}, bf16[4,240,384]{2,1,0:T(8,128)(2,1)}, u32[]{:S(2)}, u32[]{:S(2)}) collective-permute-start(bf16[4,240,384]{2,1,0:T(8,128)(2,1)} %pad_maximum_fusion.3.refs_0_), channel_id=1, source_target_pairs={{0,4},{4,0},{8,12},{12,8},{16,20},{20,16},{24,28},{28,24},{1,5},{5... | collective-permute-start | bytes 2211848 | tf_op jit(solution)/shard_map/ppermute | solution.py:99
  56.0 176.8 %copy-start.25 = (s32[4]{0:T(128)}, s32[4]{0:T(128)S(1)}, u32[]{:S(2)}) copy-start(s32[4]{0:T(128)S(1)} %pad_add_fusion.near_ref) | copy-start | bytes 52
  69.2 36.8 %copy-start = (bf16[1024,2304]{1,0:T(8,128)(2,1)}, bf16[1024,2304]{1,0:T(8,128)(2,1)S(1)}, u32[]{:S(2)}) copy-start(bf16[1024,2304]{1,0:T(8,128)(2,1)S(1)} %get-tuple-element.93.qkv_ref) | copy-start | bytes 14155780
  84.5 29.9 %copy-start.6 = (bf16[1024,384]{1,0:T(8,128)(2,1)}, bf16[1024,384]{1,0:T(8,128)(2,1)S(1)}, u32[]{:S(2)}) copy-start(bf16[1024,384]{1,0:T(8,128)(2,1)S(1)} %get-tuple-element.90.ctx_ref) | copy-start | bytes 2359300
  84.5 21.4 %collective-permute-start.11 = (bf16[4,240,384]{2,1,0:T(8,128)(2,1)}, bf16[4,240,384]{2,1,0:T(8,128)(2,1)S(1)}, u32[]{:S(2)}, u32[]{:S(2)}) collective-permute-start(bf16[4,240,384]{2,1,0:T(8,128)(2,1)} %collective-permute-done.9.refs_1_), channel_id=1, source_target_pairs={{0,2},{1,3},{2,0},{3,1},{4,6},{5,7},{6,4},{7,5},{8,10},{9,11},{10,... | collective-permute-start | bytes 2211848 | tf_op jit(solution)/shard_map/ppermute | solution.py:95
  84.8 21.2 %collective-permute-start.16 = (bf16[384,384]{1,0:T(8,128)(2,1)S(1)}, bf16[384,384]{1,0:T(8,128)(2,1)S(1)}, u32[]{:S(2)}, u32[]{:S(2)}) collective-permute-start(bf16[384,384]{1,0:T(8,128)(2,1)S(1)} %bitcast.129), channel_id=1, source_target_pairs={{0,8},{4,12},{8,16},{12,20},{16,24},{20,28},{24,0},{28,4},{1,9},{5... | collective-permute-start | bytes 884744 | tf_op jit(solution)/shard_map/ppermute | solution.py:103
  84.9 27.6 %collective-permute-start.17 = (bf16[384,384]{1,0:T(8,128)(2,1)S(1)}, bf16[384,384]{1,0:T(8,128)(2,1)S(1)}, u32[]{:S(2)}, u32[]{:S(2)}) collective-permute-start(bf16[384,384]{1,0:T(8,128)(2,1)S(1)} %bitcast.130), channel_id=1, source_target_pairs={{0,16},{4,20},{8,24},{12,28},{16,0},{20,4},{24,8},{28,12},{1,17},{... | collective-permute-start | bytes 884744 | tf_op jit(solution)/shard_map/ppermute | solution.py:103
  87.0 26.9 %collective-permute-start.18 = (bf16[384,384]{1,0:T(8,128)(2,1)S(1)}, bf16[384,384]{1,0:T(8,128)(2,1)S(1)}, u32[]{:S(2)}, u32[]{:S(2)}) collective-permute-start(bf16[384,384]{1,0:T(8,128)(2,1)S(1)} %bitcast.131), channel_id=1, source_target_pairs={{0,24},{4,28},{8,0},{12,4},{16,8},{20,12},{24,16},{28,20},{1,25},{... | collective-permute-start | bytes 884744 | tf_op jit(solution)/shard_map/ppermute | solution.py:103
  88.9 25.8 %collective-permute-start.12 = (bf16[4,240,384]{2,1,0:T(8,128)(2,1)}, bf16[4,240,384]{2,1,0:T(8,128)(2,1)S(1)}, u32[]{:S(2)}, u32[]{:S(2)}) collective-permute-start(bf16[4,240,384]{2,1,0:T(8,128)(2,1)} %pad_maximum_fusion.3.refs_0_), channel_id=1, source_target_pairs={{0,1},{1,0},{2,3},{3,2},{4,5},{5,4},{6,7},{7,6},{8,9},{9,8},{10,11... | collective-permute-start | bytes 2211848 | tf_op jit(solution)/shard_map/ppermute | solution.py:91
  106.0 9.1 %collective-permute-start.13 = (bf16[4,240,384]{2,1,0:T(8,128)(2,1)}, bf16[4,240,384]{2,1,0:T(8,128)(2,1)S(1)}, u32[]{:S(2)}, u32[]{:S(2)}) collective-permute-start(bf16[4,240,384]{2,1,0:T(8,128)(2,1)} %collective-permute-done.9.refs_1_), channel_id=1, source_target_pairs={{0,1},{1,0},{2,3},{3,2},{4,5},{5,4},{6,7},{7,6},{8,9},{9,8},{10,11... | collective-permute-start | bytes 2211848 | tf_op jit(solution)/shard_map/ppermute | solution.py:91
  106.0 9.0 %collective-permute-start.14 = (bf16[4,240,384]{2,1,0:T(8,128)(2,1)}, bf16[4,240,384]{2,1,0:T(8,128)(2,1)S(1)}, u32[]{:S(2)}, u32[]{:S(2)}) collective-permute-start(bf16[4,240,384]{2,1,0:T(8,128)(2,1)} %collective-permute-done.10.refs_2_), channel_id=1, source_target_pairs={{0,1},{1,0},{2,3},{3,2},{4,5},{5,4},{6,7},{7,6},{8,9},{9,8},{10,11... | collective-permute-start | bytes 2211848 | tf_op jit(solution)/shard_map/ppermute | solution.py:91
  112.4 3.3 collective-permute-start.15
  114.1 27.7 %collective-permute-start.19 = (bf16[4,384,384]{2,1,0:T(8,128)(2,1)S(1)}, bf16[4,384,384]{2,1,0:T(8,128)(2,1)S(1)}, u32[]{:S(2)}, u32[]{:S(2)}) collective-permute-start(bf16[4,384,384]{2,1,0:T(8,128)(2,1)S(1)} %pad_maximum_fusion.1.refs_0_), channel_id=1, source_target_pairs={{0,4},{4,0},{8,12},{12,8},{16,20},{20,16},{24,28},{28,24},{1,5},{5... | collective-permute-start | bytes 3538952 | tf_op jit(solution)/shard_map/ppermute | solution.py:99
  114.7 28.5 %collective-permute-start.20 = (bf16[4,384,384]{2,1,0:T(8,128)(2,1)S(1)}, bf16[4,384,384]{2,1,0:T(8,128)(2,1)S(1)}, u32[]{:S(2)}, u32[]{:S(2)}) collective-permute-start(bf16[4,384,384]{2,1,0:T(8,128)(2,1)S(1)} %pad_maximum_fusion.1.refs_0_), channel_id=1, source_target_pairs={{0,1},{1,0},{2,3},{3,2},{4,5},{5,4},{6,7},{7,6},{8,9},{9,8},{10,11... | collective-permute-start | bytes 3538952 | tf_op jit(solution)/shard_map/ppermute | solution.py:91
  119.4 26.5 %copy-start.31 = (f32[1024,768]{1,0:T(8,128)}, f32[1024,768]{1,0:T(8,128)S(1)}, u32[]{:S(2)}) copy-start(f32[1024,768]{1,0:T(8,128)S(1)} %get-tuple-element.187) | copy-start | bytes 9437188
  141.7 3.3 collective-permute-start.21
  184.6 7.7 %collective-permute-start.23 = (bf16[2,4,384,384]{3,2,1,0:T(8,128)(2,1)}, bf16[2,4,384,384]{3,2,1,0:T(8,128)(2,1)}, u32[]{:S(2)}, u32[]{:S(2)}) collective-permute-start(bf16[2,4,384,384]{3,2,1,0:T(8,128)(2,1)} %get-tuple-element.111), channel_id=1, source_target_pairs={{0,1},{1,0},{2,3},{3,2},{4,5},{5,4},{6,7},{7,6},{8,9},{9,8},{10,11... | collective-permute-start | bytes 7077896 | tf_op jit(solution)/shard_map/ppermute | solution.py:91
  185.0 13.3 %collective-permute-start.22 = (bf16[2,4,384,384]{3,2,1,0:T(8,128)(2,1)}, bf16[2,4,384,384]{3,2,1,0:T(8,128)(2,1)}, u32[]{:S(2)}, u32[]{:S(2)}) collective-permute-start(bf16[2,4,384,384]{3,2,1,0:T(8,128)(2,1)} %get-tuple-element.109), channel_id=1, source_target_pairs={{0,1},{1,0},{2,3},{3,2},{4,5},{5,4},{6,7},{7,6},{8,9},{9,8},{10,11... | collective-permute-start | bytes 7077896 | tf_op jit(solution)/shard_map/ppermute | solution.py:91
  194.0 27.2 %collective-permute-start.24 = (bf16[4,384,384]{2,1,0:T(8,128)(2,1)S(1)}, bf16[4,384,384]{2,1,0:T(8,128)(2,1)S(1)}, u32[]{:S(2)}, u32[]{:S(2)}) collective-permute-start(bf16[4,384,384]{2,1,0:T(8,128)(2,1)S(1)} %fusion.4), channel_id=1, source_target_pairs={{0,4},{4,0},{8,12},{12,8},{16,20},{20,16},{24,28},{28,24},{1,5},{5... | collective-permute-start | bytes 3538952 | tf_op jit(solution)/shard_map/ppermute | solution.py:99
  200.6 31.2 %collective-permute-start.25 = (bf16[2,4,192,384]{3,2,1,0:T(8,128)(2,1)S(1)}, bf16[2,4,192,384]{3,2,1,0:T(8,128)(2,1)S(1)}, u32[]{:S(2)}, u32[]{:S(2)}) collective-permute-start(bf16[2,4,192,384]{3,2,1,0:T(8,128)(2,1)S(1)} %add_convert_fusion.2), channel_id=1, source_target_pairs={{0,2},{1,3},{2,0},{3,1},{4,6},{5,7},{6,4},{7,5},{8,10},{9,11},{10,... | collective-permute-start | bytes 3538952 | tf_op jit(solution)/shard_map/ppermute | solution.py:95
  202.0 29.8 %copy-start.35 = (f32[2,4,192,384]{3,2,1,0:T(8,128)}, f32[2,4,192,384]{3,2,1,0:T(8,128)S(1)}, u32[]{:S(2)}) copy-start(f32[2,4,192,384]{3,2,1,0:T(8,128)S(1)} %dynamic-slice_convert_fusion.1) | copy-start | bytes 7077892
  215.4 15.5 %copy-start.8 = (bf16[1024,768]{1,0:T(8,128)(2,1)}, bf16[1024,768]{1,0:T(8,128)(2,1)S(1)}, u32[]{:S(2)}) copy-start(bf16[1024,768]{1,0:T(8,128)(2,1)S(1)} %get-tuple-element.114) | copy-start | bytes 4718596
  217.4 14.4 %copy-start.37 = (f32[2,4,192,384]{3,2,1,0:T(8,128)}, f32[2,4,192,384]{3,2,1,0:T(8,128)S(1)}, u32[]{:S(2)}) copy-start(f32[2,4,192,384]{3,2,1,0:T(8,128)S(1)} %dynamic-slice_convert_fusion) | copy-start | bytes 7077892
  240.0 18.3 %collective-permute-start.26 = (bf16[2,4,240,384]{3,2,1,0:T(8,128)(2,1)}, bf16[2,4,240,384]{3,2,1,0:T(8,128)(2,1)}, u32[]{:S(2)}, u32[]{:S(2)}) collective-permute-start(bf16[2,4,240,384]{3,2,1,0:T(8,128)(2,1)} %get-tuple-element.124), channel_id=1, source_target_pairs={{0,1},{1,0},{2,3},{3,2},{4,5},{5,4},{6,7},{7,6},{8,9},{9,8},{10,11... | collective-permute-start | bytes 4423688 | tf_op jit(solution)/shard_map/ppermute | solution.py:91
  243.1 15.2 %collective-permute-start.27 = (bf16[4,192,384]{2,1,0:T(8,128)(2,1)}, bf16[4,192,384]{2,1,0:T(8,128)(2,1)S(1)}, u32[]{:S(2)}, u32[]{:S(2)}) collective-permute-start(bf16[4,192,384]{2,1,0:T(8,128)(2,1)} %fusion.6), channel_id=1, source_target_pairs={{0,4},{4,0},{8,12},{12,8},{16,20},{20,16},{24,28},{28,24},{1,5},{5... | collective-permute-start | bytes 1769480 | tf_op jit(solution)/shard_map/ppermute | solution.py:99
  244.0 24.8 %collective-permute-start.28 = (bf16[384,384]{1,0:T(8,128)(2,1)}, bf16[384,384]{1,0:T(8,128)(2,1)S(1)}, u32[]{:S(2)}, u32[]{:S(2)}) collective-permute-start(bf16[384,384]{1,0:T(8,128)(2,1)} %get-tuple-element.191), channel_id=1, source_target_pairs={{0,8},{4,12},{8,16},{12,20},{16,24},{20,28},{24,0},{28,4},{1,9},{5... | collective-permute-start | bytes 884744 | tf_op jit(solution)/shard_map/ppermute | solution.py:103
  244.0 26.1 %collective-permute-start.29 = (bf16[384,384]{1,0:T(8,128)(2,1)}, bf16[384,384]{1,0:T(8,128)(2,1)S(1)}, u32[]{:S(2)}, u32[]{:S(2)}) collective-permute-start(bf16[384,384]{1,0:T(8,128)(2,1)} %get-tuple-element.190), channel_id=1, source_target_pairs={{0,16},{4,20},{8,24},{12,28},{16,0},{20,4},{24,8},{28,12},{1,17},{... | collective-permute-start | bytes 884744 | tf_op jit(solution)/shard_map/ppermute | solution.py:103
  244.0 26.1 %collective-permute-start.30 = (bf16[384,384]{1,0:T(8,128)(2,1)S(1)}, bf16[384,384]{1,0:T(8,128)(2,1)S(1)}, u32[]{:S(2)}, u32[]{:S(2)}) collective-permute-start(bf16[384,384]{1,0:T(8,128)(2,1)S(1)} %get-tuple-element.189), channel_id=1, source_target_pairs={{0,24},{4,28},{8,0},{12,4},{16,8},{20,12},{24,16},{28,20},{1,25},{... | collective-permute-start | bytes 884744 | tf_op jit(solution)/shard_map/ppermute | solution.py:103
  261.3 36.1 %collective-permute-start.34 = (bf16[4,240,384]{2,1,0:T(8,128)(2,1)}, bf16[4,240,384]{2,1,0:T(8,128)(2,1)}, u32[]{:S(2)}, u32[]{:S(2)}) collective-permute-start(bf16[4,240,384]{2,1,0:T(8,128)(2,1)} %fusion.5), channel_id=1, source_target_pairs={{0,4},{4,0},{8,12},{12,8},{16,20},{20,16},{24,28},{28,24},{1,5},{5... | collective-permute-start | bytes 2211848 | tf_op jit(solution)/shard_map/ppermute | solution.py:99
  286.8 15.1 %collective-permute-start.36 = (bf16[2,4,160,384]{3,2,1,0:T(8,128)(2,1)}, bf16[2,4,160,384]{3,2,1,0:T(8,128)(2,1)S(1)}, u32[]{:S(2)}, u32[]{:S(2)}) collective-permute-start(bf16[2,4,160,384]{3,2,1,0:T(8,128)(2,1)} %get-tuple-element.142), channel_id=1, source_target_pairs={{0,1},{1,0},{2,3},{3,2},{4,5},{5,4},{6,7},{7,6},{8,9},{9,8},{10,11... | collective-permute-start | bytes 2949128 | tf_op jit(solution)/shard_map/ppermute | solution.py:91
  287.9 8.7 %collective-permute-start.35 = (bf16[384,384]{1,0:T(8,128)(2,1)S(1)}, bf16[384,384]{1,0:T(8,128)(2,1)S(1)}, u32[]{:S(2)}, u32[]{:S(2)}) collective-permute-start(bf16[384,384]{1,0:T(8,128)(2,1)S(1)} %fusion.7), channel_id=1, source_target_pairs={{0,2},{1,3},{2,0},{3,1},{4,6},{5,7},{6,4},{7,5},{8,10},{9,11},{10,... | collective-permute-start | bytes 884744 | tf_op jit(solution)/shard_map/ppermute | solution.py:95
  289.4 13.3 %collective-permute-start.31 = (bf16[192,384]{1,0:T(8,128)(2,1)S(1)}, bf16[192,384]{1,0:T(8,128)(2,1)S(1)}, u32[]{:S(2)}, u32[]{:S(2)}) collective-permute-start(bf16[192,384]{1,0:T(8,128)(2,1)S(1)} %copy-done.50), channel_id=1, source_target_pairs={{0,8},{4,12},{8,16},{12,20},{16,24},{20,28},{24,0},{28,4},{1,9},{5... | collective-permute-start | bytes 442376 | tf_op jit(solution)/shard_map/ppermute | solution.py:103
  289.5 16.0 %collective-permute-start.32 = (bf16[192,384]{1,0:T(8,128)(2,1)S(1)}, bf16[192,384]{1,0:T(8,128)(2,1)S(1)}, u32[]{:S(2)}, u32[]{:S(2)}) collective-permute-start(bf16[192,384]{1,0:T(8,128)(2,1)S(1)} %copy-done.49), channel_id=1, source_target_pairs={{0,16},{4,20},{8,24},{12,28},{16,0},{20,4},{24,8},{28,12},{1,17},{... | collective-permute-start | bytes 442376 | tf_op jit(solution)/shard_map/ppermute | solution.py:103
  296.6 10.1 %collective-permute-start.33 = (bf16[192,384]{1,0:T(8,128)(2,1)S(1)}, bf16[192,384]{1,0:T(8,128)(2,1)S(1)}, u32[]{:S(2)}, u32[]{:S(2)}) collective-permute-start(bf16[192,384]{1,0:T(8,128)(2,1)S(1)} %get-tuple-element.195), channel_id=1, source_target_pairs={{0,24},{4,28},{8,0},{12,4},{16,8},{20,12},{24,16},{28,20},{1,25},{... | collective-permute-start | bytes 442376 | tf_op jit(solution)/shard_map/ppermute | solution.py:103
  299.2 17.7 %collective-permute-start.37 = (bf16[240,384]{1,0:T(8,128)(2,1)S(1)}, bf16[240,384]{1,0:T(8,128)(2,1)S(1)}, u32[]{:S(2)}, u32[]{:S(2)}) collective-permute-start(bf16[240,384]{1,0:T(8,128)(2,1)S(1)} %get-tuple-element.194), channel_id=1, source_target_pairs={{0,8},{4,12},{8,16},{12,20},{16,24},{20,28},{24,0},{28,4},{1,9},{5... | collective-permute-start | bytes 552968 | tf_op jit(solution)/shard_map/ppermute | solution.py:103
  301.8 19.5 %collective-permute-start.38 = (bf16[240,384]{1,0:T(8,128)(2,1)S(1)}, bf16[240,384]{1,0:T(8,128)(2,1)S(1)}, u32[]{:S(2)}, u32[]{:S(2)}) collective-permute-start(bf16[240,384]{1,0:T(8,128)(2,1)S(1)} %get-tuple-element.193), channel_id=1, source_target_pairs={{0,16},{4,20},{8,24},{12,28},{16,0},{20,4},{24,8},{28,12},{1,17},{... | collective-permute-start | bytes 552968 | tf_op jit(solution)/shard_map/ppermute | solution.py:103
  302.7 18.6 %collective-permute-start.39 = (bf16[240,384]{1,0:T(8,128)(2,1)S(1)}, bf16[240,384]{1,0:T(8,128)(2,1)S(1)}, u32[]{:S(2)}, u32[]{:S(2)}) collective-permute-start(bf16[240,384]{1,0:T(8,128)(2,1)S(1)} %get-tuple-element.192), channel_id=1, source_target_pairs={{0,24},{4,28},{8,0},{12,4},{16,8},{20,12},{24,16},{28,20},{1,25},{... | collective-permute-start | bytes 552968 | tf_op jit(solution)/shard_map/ppermute | solution.py:103
  305.5 11.2 %collective-permute-start.41 = (bf16[4,160,384]{2,1,0:T(8,128)(2,1)S(1)}, bf16[4,160,384]{2,1,0:T(8,128)(2,1)S(1)}, u32[]{:S(2)}, u32[]{:S(2)}) collective-permute-start(bf16[4,160,384]{2,1,0:T(8,128)(2,1)S(1)} %fusion.12), channel_id=1, source_target_pairs={{0,4},{4,0},{8,12},{12,8},{16,20},{20,16},{24,28},{28,24},{1,5},{5... | collective-permute-start | bytes 1474568 | tf_op jit(solution)/shard_map/ppermute | solution.py:99
  306.8 27.2 %collective-permute-start.52 = (bf16[384,384]{1,0:T(8,128)(2,1)S(1)}, bf16[384,384]{1,0:T(8,128)(2,1)S(1)}, u32[]{:S(2)}, u32[]{:S(2)}) collective-permute-start(bf16[384,384]{1,0:T(8,128)(2,1)S(1)} %add_convert_fusion.6), channel_id=1, source_target_pairs={{0,1},{1,0},{2,3},{3,2},{4,5},{5,4},{6,7},{7,6},{8,9},{9,8},{10,11... | collective-permute-start | bytes 884744 | tf_op jit(solution)/shard_map/ppermute | solution.py:91
  316.7 5.2 %collective-permute-start.40 = (bf16[192,384]{1,0:T(8,128)(2,1)S(1)}, bf16[192,384]{1,0:T(8,128)(2,1)S(1)}, u32[]{:S(2)}, u32[]{:S(2)}) collective-permute-start(bf16[192,384]{1,0:T(8,128)(2,1)S(1)} %fusion.17), channel_id=1, source_target_pairs={{0,2},{1,3},{2,0},{3,1},{4,6},{5,7},{6,4},{7,5},{8,10},{9,11},{10,... | collective-permute-start | bytes 442376 | tf_op jit(solution)/shard_map/ppermute | solution.py:95
  316.9 6.7 %collective-permute-start.45 = (bf16[160,384]{1,0:T(8,128)(2,1)S(1)}, bf16[160,384]{1,0:T(8,128)(2,1)S(1)}, u32[]{:S(2)}, u32[]{:S(2)}) collective-permute-start(bf16[160,384]{1,0:T(8,128)(2,1)S(1)} %get-tuple-element.200), channel_id=1, source_target_pairs={{0,8},{4,12},{8,16},{12,20},{16,24},{20,28},{24,0},{28,4},{1,9},{5... | collective-permute-start | bytes 368648 | tf_op jit(solution)/shard_map/ppermute | solution.py:103
  321.3 10.8 %collective-permute-start.46 = (bf16[160,384]{1,0:T(8,128)(2,1)S(1)}, bf16[160,384]{1,0:T(8,128)(2,1)S(1)}, u32[]{:S(2)}, u32[]{:S(2)}) collective-permute-start(bf16[160,384]{1,0:T(8,128)(2,1)S(1)} %get-tuple-element.199), channel_id=1, source_target_pairs={{0,16},{4,20},{8,24},{12,28},{16,0},{20,4},{24,8},{28,12},{1,17},{... | collective-permute-start | bytes 368648 | tf_op jit(solution)/shard_map/ppermute | solution.py:103
  321.3 12.6 %collective-permute-start.47 = (bf16[160,384]{1,0:T(8,128)(2,1)S(1)}, bf16[160,384]{1,0:T(8,128)(2,1)S(1)}, u32[]{:S(2)}, u32[]{:S(2)}) collective-permute-start(bf16[160,384]{1,0:T(8,128)(2,1)S(1)} %get-tuple-element.198), channel_id=1, source_target_pairs={{0,24},{4,28},{8,0},{12,4},{16,8},{20,12},{24,16},{28,20},{1,25},{... | collective-permute-start | bytes 368648 | tf_op jit(solution)/shard_map/ppermute | solution.py:103
  322.0 12.7 %collective-permute-start.42 = (bf16[240,384]{1,0:T(8,128)(2,1)S(1)}, bf16[240,384]{1,0:T(8,128)(2,1)S(1)}, u32[]{:S(2)}, u32[]{:S(2)}) collective-permute-start(bf16[240,384]{1,0:T(8,128)(2,1)S(1)} %fusion.13.refs_0_), channel_id=1, source_target_pairs={{0,2},{1,3},{2,0},{3,1},{4,6},{5,7},{6,4},{7,5},{8,10},{9,11},{10,... | collective-permute-start | bytes 552968 | tf_op jit(solution)/shard_map/ppermute | solution.py:245
  323.6 11.9 %collective-permute-start.43 = (bf16[240,384]{1,0:T(8,128)(2,1)S(1)}, bf16[240,384]{1,0:T(8,128)(2,1)S(1)}, u32[]{:S(2)}, u32[]{:S(2)}) collective-permute-start(bf16[240,384]{1,0:T(8,128)(2,1)S(1)} %fusion.13.refs_0_), channel_id=1, source_target_pairs={{0,1},{1,0},{2,3},{3,2},{4,5},{5,4},{6,7},{7,6},{8,9},{9,8},{10,11... | collective-permute-start | bytes 552968 | tf_op jit(solution)/shard_map/ppermute | solution.py:245
  332.1 7.0 %collective-permute-start.44 = (bf16[240,384]{1,0:T(8,128)(2,1)S(1)}, bf16[240,384]{1,0:T(8,128)(2,1)S(1)}, u32[]{:S(2)}, u32[]{:S(2)}) collective-permute-start(bf16[240,384]{1,0:T(8,128)(2,1)S(1)} %fusion.13.refs_0_), channel_id=1, source_target_pairs={{0,3},{1,2},{2,1},{3,0},{4,7},{5,6},{6,5},{7,4},{8,11},{9,10},{10,... | collective-permute-start | bytes 552968 | tf_op jit(solution)/shard_map/ppermute | solution.py:245
  333.9 12.7 %collective-permute-start.51 = (bf16[384,384]{1,0:T(8,128)(2,1)S(1)}, bf16[384,384]{1,0:T(8,128)(2,1)S(1)}, u32[]{:S(2)}, u32[]{:S(2)}) collective-permute-start(bf16[384,384]{1,0:T(8,128)(2,1)S(1)} %maximum_select_fusion.2), channel_id=1, source_target_pairs={{0,1},{1,0},{2,3},{3,2},{4,5},{5,4},{6,7},{7,6},{8,9},{9,8},{10,11... | collective-permute-start | bytes 884744 | tf_op jit(solution)/shard_map/ppermute | solution.py:91
  334.0 8.1 %collective-permute-start.48 = (bf16[160,384]{1,0:T(8,128)(2,1)S(1)}, bf16[160,384]{1,0:T(8,128)(2,1)S(1)}, u32[]{:S(2)}, u32[]{:S(2)}) collective-permute-start(bf16[160,384]{1,0:T(8,128)(2,1)S(1)} %fusion.18.refs_4_), channel_id=1, source_target_pairs={{0,2},{1,3},{2,0},{3,1},{4,6},{5,7},{6,4},{7,5},{8,10},{9,11},{10,... | collective-permute-start | bytes 368648 | tf_op jit(solution)/shard_map/ppermute | solution.py:245
  334.7 7.4 %collective-permute-start.49 = (bf16[160,384]{1,0:T(8,128)(2,1)S(1)}, bf16[160,384]{1,0:T(8,128)(2,1)S(1)}, u32[]{:S(2)}, u32[]{:S(2)}) collective-permute-start(bf16[160,384]{1,0:T(8,128)(2,1)S(1)} %fusion.18.refs_4_), channel_id=1, source_target_pairs={{0,1},{1,0},{2,3},{3,2},{4,5},{5,4},{6,7},{7,6},{8,9},{9,8},{10,11... | collective-permute-start | bytes 368648 | tf_op jit(solution)/shard_map/ppermute | solution.py:245
  335.5 8.9 %collective-permute-start.50 = (bf16[160,384]{1,0:T(8,128)(2,1)S(1)}, bf16[160,384]{1,0:T(8,128)(2,1)S(1)}, u32[]{:S(2)}, u32[]{:S(2)}) collective-permute-start(bf16[160,384]{1,0:T(8,128)(2,1)S(1)} %fusion.18.refs_4_), channel_id=1, source_target_pairs={{0,3},{1,2},{2,1},{3,0},{4,7},{5,6},{6,5},{7,4},{8,11},{9,10},{10,... | collective-permute-start | bytes 368648 | tf_op jit(solution)/shard_map/ppermute | solution.py:245
  (47 other events, 251.4 us)
